TPU v7x, 32 devices: a whole 2x2x4 slice. The times are simulated.
32 devices in a mesh: rows: 8 (over z, y), rhs: 4 (over x, core).
Axes of the slice: x: 2, y: 2, z: 4, core: 2. Of those that a mesh axis runs over, the one named last changes fastest.
Arguments:
- lower_panels: bfloat16 [32768, 1024], P('rows', 'rhs'), may hold values from -0.046875 to 0.046875
- parent_solution: bfloat16 [32768, 2048], P('rows', 'rhs'), may hold values from -6 to 6
- parent_rows: int32 [32768], P('rows'), may hold values from 0 to 32767, as said below
- live_counts: int32 [8], P('rows'), may hold values from 512 to 4096, as said below
- front_rhs: bfloat16 [1024, 2048], P('rows', 'rhs'), may hold values from -6 to 6
- coupling: float32 [512, 512], replicated, may hold values from -0.25 to 0.25
- inverse_one: float32 [512, 512], replicated, as said below
- inverse_two: float32 [512, 512], replicated, as said below
Outputs:
- solution: float32 [1024, 2048], P('rows', 'rhs')
Inputs may be any that keep to these rules, and one draw needn't show every extreme that they name: `parent_rows`: the 128 entries of an aligned block of one device's 4096 entries all lie among the 4096 rows of one index of rows, the block's owner; two blocks of one device have the same owner exactly when their block numbers differ by a multiple of 8. `live_counts`: the live rows of an index are its first ones. Each count is 4096 divided by 1, 2, 4 or 8, and some index has all 4096. `inverse_one`: upper triangular. `inverse_two`: upper triangular.
All inputs are finite; a program needn't handle non-finite values.
Results may differ from a plain program's by a relative error of at most 0.0003.
Values may be sent and summed in bfloat16 or wider, within the bound.
No kernel may reach another device: no remote copies, remote signals or barrier semaphores. Data moves between devices by JAX's collectives and lax.ppermute only.
A program may use at most 64 MiB of HBM per device.

v0:
```python
import jax
import jax.numpy as jnp
from jax import lax
from jax.sharding import PartitionSpec as P

BLK = 128


def right_apply(left, matrix):
    return lax.dot_general(
        left,
        matrix,
        (((1,), (1,)), ((), ())),
        precision=lax.Precision.HIGHEST,
        preferred_element_type=jnp.float32,
    )


def body(
    lower_panels,
    parent_solution,
    parent_rows,
    live_counts,
    front_rhs,
    coupling,
    inverse_one,
    inverse_two,
):
    groups = lax.axis_size("rows")
    rows_dev = parent_rows.shape[0]
    block_count = rows_dev // BLK
    slot_count = (block_count + groups - 1) // groups
    columns_dev = parent_solution.shape[1]
    panel_width = inverse_one.shape[0]
    pivot_width = 2 * panel_width
    pivot_share = front_rhs.shape[0]
    start_own = lax.axis_index("rows") * pivot_share
    block_lists = parent_rows.reshape(block_count, BLK)
    owners = block_lists[:, 0] // rows_dev
    local_rows = block_lists - owners[:, None] * rows_dev
    slot_of = jnp.arange(block_count, dtype=jnp.int32) // groups
    requests = jnp.zeros((groups, slot_count, BLK), jnp.int32).at[owners, slot_of].set(local_rows)
    received = lax.all_to_all(requests, "rows", split_axis=0, concat_axis=0, tiled=True)
    picked = parent_solution[received.reshape(-1)].reshape(received.shape + (columns_dev,))
    returned = lax.all_to_all(picked, "rows", split_axis=0, concat_axis=0, tiled=True)
    fetched = returned[owners, slot_of].reshape(rows_dev, columns_dev)
    live_mask = jnp.arange(rows_dev, dtype=jnp.int32) < live_counts[0]
    values = jnp.where(live_mask[:, None], fetched, jnp.zeros((), fetched.dtype))
    rhs_float = front_rhs.astype(jnp.float32)
    placed_t = lax.dynamic_update_slice(
        jnp.zeros((columns_dev, pivot_width), jnp.float32), rhs_float.T, (0, start_own)
    )
    product_t = lax.dot_general(
        values,
        lax.all_gather(lower_panels, "rhs", axis=1, tiled=True),
        (((0,), (0,)), ((), ())),
        preferred_element_type=jnp.float32,
    )
    resid_t = lax.psum_scatter(placed_t - product_t, "rows", scatter_dimension=0, tiled=True)
    second_t = right_apply(resid_t[:, panel_width:], inverse_two)
    reduced_t = resid_t[:, :panel_width] - right_apply(second_t, coupling)
    first_t = right_apply(reduced_t, inverse_one)
    solved_t = jnp.concatenate([first_t, second_t], axis=1)
    regrouped = lax.all_to_all(solved_t, "rows", split_axis=1, concat_axis=0, tiled=True)
    return regrouped.T


def solution(mesh):
    return jax.shard_map(
        body,
        mesh=mesh,
        in_specs=(
            P("rows", "rhs"),
            P("rows", "rhs"),
            P("rows"),
            P("rows"),
            P("rows", "rhs"),
            P(),
            P(),
            P(),
        ),
        out_specs=P("rows", "rhs"),
        check_vma=False,
    )
```

profile of v0, /device:TPU:0, one launch (start us, length us, event | category | flops | bytes accessed | tf_op | source)
XLA Modules:
  0.0 253.6 jit_solution(1169365794823633326)
XLA Ops:
  6.5 0.0 copy-start
  6.5 0.0 all-gather.2.cloned.1.call-start
  6.5 0.7 all-gather.2.cloned.1.call-update
  7.3 0.9 fusion.9
  8.1 0.8 broadcast_subtract_fusion
  8.9 2.1 scatter_fusion
  11.0 13.7 %all_to_all.29 = s32[8,4,128]{2,1,0:T(4,128)S(1)} all-to-all(s32[8,4,128]{2,1,0:T(4,128)S(1)} %scatter_fusion), channel_id=1, replica_groups=mesh['rows'=8,'rhs'=4] {'rows'}, dimensions={0} | all-to-all | bytes 32768 | tf_op jit(solution)/shard_map/all_to_all | solution.py:43
  24.7 20.2 %gather_fusion = bf16[4096,512]{1,0:T(8,128)(2,1)} fusion(bf16[4096,512]{1,0:T(8,128)(2,1)} %param.9, s32[4096]{0:T(1024)S(1)} %broadcast_clamp_fusion), kind=kCustom, calls=%fused_computation | custom fusion | bytes 8404992 | tf_op jit(solution)/shard_map/gather | solution.py:44
  44.9 0.0 copy-start.2
  44.9 4.8 %all-to-all-start.1 = ((bf16[8,4,128,512]{3,2,1,0:T(8,128)(2,1)}), bf16[8,4,128,512]{3,2,1,0:T(8,128)(2,1)}, u32[]{:S(2)}, u32[]{:S(2)}) async-start(bf16[8,4,128,512]{3,2,1,0:T(8,128)(2,1)} %bitcast.28), calls=%async_computation.1 | async-start | bytes 8388608 | tf_op jit(solution)/shard_map/all_to_all | solution.py:45
  49.7 0.0 reduce-scatter.2.cloned.1.call-start
  50.4 0.0 copy-done.2
  50.4 0.1 copy.14
  50.6 0.2 broadcast_in_dim.12
  50.9 90.9 %all-to-all-done.1 = bf16[8,4,128,512]{3,2,1,0:T(8,128)(2,1)} async-done(((bf16[8,4,128,512]{3,2,1,0:T(8,128)(2,1)}), bf16[8,4,128,512]{3,2,1,0:T(8,128)(2,1)}, u32[]{:S(2)}, u32[]{:S(2)}) %all-to-all-start.1) | async-done | bytes 4194336 | tf_op jit(solution)/shard_map/all_to_all | solution.py:45
  141.8 5.0 %gather_fusion.1 = bf16[32,128,512]{2,1,0:T(8,128)(2,1)} fusion(bf16[8,4,128,512]{3,2,1,0:T(8,128)(2,1)} %all-to-all-done.1, s32[32]{0:T(128)S(1)} %get-tuple-element.5), kind=kCustom, calls=%fused_computation.1 | custom fusion | bytes 8388864 | tf_op jit(solution)/shard_map/gather | solution.py:46
  146.7 3.9 %bitcast_select_fusion = bf16[4096,512]{1,0:T(8,128)(2,1)} fusion(bf16[32,128,512]{2,1,0:T(8,128)(2,1)} %gather_fusion.1, pred[4096]{0:T(1024)(128)(4,1)S(1)} %iota_compare_fusion), kind=kLoop, calls=%fused_computation.3 | loop fusion | flops 2097152 | bytes 8392704 | tf_op jit(solution)/shard_map/jit(_where)/select_n | solution.py:48
  150.7 0.0 all-gather.2.cloned.1.call-done
  150.7 10.5 %convolution_subtract_fusion = f32[512,1024]{1,0:T(8,128)} fusion(f32[512,1024]{1,0:T(8,128)S(1)} %bitcast_dynamic-update-slice_fusion, bf16[4096,512]{1,0:T(8,128)(2,1)} %bitcast_select_fusion, bf16[4096,1024]{1,0:T(8,128)(2,1)} %all-gather.2.cloned.1.call-done), kind=kOutput, calls=%fused_computation.4 | convolution fusion | flops 4295491584 | bytes 16777216 | tf_op jit(solution)/shard_map/dot_general | solution.py:53
  161.2 0.0 copy-start.1
  161.2 0.0 reduce-scatter.2.cloned.1.call-update
  161.2 67.6 %reduce-scatter.2.cloned.1.call-done = f32[64,1024]{1,0:T(8,128)} async-done(((f32[512,1024]{1,0:T(8,128)}), f32[64,1024]{1,0:T(8,128)}) %reduce-scatter.2.cloned.1.call-update) | async-done | bytes 262160 | tf_op jit(solution)/shard_map/reduce_scatter | solution.py:59
  228.8 0.0 copy-done
  228.8 2.0 fusion
  230.8 2.3 convolution_subtract_fusion.1
  233.1 0.0 copy-done.1
  233.2 1.1 fusion.10
  234.3 11.7 %all_to_all.30 = f32[64,8,128]{2,0,1:T(8,128)S(1)} all-to-all(f32[64,8,128]{2,0,1:T(8,128)S(1)} %copy_bitcast_fusion), channel_id=1, replica_groups=mesh['rows'=8,'rhs'=4] {'rows'}, dimensions={1} | all-to-all | bytes 524288 | tf_op jit(solution)/shard_map/all_to_all | solution.py:64
  246.0 0.8 copy.16
  (6 shorter events, 0.1 us)
Async XLA Ops:
  6.5 222.3 %copy-start = (f32[512,512]{1,0:T(8,128)S(1)}, f32[512,512]{1,0:T(8,128)}, u32[]{:S(2)}) copy-start(f32[512,512]{1,0:T(8,128)} %param.15) | copy-start | bytes 3145732
  6.5 144.1 %all-gather.2.cloned.1.call-start = ((), (), s32[]{:S(2)}) async-start(), calls=%async_computation.4 | async-start | bytes 10485760 | tf_op jit(solution)/shard_map/all_gather | solution.py:55
  44.9 5.5 %copy-start.2 = (bf16[128,512]{1,0:T(8,128)(2,1)S(1)}, bf16[128,512]{1,0:T(8,128)(2,1)}, u32[]{:S(2)}) copy-start(bf16[128,512]{1,0:T(8,128)(2,1)} %param.12) | copy-start | bytes 393220
  44.9 96.8 %all-to-all-start.1 = ((bf16[8,4,128,512]{3,2,1,0:T(8,128)(2,1)}), bf16[8,4,128,512]{3,2,1,0:T(8,128)(2,1)}, u32[]{:S(2)}, u32[]{:S(2)}) async-start(bf16[8,4,128,512]{3,2,1,0:T(8,128)(2,1)} %bitcast.28), calls=%async_computation.1 | async-start | bytes 8388608 | tf_op jit(solution)/shard_map/all_to_all | solution.py:45
  49.7 179.1 %reduce-scatter.2.cloned.1.call-start = ((), (), s32[]{:S(2)}) async-start(), calls=%async_computation.5 | async-start | bytes 2359296 | tf_op jit(solution)/shard_map/reduce_scatter | solution.py:59
  161.2 72.0 %copy-start.1 = (f32[512,512]{1,0:T(8,128)S(1)}, f32[512,512]{1,0:T(8,128)}, u32[]{:S(2)}) copy-start(f32[512,512]{1,0:T(8,128)} %param.14) | copy-start | bytes 3145732
Sparse Core Ops, SparseCore 0:
  8.9 62.0 all-gather.1
  161.3 67.4 reduce-scatter.1
where the time goes:
time: 254 us
  waiting for transfers between devices  159 us (63%)
  local copies, waits for them, and re-layouts  28.5 us (11%)
  blocking collectives  25.3 us (10%)
  matrix products  16 us (6%)
  between operations  14.1 us (6%)
  other arithmetic  5.67 us (2%)
  starting transfers between devices  4.82 us (2%)
    all_to_all x1, waiting for transfers between devices, body(): lax.all_to_all(picked, 'rows', split_axis=0, concat_axis=0, tiled=True)  90.9 us
    reduce_scatter x1, waiting for transfers between devices, body(): lax.psum_scatter(placed_t - product_t, 'rows', scatter_dimension=0, tiled...  67.6 us
    gather x1, local copies, waits for them, and re-layouts, body(): parent_solution[received.reshape(-1)]  20.2 us
    all_to_all x1, blocking collectives, body(): lax.all_to_all(requests, 'rows', split_axis=0, concat_axis=0, tiled=True)  13.7 us
    all_to_all x1, blocking collectives, body(): lax.all_to_all(solved_t, 'rows', split_axis=1, concat_axis=0, tiled=True)  11.7 us
    dot_general x1, matrix products, body(): lax.dot_general(values, lax.all_gather(lower_panels, 'rhs', axis=1, tiled...  10.5 us
    dot_general x3, matrix products, right_apply(): lax.dot_general(left, matrix, (((1,), (1,)), ((), ())), precision=lax.Pre...  5.47 us
  transfers between devices with their start and end apart: 3, of which 2 were waited for; matrix products, arithmetic and copies ran while one was open for 13% of the time, Pallas kernels for 0%

commit v1 on v0

v1 whole, which is shorter than its diff:
```python
import jax
import jax.numpy as jnp
from jax import lax
from jax.sharding import PartitionSpec as P

BLK = 128


def swap(array, axis, mask):
    size = lax.axis_size(axis)
    return lax.ppermute(array, axis, [(i, i ^ mask) for i in range(size)])


def full_dot(left, right):
    return jnp.dot(
        left, right, precision=lax.Precision.HIGHEST, preferred_element_type=jnp.float32
    )


def panel_dot(panel, rows):
    return lax.dot_general(
        panel, rows, (((0,), (0,)), ((), ())), preferred_element_type=jnp.float32
    )


def halving_sum(parts, order):
    for mask in order:
        keep = [r for r in parts if not r & mask]
        sent = jnp.stack([parts[r | mask] for r in keep])
        came = swap(sent, "rows", mask)
        parts = {r: parts[r] + came[i] for i, r in enumerate(keep)}
    return parts[0]


def body(
    lower_panels,
    parent_solution,
    parent_rows,
    live_counts,
    front_rhs,
    coupling,
    inverse_one,
    inverse_two,
):
    groups = lax.axis_size("rows")
    shares = lax.axis_size("rhs")
    me = lax.axis_index("rows")
    share = lax.axis_index("rhs")
    rows_dev = parent_rows.shape[0]
    slots = rows_dev // BLK // groups
    width = lower_panels.shape[1]
    columns = parent_solution.shape[1]
    panel = inverse_one.shape[0]
    pivot_share = front_rhs.shape[0]

    lists = parent_rows.reshape(slots, groups, BLK)
    owners = lists[0, :, 0] // rows_dev
    local = lists - (owners * rows_dev)[None, :, None]
    places = jnp.arange(groups, dtype=jnp.int32)
    blocks = lower_panels.reshape(slots, groups, BLK, width)
    live = (jnp.arange(rows_dev, dtype=jnp.int32) < live_counts[0]).reshape(slots, groups, BLK)

    def for_owner(mask):
        place = jnp.sum(jnp.where(owners == me ^ mask, places, 0))
        take = lambda a: lax.dynamic_index_in_dim(a, place, 1, keepdims=False)
        chunk = jnp.where(take(live)[..., None], take(blocks), jnp.zeros((), blocks.dtype))
        return chunk.reshape(slots * BLK, width), take(local)

    sends = [for_owner(mask) for mask in range(groups)]
    asked = [sends[0][1]] + [swap(sends[mask][1], "rows", mask) for mask in range(1, groups)]

    half = groups // 2
    chunks = {0: sends[0][0]}
    last = None
    for mask in list(range(half, groups)):
        sent = sends[mask][0]
        if last is not None:
            sent, last = lax.optimization_barrier((sent, last))
        chunks[mask] = last = swap(sent, "rows", mask)
    for mask in range(1, half):
        chunks[mask] = swap(sends[mask][0], "rows", mask)

    total = 0.0
    for mask in [0] + list(range(1, half)) + list(range(half, groups)):
        chunk = chunks[mask]
        near = jnp.concatenate(
            [chunk] + [swap(chunk, "rhs", other) for other in range(2, shares, 2)], axis=1
        )
        far = swap(near, "rhs", 1)
        picked = parent_solution[asked[mask].reshape(-1)]
        total = total + panel_dot(jnp.concatenate([near, far], axis=1), picked)

    shape = (shares, width, columns)
    order = jnp.arange(shares, dtype=jnp.int32) ^ share
    position = (order & 1) * (shares // 2) + (order >> 1)
    product = total.reshape(shape)[position].reshape(2 * panel, columns)
    placed = lax.dynamic_update_slice(
        jnp.zeros((2 * panel, columns), jnp.float32), front_rhs.astype(jnp.float32), (me * pivot_share, 0)
    )
    resid = placed - product

    outs = []
    middle = columns // 2
    bits = [1 << b for b in range(groups.bit_length() - 1)]
    for at, order in ((0, bits), (middle, bits[1:] + bits[:1])):
        part = resid[:, at : at + middle]
        second = full_dot(inverse_two, part[panel:])
        first = full_dot(inverse_one, part[:panel] - full_dot(coupling, second))
        solved = jnp.concatenate([first, second], axis=0).reshape(groups, pivot_share, middle)
        parts = {
            r: lax.dynamic_index_in_dim(solved, me ^ r, 0, keepdims=False) for r in range(groups)
        }
        outs.append(halving_sum(parts, order))
    return jnp.concatenate(outs, axis=1)


def solution(mesh):
    return jax.shard_map(
        body,
        mesh=mesh,
        in_specs=(
            P("rows", "rhs"),
            P("rows", "rhs"),
            P("rows"),
            P("rows"),
            P("rows", "rhs"),
            P(),
            P(),
            P(),
        ),
        out_specs=P("rows", "rhs"),
        check_vma=False,
    )
```

time: 254 us -> 222 us (0.87)
  waiting for transfers between devices: 159 us -> 52.4 us
  starting transfers between devices: 4.82 us -> 52.4 us
  local copies, waits for them, and re-layouts: 28.5 us -> 55.5 us
  blocking collectives: 25.3 us -> 0 us
  other arithmetic: 5.67 us -> 26.2 us
  matrix products: 16 us -> 18.6 us
    all_to_all x1 -> x0, waiting for transfers between devices: 90.9 us -> none  [body(): lax.all_to_all(picked, 'rows', split_axis=0, concat_axis=0, tiled=True)]
    reduce_scatter x1 -> x0, waiting for transfers between devices: 67.6 us -> none  [body(): lax.psum_scatter(placed_t - product_t, 'rows', scatter_dimension=0, tiled...]
    ppermute x0 -> x36, waiting for transfers between devices: none -> 52.4 us  [swap(): return lax.ppermute(array, axis, [(i, i ^ mask) for i in range(size)])]
    ppermute x0 -> x36, starting transfers between devices: none -> 52.4 us  [swap(): return lax.ppermute(array, axis, [(i, i ^ mask) for i in range(size)])]
    all_to_all x2 -> x0, blocking collectives: 25.3 us -> none  [the longest x1 13.7 us: body(): lax.all_to_all(requests, 'rows', split_axis=0, concat_axis=0, tiled=True)]
    gather x2 -> x9, local copies, waits for them, and re-layouts: 25.2 us -> 43.3 us  [the longest x8 41.2 us: body(): picked = parent_solution[asked[mask].reshape(-1)]]
    concatenate x1 -> x11, other arithmetic: 0.88 us -> 8.02 us  [the longest x8 5.18 us: body(): jnp.concatenate([chunk] + [swap(chunk, 'rhs', other) for other in range(2...]
    reshape x0 -> x3, local copies, waits for them, and re-layouts: none -> 7.09 us  [the longest x2 4.18 us: body(): jnp.concatenate([first, second], axis=0)]
  transfers between devices with their start and end apart: 3 -> 36, of which waited for: 2 -> 14; matrix products, arithmetic and copies ran while one was open for 13% -> 34% of each run, Pallas kernels for 0% -> 0%
where the time goes in v1:
time: 222 us; the launch traced here: 221 us
  local copies, waits for them, and re-layouts  55.5 us (25%)
  starting transfers between devices  52.4 us (24%)
  waiting for transfers between devices  52.4 us (24%)
  other arithmetic  26.2 us (12%)
  matrix products  18.6 us (8%)
  between operations  16.2 us (7%)
    ppermute x36, waiting for transfers between devices, swap(): return lax.ppermute(array, axis, [(i, i ^ mask) for i in range(size)])  52.4 us
    ppermute x36, starting transfers between devices, swap(): return lax.ppermute(array, axis, [(i, i ^ mask) for i in range(size)])  52.4 us
    gather x8, local copies, waits for them, and re-layouts, body(): picked = parent_solution[asked[mask].reshape(-1)]  41.2 us
    dot_general x8, matrix products, panel_dot(): lax.dot_general(panel, rows, (((0,), (0,)), ((), ())), preferred_element_...  11.5 us
    dot_general x6, matrix products, full_dot(): jnp.dot(left, right, precision=lax.Precision.HIGHEST, preferred_element_t...  7.1 us
    add x6, other arithmetic, halving_sum(): parts = {r: parts[r] + came[i] for i, r in enumerate(keep)}  5.87 us
    concatenate x8, other arithmetic, body(): jnp.concatenate([chunk] + [swap(chunk, 'rhs', other) for other in range(2...  5.18 us
  transfers between devices with their start and end apart: 36, of which 14 were waited for; matrix products, arithmetic and copies ran while one was open for 34% of the time, Pallas kernels for 0%

profile of v1, /device:TPU:0, one launch (start us, length us, event | category | flops | bytes accessed | tf_op | source)
XLA Modules:
  0.0 221.2 jit_solution(6862720270396557264)
XLA Ops:
  17.4 1.7 constant_dynamic-slice_fusion.27
  19.3 3.1 %collective-permute-start.6 = (bf16[512,256]{1,0:T(8,128)(2,1)S(1)}, bf16[512,256]{1,0:T(8,128)(2,1)}, u32[]{:S(2)}, u32[]{:S(2)}) collective-permute-start(bf16[512,256]{1,0:T(8,128)(2,1)S(1)} %bitcast_select_fusion.5), channel_id=1, source_target_pairs={{0,8},{4,12},{8,0},{12,4},{16,24},{20,28},{24,16},{28,20},{1,9},{5... | collective-permute-start | bytes 786440 | tf_op jit(solution)/shard_map/ppermute | solution.py:11
  22.6 3.0 %collective-permute-start.13 = (s32[4,128]{1,0:T(4,128)S(1)}, s32[4,128]{1,0:T(4,128)S(1)}, u32[]{:S(2)}, u32[]{:S(2)}) collective-permute-start(s32[4,128]{1,0:T(4,128)S(1)} %bitcast.132), channel_id=1, source_target_pairs={{0,12},{4,8},{8,4},{12,0},{16,28},{20,24},{24,20},{28,16},{1,13},{... | collective-permute-start | bytes 6152 | tf_op jit(solution)/shard_map/ppermute | solution.py:11
  27.3 3.0 %collective-permute-start.14 = (bf16[512,256]{1,0:T(8,128)(2,1)}, bf16[512,256]{1,0:T(8,128)(2,1)}, u32[]{:S(2)}, u32[]{:S(2)}) collective-permute-start(bf16[512,256]{1,0:T(8,128)(2,1)} %bitcast_select_fusion.3), channel_id=1, source_target_pairs={{0,16},{4,20},{8,24},{12,28},{16,0},{20,4},{24,8},{28,12},{1,17},{... | collective-permute-start | bytes 786440 | tf_op jit(solution)/shard_map/ppermute | solution.py:11
  32.5 1.6 broadcast_in_dim.100
  34.9 1.9 collective-permute-start.5
  36.8 2.0 collective-permute-done.5
  38.8 3.6 %collective-permute-start.21 = (s32[4,128]{1,0:T(4,128)S(1)}, s32[4,128]{1,0:T(4,128)S(1)}, u32[]{:S(2)}, u32[]{:S(2)}) collective-permute-start(s32[4,128]{1,0:T(4,128)S(1)} %bitcast.129), channel_id=1, source_target_pairs={{0,20},{4,16},{8,28},{12,24},{16,4},{20,0},{24,12},{28,8},{1,21},{... | collective-permute-start | bytes 6152 | tf_op jit(solution)/shard_map/ppermute | solution.py:11
  42.4 2.7 %collective-permute-start.25 = (s32[4,128]{1,0:T(4,128)S(1)}, s32[4,128]{1,0:T(4,128)S(1)}, u32[]{:S(2)}, u32[]{:S(2)}) collective-permute-start(s32[4,128]{1,0:T(4,128)S(1)} %bitcast.128), channel_id=1, source_target_pairs={{0,24},{4,28},{8,16},{12,20},{16,8},{20,12},{24,0},{28,4},{1,25},{... | collective-permute-start | bytes 6152 | tf_op jit(solution)/shard_map/ppermute | solution.py:11
  45.2 3.7 %collective-permute-start.29 = (s32[4,128]{1,0:T(4,128)S(1)}, s32[4,128]{1,0:T(4,128)S(1)}, u32[]{:S(2)}, u32[]{:S(2)}) collective-permute-start(s32[4,128]{1,0:T(4,128)S(1)} %bitcast.127), channel_id=1, source_target_pairs={{0,28},{4,24},{8,20},{12,16},{16,12},{20,8},{24,4},{28,0},{1,29},{... | collective-permute-start | bytes 6152 | tf_op jit(solution)/shard_map/ppermute | solution.py:11
  48.9 1.6 collective-permute-start
  53.0 1.6 collective-permute-start.7
  55.3 2.9 %collective-permute-done = bf16[512,256]{1,0:T(8,128)(2,1)S(1)} collective-permute-done((bf16[512,256]{1,0:T(8,128)(2,1)S(1)}, bf16[512,256]{1,0:T(8,128)(2,1)S(1)}, u32[]{:S(2)}, u32[]{:S(2)}) %collective-permute-start) | collective-permute-done | bytes 262176 | tf_op jit(solution)/shard_map/ppermute | solution.py:11
  60.5 1.4 collective-permute-start.15
  62.0 5.6 %gather_fusion.2 = bf16[512,512]{1,0:T(8,128)(2,1)} fusion(bf16[4096,512]{1,0:T(8,128)(2,1)} %param.9, s32[1024]{0:T(1024)S(1)} %pad_clamp_fusion.6), kind=kCustom, calls=%fused_computation.2 | custom fusion | bytes 1050624 | tf_op jit(solution)/shard_map/gather | solution.py:90
  67.5 5.4 %gather_fusion.3 = bf16[512,512]{1,0:T(8,128)(2,1)} fusion(bf16[4096,512]{1,0:T(8,128)(2,1)} %param.9, s32[1024]{0:T(1024)S(1)} %pad_clamp_fusion.5), kind=kCustom, calls=%fused_computation.3 | custom fusion | bytes 1050624 | tf_op jit(solution)/shard_map/gather | solution.py:90
  72.9 5.4 %gather_fusion.4 = bf16[512,512]{1,0:T(8,128)(2,1)} fusion(bf16[4096,512]{1,0:T(8,128)(2,1)} %param.9, s32[1024]{0:T(1024)S(1)} %pad_clamp_fusion.4), kind=kCustom, calls=%fused_computation.4 | custom fusion | bytes 1050624 | tf_op jit(solution)/shard_map/gather | solution.py:90
  78.3 4.7 %gather_fusion.5 = bf16[512,512]{1,0:T(8,128)(2,1)S(1)} fusion(bf16[4096,512]{1,0:T(8,128)(2,1)} %param.9, s32[1024]{0:T(1024)S(1)} %pad_clamp_fusion.3), kind=kCustom, calls=%fused_computation.5 | custom fusion | bytes 1050624 | tf_op jit(solution)/shard_map/gather | solution.py:90
  83.0 5.4 %gather_fusion = bf16[512,512]{1,0:T(8,128)(2,1)} fusion(bf16[4096,512]{1,0:T(8,128)(2,1)} %param.9, s32[1024]{0:T(1024)S(1)} %pad_clamp_fusion.8), kind=kCustom, calls=%fused_computation | custom fusion | bytes 1050624 | tf_op jit(solution)/shard_map/gather | solution.py:90
  88.4 4.7 %gather_fusion.6 = bf16[512,512]{1,0:T(8,128)(2,1)S(1)} fusion(bf16[4096,512]{1,0:T(8,128)(2,1)} %param.9, s32[1024]{0:T(1024)S(1)} %pad_clamp_fusion.2), kind=kCustom, calls=%fused_computation.6 | custom fusion | bytes 1050624 | tf_op jit(solution)/shard_map/gather | solution.py:90
  93.1 4.7 %gather_fusion.7 = bf16[512,512]{1,0:T(8,128)(2,1)S(1)} fusion(bf16[4096,512]{1,0:T(8,128)(2,1)} %param.9, s32[1024]{0:T(1024)S(1)} %pad_clamp_fusion.1), kind=kCustom, calls=%fused_computation.7 | custom fusion | bytes 1050624 | tf_op jit(solution)/shard_map/gather | solution.py:90
  97.8 5.4 %gather_fusion.1 = bf16[512,512]{1,0:T(8,128)(2,1)} fusion(bf16[4096,512]{1,0:T(8,128)(2,1)} %param.9, s32[1024]{0:T(1024)S(1)} %pad_clamp_fusion.7), kind=kCustom, calls=%fused_computation.1 | custom fusion | bytes 1050624 | tf_op jit(solution)/shard_map/gather | solution.py:90
  105.0 3.0 %collective-permute-start.22 = (bf16[512,256]{1,0:T(8,128)(2,1)}, bf16[512,256]{1,0:T(8,128)(2,1)S(1)}, u32[]{:S(2)}, u32[]{:S(2)}) collective-permute-start(bf16[512,256]{1,0:T(8,128)(2,1)} %bitcast_select_fusion.1), channel_id=1, source_target_pairs={{0,24},{4,28},{8,16},{12,20},{16,8},{20,12},{24,0},{28,4},{1,25},{... | collective-permute-start | bytes 786440 | tf_op jit(solution)/shard_map/ppermute | solution.py:11
  111.5 4.4 %collective-permute-done.22 = bf16[512,256]{1,0:T(8,128)(2,1)S(1)} collective-permute-done((bf16[512,256]{1,0:T(8,128)(2,1)}, bf16[512,256]{1,0:T(8,128)(2,1)S(1)}, u32[]{:S(2)}, u32[]{:S(2)}) %collective-permute-start.22) | collective-permute-done | bytes 262176 | tf_op jit(solution)/shard_map/ppermute | solution.py:11
  115.9 1.4 collective-permute-start.23
  117.3 1.8 fusion.2
  121.3 3.8 %collective-permute-done.23 = bf16[512,256]{1,0:T(8,128)(2,1)S(1)} collective-permute-done((bf16[512,256]{1,0:T(8,128)(2,1)S(1)}, bf16[512,256]{1,0:T(8,128)(2,1)S(1)}, u32[]{:S(2)}, u32[]{:S(2)}) %collective-permute-start.23) | collective-permute-done | bytes 262176 | tf_op jit(solution)/shard_map/ppermute | solution.py:11
  125.2 2.4 %collective-permute-start.26 = (bf16[512,256]{1,0:T(8,128)(2,1)S(1)}, bf16[512,256]{1,0:T(8,128)(2,1)S(1)}, u32[]{:S(2)}, u32[]{:S(2)}) collective-permute-start(bf16[512,256]{1,0:T(8,128)(2,1)S(1)} %bitcast_select_fusion), channel_id=1, source_target_pairs={{0,28},{4,24},{8,20},{12,16},{16,12},{20,8},{24,4},{28,0},{1,29},{... | collective-permute-start | bytes 786440 | tf_op jit(solution)/shard_map/ppermute | solution.py:11
  127.7 1.8 fusion.16
  129.7 7.0 %collective-permute-done.26 = bf16[512,256]{1,0:T(8,128)(2,1)S(1)} collective-permute-done((bf16[512,256]{1,0:T(8,128)(2,1)S(1)}, bf16[512,256]{1,0:T(8,128)(2,1)S(1)}, u32[]{:S(2)}, u32[]{:S(2)}) %collective-permute-start.26) | collective-permute-done | bytes 262176 | tf_op jit(solution)/shard_map/ppermute | solution.py:11
  137.4 1.8 fusion.22
  139.1 1.8 fusion.28
  140.9 3.8 %collective-permute-done.27 = bf16[512,256]{1,0:T(8,128)(2,1)S(1)} collective-permute-done((bf16[512,256]{1,0:T(8,128)(2,1)S(1)}, bf16[512,256]{1,0:T(8,128)(2,1)S(1)}, u32[]{:S(2)}, u32[]{:S(2)}) %collective-permute-start.27) | collective-permute-done | bytes 262176 | tf_op jit(solution)/shard_map/ppermute | solution.py:11
  144.8 1.7 fusion.34
  149.5 2.1 gather_fusion.8
  151.6 2.9 %copy.59 = f32[1024,512]{0,1:T(8,128)} copy(f32[1024,512]{1,0:T(8,128)} %bitcast.106) | data formatting | bytes 4194304 | tf_op jit(solution)/shard_map/reshape | solution.py:96
  154.5 2.6 %sub.30 = f32[1024,512]{0,1:T(8,128)S(1)} subtract(f32[1024,512]{0,1:T(8,128)} %convert_dynamic-update-slice_fusion, f32[1024,512]{0,1:T(8,128)} %copy.59) | non-fusion elementwise | flops 524288 | bytes 6291456 | tf_op jit(solution)/shard_map/sub | solution.py:100
  158.2 1.8 fusion.52
  163.2 2.5 %copy.60 = f32[1024,256]{1,0:T(8,128)} copy(f32[1024,256]{0,1:T(8,128)} %pad_maximum_fusion) | data formatting | bytes 2097152 | tf_op jit(solution)/shard_map/reshape | solution.py:109
  171.6 1.6 copy.61
  174.2 6.1 %collective-permute-start.33 = (f32[4,128,256]{2,1,0:T(8,128)}, f32[4,128,256]{2,1,0:T(8,128)}, u32[]{:S(2)}, u32[]{:S(2)}) collective-permute-start(f32[4,128,256]{2,1,0:T(8,128)} %pad_maximum_fusion.11), channel_id=1, source_target_pairs={{0,8},{4,12},{8,0},{12,4},{16,24},{20,28},{24,16},{28,20},{1,9},{5... | collective-permute-start | bytes 1572872 | tf_op jit(solution)/shard_map/ppermute | solution.py:11
  180.2 2.3 %collective-permute-done.30 = f32[4,128,256]{2,1,0:T(8,128)} collective-permute-done((f32[4,128,256]{2,1,0:T(8,128)}, f32[4,128,256]{2,1,0:T(8,128)}, u32[]{:S(2)}, u32[]{:S(2)}) %collective-permute-start.30) | collective-permute-done | bytes 524320 | tf_op jit(solution)/shard_map/ppermute | solution.py:11
  184.2 5.2 %collective-permute-start.31 = (f32[2,128,256]{2,1,0:T(8,128)}, f32[2,128,256]{2,1,0:T(8,128)S(1)}, u32[]{:S(2)}, u32[]{:S(2)}) collective-permute-start(f32[2,128,256]{2,1,0:T(8,128)} %pad_maximum_fusion.12), channel_id=1, source_target_pairs={{0,8},{4,12},{8,0},{12,4},{16,24},{20,28},{24,16},{28,20},{1,9},{5... | collective-permute-start | bytes 786440 | tf_op jit(solution)/shard_map/ppermute | solution.py:11
  189.4 3.9 %collective-permute-done.33 = f32[4,128,256]{2,1,0:T(8,128)} collective-permute-done((f32[4,128,256]{2,1,0:T(8,128)}, f32[4,128,256]{2,1,0:T(8,128)}, u32[]{:S(2)}, u32[]{:S(2)}) %collective-permute-start.33) | collective-permute-done | bytes 524320 | tf_op jit(solution)/shard_map/ppermute | solution.py:11
  195.0 1.8 collective-permute-start.34
  196.8 2.9 %collective-permute-done.31 = f32[2,128,256]{2,1,0:T(8,128)S(1)} collective-permute-done((f32[2,128,256]{2,1,0:T(8,128)}, f32[2,128,256]{2,1,0:T(8,128)S(1)}, u32[]{:S(2)}, u32[]{:S(2)}) %collective-permute-start.31) | collective-permute-done | bytes 262176 | tf_op jit(solution)/shard_map/ppermute | solution.py:11
  201.1 12.3 %collective-permute-done.34 = f32[2,128,256]{2,1,0:T(8,128)} collective-permute-done((f32[2,128,256]{2,1,0:T(8,128)}, f32[2,128,256]{2,1,0:T(8,128)}, u32[]{:S(2)}, u32[]{:S(2)}) %collective-permute-start.34) | collective-permute-done | bytes 262176 | tf_op jit(solution)/shard_map/ppermute | solution.py:11
  216.1 3.4 %collective-permute-done.35 = f32[1,128,256]{2,1,0:T(8,128)S(1)} collective-permute-done((f32[1,128,256]{2,1,0:T(8,128)S(1)}, f32[1,128,256]{2,1,0:T(8,128)S(1)}, u32[]{:S(2)}, u32[]{:S(2)}) %collective-permute-start.35) | collective-permute-done | bytes 131104 | tf_op jit(solution)/shard_map/ppermute | solution.py:11
  (138 shorter events, 44.1 us)
Async XLA Ops:
  0.0 157.1 %copy-start = (f32[512,512]{1,0:T(8,128)S(1)}, f32[512,512]{1,0:T(8,128)}, u32[]{:S(2)}) copy-start(f32[512,512]{1,0:T(8,128)} %param.15) | copy-start | bytes 3145732
  17.4 5.0 %copy-start.15 = (s32[4096]{0:T(1024)S(1)}, s32[4096]{0:T(1024)}, u32[]{:S(2)}) copy-start(s32[4096]{0:T(1024)} %param.10) | copy-start | bytes 49156
  17.4 12.8 %copy-start.14 = (bf16[128,512]{1,0:T(8,128)(2,1)S(1)}, bf16[128,512]{1,0:T(8,128)(2,1)}, u32[]{:S(2)}) copy-start(bf16[128,512]{1,0:T(8,128)(2,1)} %param.12) | copy-start | bytes 393220
  19.3 33.7 %collective-permute-start.6 = (bf16[512,256]{1,0:T(8,128)(2,1)S(1)}, bf16[512,256]{1,0:T(8,128)(2,1)}, u32[]{:S(2)}, u32[]{:S(2)}) collective-permute-start(bf16[512,256]{1,0:T(8,128)(2,1)S(1)} %bitcast_select_fusion.5), channel_id=1, source_target_pairs={{0,8},{4,12},{8,0},{12,4},{16,24},{20,28},{24,16},{28,20},{1,9},{5... | collective-permute-start | bytes 786440 | tf_op jit(solution)/shard_map/ppermute | solution.py:11
  22.5 12.4 %collective-permute-start.9 = (s32[4,128]{1,0:T(4,128)S(1)}, s32[4,128]{1,0:T(4,128)S(1)}, u32[]{:S(2)}, u32[]{:S(2)}) collective-permute-start(s32[4,128]{1,0:T(4,128)S(1)} %bitcast.133), channel_id=1, source_target_pairs={{0,8},{4,12},{8,0},{12,4},{16,24},{20,28},{24,16},{28,20},{1,9},{5... | collective-permute-start | bytes 6152 | tf_op jit(solution)/shard_map/ppermute | solution.py:11
  22.6 12.4 %collective-permute-start.13 = (s32[4,128]{1,0:T(4,128)S(1)}, s32[4,128]{1,0:T(4,128)S(1)}, u32[]{:S(2)}, u32[]{:S(2)}) collective-permute-start(s32[4,128]{1,0:T(4,128)S(1)} %bitcast.132), channel_id=1, source_target_pairs={{0,12},{4,8},{8,4},{12,0},{16,28},{20,24},{24,20},{28,16},{1,13},{... | collective-permute-start | bytes 6152 | tf_op jit(solution)/shard_map/ppermute | solution.py:11
  26.4 28.3 %collective-permute-start.10 = (bf16[512,256]{1,0:T(8,128)(2,1)}, bf16[512,256]{1,0:T(8,128)(2,1)}, u32[]{:S(2)}, u32[]{:S(2)}) collective-permute-start(bf16[512,256]{1,0:T(8,128)(2,1)} %bitcast_select_fusion.4), channel_id=1, source_target_pairs={{0,12},{4,8},{8,4},{12,0},{16,28},{20,24},{24,20},{28,16},{1,13},{... | collective-permute-start | bytes 786440 | tf_op jit(solution)/shard_map/ppermute | solution.py:11
  27.3 27.3 %collective-permute-start.14 = (bf16[512,256]{1,0:T(8,128)(2,1)}, bf16[512,256]{1,0:T(8,128)(2,1)}, u32[]{:S(2)}, u32[]{:S(2)}) collective-permute-start(bf16[512,256]{1,0:T(8,128)(2,1)} %bitcast_select_fusion.3), channel_id=1, source_target_pairs={{0,16},{4,20},{8,24},{12,28},{16,0},{20,4},{24,8},{28,12},{1,17},{... | collective-permute-start | bytes 786440 | tf_op jit(solution)/shard_map/ppermute | solution.py:11
  34.9 7.6 %collective-permute-start.17 = (s32[4,128]{1,0:T(4,128)S(1)}, s32[4,128]{1,0:T(4,128)S(1)}, u32[]{:S(2)}, u32[]{:S(2)}) collective-permute-start(s32[4,128]{1,0:T(4,128)S(1)} %bitcast.130), channel_id=1, source_target_pairs={{0,16},{4,20},{8,24},{12,28},{16,0},{20,4},{24,8},{28,12},{1,17},{... | collective-permute-start | bytes 6152 | tf_op jit(solution)/shard_map/ppermute | solution.py:11
  34.9 3.9 %collective-permute-start.5 = (s32[4,128]{1,0:T(4,128)S(1)}, s32[4,128]{1,0:T(4,128)S(1)}, u32[]{:S(2)}, u32[]{:S(2)}) collective-permute-start(s32[4,128]{1,0:T(4,128)S(1)} %bitcast.131), channel_id=1, source_target_pairs={{0,4},{4,0},{8,12},{12,8},{16,20},{20,16},{24,28},{28,24},{1,5},{5... | collective-permute-start | bytes 6152 | tf_op jit(solution)/shard_map/ppermute | solution.py:11
  38.8 6.4 %collective-permute-start.21 = (s32[4,128]{1,0:T(4,128)S(1)}, s32[4,128]{1,0:T(4,128)S(1)}, u32[]{:S(2)}, u32[]{:S(2)}) collective-permute-start(s32[4,128]{1,0:T(4,128)S(1)} %bitcast.129), channel_id=1, source_target_pairs={{0,20},{4,16},{8,28},{12,24},{16,4},{20,0},{24,12},{28,8},{1,21},{... | collective-permute-start | bytes 6152 | tf_op jit(solution)/shard_map/ppermute | solution.py:11
  42.4 6.4 %collective-permute-start.25 = (s32[4,128]{1,0:T(4,128)S(1)}, s32[4,128]{1,0:T(4,128)S(1)}, u32[]{:S(2)}, u32[]{:S(2)}) collective-permute-start(s32[4,128]{1,0:T(4,128)S(1)} %bitcast.128), channel_id=1, source_target_pairs={{0,24},{4,28},{8,16},{12,20},{16,8},{20,12},{24,0},{28,4},{1,25},{... | collective-permute-start | bytes 6152 | tf_op jit(solution)/shard_map/ppermute | solution.py:11
  45.2 6.4 %collective-permute-start.29 = (s32[4,128]{1,0:T(4,128)S(1)}, s32[4,128]{1,0:T(4,128)S(1)}, u32[]{:S(2)}, u32[]{:S(2)}) collective-permute-start(s32[4,128]{1,0:T(4,128)S(1)} %bitcast.127), channel_id=1, source_target_pairs={{0,28},{4,24},{8,20},{12,16},{16,12},{20,8},{24,4},{28,0},{1,29},{... | collective-permute-start | bytes 6152 | tf_op jit(solution)/shard_map/ppermute | solution.py:11
  48.9 9.3 %collective-permute-start = (bf16[512,256]{1,0:T(8,128)(2,1)S(1)}, bf16[512,256]{1,0:T(8,128)(2,1)S(1)}, u32[]{:S(2)}, u32[]{:S(2)}) collective-permute-start(bf16[512,256]{1,0:T(8,128)(2,1)S(1)} %bitcast_select_fusion.7), channel_id=1, source_target_pairs={{0,2},{1,3},{2,0},{3,1},{4,6},{5,7},{6,4},{7,5},{8,10},{9,11},{10,... | collective-permute-start | bytes 786440 | tf_op jit(solution)/shard_map/ppermute | solution.py:11
  51.5 9.0 %collective-permute-start.2 = (bf16[512,256]{1,0:T(8,128)(2,1)S(1)}, bf16[512,256]{1,0:T(8,128)(2,1)S(1)}, u32[]{:S(2)}, u32[]{:S(2)}) collective-permute-start(bf16[512,256]{1,0:T(8,128)(2,1)S(1)} %bitcast_select_fusion.6), channel_id=1, source_target_pairs={{0,4},{4,0},{8,12},{12,8},{16,20},{20,16},{24,28},{28,24},{1,5},{5... | collective-permute-start | bytes 786440 | tf_op jit(solution)/shard_map/ppermute | solution.py:11
  53.0 50.2 %collective-permute-start.7 = (bf16[512,256]{1,0:T(8,128)(2,1)}, bf16[512,256]{1,0:T(8,128)(2,1)}, u32[]{:S(2)}, u32[]{:S(2)}) collective-permute-start(bf16[512,256]{1,0:T(8,128)(2,1)} %collective-permute-done.6), channel_id=1, source_target_pairs={{0,2},{1,3},{2,0},{3,1},{4,6},{5,7},{6,4},{7,5},{8,10},{9,11},{10,... | collective-permute-start | bytes 786440 | tf_op jit(solution)/shard_map/ppermute | solution.py:11
  54.6 50.4 %collective-permute-start.18 = (bf16[512,256]{1,0:T(8,128)(2,1)}, bf16[512,256]{1,0:T(8,128)(2,1)}, u32[]{:S(2)}, u32[]{:S(2)}) collective-permute-start(bf16[512,256]{1,0:T(8,128)(2,1)} %bitcast_select_fusion.2), channel_id=1, source_target_pairs={{0,20},{4,16},{8,28},{12,24},{16,4},{20,0},{24,12},{28,8},{1,21},{... | collective-permute-start | bytes 786440 | tf_op jit(solution)/shard_map/ppermute | solution.py:11
  54.7 50.4 %collective-permute-start.11 = (bf16[512,256]{1,0:T(8,128)(2,1)}, bf16[512,256]{1,0:T(8,128)(2,1)}, u32[]{:S(2)}, u32[]{:S(2)}) collective-permute-start(bf16[512,256]{1,0:T(8,128)(2,1)} %collective-permute-done.10), channel_id=1, source_target_pairs={{0,2},{1,3},{2,0},{3,1},{4,6},{5,7},{6,4},{7,5},{8,10},{9,11},{10,... | collective-permute-start | bytes 786440 | tf_op jit(solution)/shard_map/ppermute | solution.py:11
  58.2 9.3 %copy-start.12 = (bf16[512,256]{1,0:T(8,128)(2,1)}, bf16[512,256]{1,0:T(8,128)(2,1)S(1)}, u32[]{:S(2)}) copy-start(bf16[512,256]{1,0:T(8,128)(2,1)S(1)} %collective-permute-done) | copy-start | bytes 786436
  59.1 51.8 %collective-permute-start.1 = (bf16[512,512]{1,0:T(8,128)(2,1)}, bf16[512,512]{1,0:T(8,128)(2,1)}, u32[]{:S(2)}, u32[]{:S(2)}) collective-permute-start(bf16[512,512]{1,0:T(8,128)(2,1)} %pad_maximum_fusion.2), channel_id=1, source_target_pairs={{0,1},{1,0},{2,3},{3,2},{4,5},{5,4},{6,7},{7,6},{8,9},{9,8},{10,11... | collective-permute-start | bytes 1572872 | tf_op jit(solution)/shard_map/ppermute | solution.py:11
  60.5 48.6 %collective-permute-start.15 = (bf16[512,256]{1,0:T(8,128)(2,1)}, bf16[512,256]{1,0:T(8,128)(2,1)}, u32[]{:S(2)}, u32[]{:S(2)}) collective-permute-start(bf16[512,256]{1,0:T(8,128)(2,1)} %collective-permute-done.14), channel_id=1, source_target_pairs={{0,2},{1,3},{2,0},{3,1},{4,6},{5,7},{6,4},{7,5},{8,10},{9,11},{10,... | collective-permute-start | bytes 786440 | tf_op jit(solution)/shard_map/ppermute | solution.py:11
  103.2 14.1 %copy-start.11 = (bf16[512,512]{1,0:T(8,128)(2,1)S(1)}, bf16[512,512]{1,0:T(8,128)(2,1)}, u32[]{:S(2)}) copy-start(bf16[512,512]{1,0:T(8,128)(2,1)} %gather_fusion) | copy-start | bytes 1572868
  103.2 14.1 %copy-start.13 = (bf16[512,256]{1,0:T(8,128)(2,1)S(1)}, bf16[512,256]{1,0:T(8,128)(2,1)}, u32[]{:S(2)}) copy-start(bf16[512,256]{1,0:T(8,128)(2,1)} %copy-done.12) | copy-start | bytes 786436
  103.2 7.2 %collective-permute-start.3 = (bf16[512,256]{1,0:T(8,128)(2,1)S(1)}, bf16[512,256]{1,0:T(8,128)(2,1)S(1)}, u32[]{:S(2)}, u32[]{:S(2)}) collective-permute-start(bf16[512,256]{1,0:T(8,128)(2,1)S(1)} %collective-permute-done.2), channel_id=1, source_target_pairs={{0,2},{1,3},{2,0},{3,1},{4,6},{5,7},{6,4},{7,5},{8,10},{9,11},{10,... | collective-permute-start | bytes 786440 | tf_op jit(solution)/shard_map/ppermute | solution.py:11
  104.9 20.2 %collective-permute-start.8 = (bf16[512,512]{1,0:T(8,128)(2,1)S(1)}, bf16[512,512]{1,0:T(8,128)(2,1)S(1)}, u32[]{:S(2)}, u32[]{:S(2)}) collective-permute-start(bf16[512,512]{1,0:T(8,128)(2,1)S(1)} %pad_maximum_fusion.4), channel_id=1, source_target_pairs={{0,1},{1,0},{2,3},{3,2},{4,5},{5,4},{6,7},{7,6},{8,9},{9,8},{10,11... | collective-permute-start | bytes 1572872 | tf_op jit(solution)/shard_map/ppermute | solution.py:11
  105.0 10.8 %collective-permute-start.22 = (bf16[512,256]{1,0:T(8,128)(2,1)}, bf16[512,256]{1,0:T(8,128)(2,1)S(1)}, u32[]{:S(2)}, u32[]{:S(2)}) collective-permute-start(bf16[512,256]{1,0:T(8,128)(2,1)} %bitcast_select_fusion.1), channel_id=1, source_target_pairs={{0,24},{4,28},{8,16},{12,20},{16,8},{20,12},{24,0},{28,4},{1,25},{... | collective-permute-start | bytes 786440 | tf_op jit(solution)/shard_map/ppermute | solution.py:11
  109.1 20.3 %collective-permute-start.12 = (bf16[512,512]{1,0:T(8,128)(2,1)S(1)}, bf16[512,512]{1,0:T(8,128)(2,1)S(1)}, u32[]{:S(2)}, u32[]{:S(2)}) collective-permute-start(bf16[512,512]{1,0:T(8,128)(2,1)S(1)} %pad_maximum_fusion.5), channel_id=1, source_target_pairs={{0,1},{1,0},{2,3},{3,2},{4,5},{5,4},{6,7},{7,6},{8,9},{9,8},{10,11... | collective-permute-start | bytes 1572872 | tf_op jit(solution)/shard_map/ppermute | solution.py:11
  110.4 28.7 %collective-permute-start.16 = (bf16[512,512]{1,0:T(8,128)(2,1)S(1)}, bf16[512,512]{1,0:T(8,128)(2,1)S(1)}, u32[]{:S(2)}, u32[]{:S(2)}) collective-permute-start(bf16[512,512]{1,0:T(8,128)(2,1)S(1)} %pad_maximum_fusion.6), channel_id=1, source_target_pairs={{0,1},{1,0},{2,3},{3,2},{4,5},{5,4},{6,7},{7,6},{8,9},{9,8},{10,11... | collective-permute-start | bytes 1572872 | tf_op jit(solution)/shard_map/ppermute | solution.py:11
  110.9 9.4 %collective-permute-start.19 = (bf16[512,256]{1,0:T(8,128)(2,1)}, bf16[512,256]{1,0:T(8,128)(2,1)S(1)}, u32[]{:S(2)}, u32[]{:S(2)}) collective-permute-start(bf16[512,256]{1,0:T(8,128)(2,1)} %collective-permute-done.18), channel_id=1, source_target_pairs={{0,2},{1,3},{2,0},{3,1},{4,6},{5,7},{6,4},{7,5},{8,10},{9,11},{10,... | collective-permute-start | bytes 786440 | tf_op jit(solution)/shard_map/ppermute | solution.py:11
  115.9 9.3 %collective-permute-start.23 = (bf16[512,256]{1,0:T(8,128)(2,1)S(1)}, bf16[512,256]{1,0:T(8,128)(2,1)S(1)}, u32[]{:S(2)}, u32[]{:S(2)}) collective-permute-start(bf16[512,256]{1,0:T(8,128)(2,1)S(1)} %collective-permute-done.22), channel_id=1, source_target_pairs={{0,2},{1,3},{2,0},{3,1},{4,6},{5,7},{6,4},{7,5},{8,10},{9,11},{10,... | collective-permute-start | bytes 786440 | tf_op jit(solution)/shard_map/ppermute | solution.py:11
  119.1 8.6 %copy-start.10 = (bf16[512,512]{1,0:T(8,128)(2,1)S(1)}, bf16[512,512]{1,0:T(8,128)(2,1)}, u32[]{:S(2)}) copy-start(bf16[512,512]{1,0:T(8,128)(2,1)} %gather_fusion.2) | copy-start | bytes 1572868
  120.3 27.7 %collective-permute-start.4 = (bf16[512,512]{1,0:T(8,128)(2,1)S(1)}, bf16[512,512]{1,0:T(8,128)(2,1)S(1)}, u32[]{:S(2)}, u32[]{:S(2)}) collective-permute-start(bf16[512,512]{1,0:T(8,128)(2,1)S(1)} %pad_maximum_fusion.3), channel_id=1, source_target_pairs={{0,1},{1,0},{2,3},{3,2},{4,5},{5,4},{6,7},{7,6},{8,9},{9,8},{10,11... | collective-permute-start | bytes 1572872 | tf_op jit(solution)/shard_map/ppermute | solution.py:11
  125.1 19.6 %collective-permute-start.20 = (bf16[512,512]{1,0:T(8,128)(2,1)S(1)}, bf16[512,512]{1,0:T(8,128)(2,1)S(1)}, u32[]{:S(2)}, u32[]{:S(2)}) collective-permute-start(bf16[512,512]{1,0:T(8,128)(2,1)S(1)} %pad_maximum_fusion.7), channel_id=1, source_target_pairs={{0,1},{1,0},{2,3},{3,2},{4,5},{5,4},{6,7},{7,6},{8,9},{9,8},{10,11... | collective-permute-start | bytes 1572872 | tf_op jit(solution)/shard_map/ppermute | solution.py:11
  125.2 12.2 %copy-start.9 = (bf16[512,512]{1,0:T(8,128)(2,1)S(1)}, bf16[512,512]{1,0:T(8,128)(2,1)}, u32[]{:S(2)}) copy-start(bf16[512,512]{1,0:T(8,128)(2,1)} %gather_fusion.3) | copy-start | bytes 1572868
  125.2 11.6 %collective-permute-start.26 = (bf16[512,256]{1,0:T(8,128)(2,1)S(1)}, bf16[512,256]{1,0:T(8,128)(2,1)S(1)}, u32[]{:S(2)}, u32[]{:S(2)}) collective-permute-start(bf16[512,256]{1,0:T(8,128)(2,1)S(1)} %bitcast_select_fusion), channel_id=1, source_target_pairs={{0,28},{4,24},{8,20},{12,16},{16,12},{20,8},{24,4},{28,0},{1,29},{... | collective-permute-start | bytes 786440 | tf_op jit(solution)/shard_map/ppermute | solution.py:11
  129.4 9.7 %copy-start.8 = (bf16[512,512]{1,0:T(8,128)(2,1)S(1)}, bf16[512,512]{1,0:T(8,128)(2,1)}, u32[]{:S(2)}) copy-start(bf16[512,512]{1,0:T(8,128)(2,1)} %gather_fusion.4) | copy-start | bytes 1572868
  129.4 17.0 %collective-permute-start.24 = (bf16[512,512]{1,0:T(8,128)(2,1)S(1)}, bf16[512,512]{1,0:T(8,128)(2,1)S(1)}, u32[]{:S(2)}, u32[]{:S(2)}) collective-permute-start(bf16[512,512]{1,0:T(8,128)(2,1)S(1)} %pad_maximum_fusion.8), channel_id=1, source_target_pairs={{0,1},{1,0},{2,3},{3,2},{4,5},{5,4},{6,7},{7,6},{8,9},{9,8},{10,11... | collective-permute-start | bytes 1572872 | tf_op jit(solution)/shard_map/ppermute | solution.py:11
  136.8 7.9 %collective-permute-start.27 = (bf16[512,256]{1,0:T(8,128)(2,1)S(1)}, bf16[512,256]{1,0:T(8,128)(2,1)S(1)}, u32[]{:S(2)}, u32[]{:S(2)}) collective-permute-start(bf16[512,256]{1,0:T(8,128)(2,1)S(1)} %collective-permute-done.26), channel_id=1, source_target_pairs={{0,2},{1,3},{2,0},{3,1},{4,6},{5,7},{6,4},{7,5},{8,10},{9,11},{10,... | collective-permute-start | bytes 786440 | tf_op jit(solution)/shard_map/ppermute | solution.py:11
  144.7 2.5 %collective-permute-start.28 = (bf16[512,512]{1,0:T(8,128)(2,1)S(1)}, bf16[512,512]{1,0:T(8,128)(2,1)S(1)}, u32[]{:S(2)}, u32[]{:S(2)}) collective-permute-start(bf16[512,512]{1,0:T(8,128)(2,1)S(1)} %pad_maximum_fusion.9), channel_id=1, source_target_pairs={{0,1},{1,0},{2,3},{3,2},{4,5},{5,4},{6,7},{7,6},{8,9},{9,8},{10,11... | collective-permute-start | bytes 1572872 | tf_op jit(solution)/shard_map/ppermute | solution.py:11
  157.1 2.9 %copy-start.2 = (f32[512,512]{1,0:T(8,128)S(1)}, f32[512,512]{1,0:T(8,128)}, u32[]{:S(2)}) copy-start(f32[512,512]{1,0:T(8,128)} %param.13) | copy-start | bytes 3145732
  158.2 2.9 %copy-start.4 = (f32[512,512]{1,0:T(8,128)S(1)}, f32[512,512]{1,0:T(8,128)}, u32[]{:S(2)}) copy-start(f32[512,512]{1,0:T(8,128)} %param.14) | copy-start | bytes 3145732
  167.9 14.6 %collective-permute-start.30 = (f32[4,128,256]{2,1,0:T(8,128)}, f32[4,128,256]{2,1,0:T(8,128)}, u32[]{:S(2)}, u32[]{:S(2)}) collective-permute-start(f32[4,128,256]{2,1,0:T(8,128)} %pad_maximum_fusion.10), channel_id=1, source_target_pairs={{0,4},{4,0},{8,12},{12,8},{16,20},{20,16},{24,28},{28,24},{1,5},{5... | collective-permute-start | bytes 1572872 | tf_op jit(solution)/shard_map/ppermute | solution.py:11
  171.6 10.9 %copy-start.6 = (f32[1024,256]{1,0:T(8,128)S(1)}, f32[1024,256]{1,0:T(8,128)}, u32[]{:S(2)}) copy-start(f32[1024,256]{1,0:T(8,128)} %copy.60) | copy-start | bytes 3145732
  174.2 19.1 %collective-permute-start.33 = (f32[4,128,256]{2,1,0:T(8,128)}, f32[4,128,256]{2,1,0:T(8,128)}, u32[]{:S(2)}, u32[]{:S(2)}) collective-permute-start(f32[4,128,256]{2,1,0:T(8,128)} %pad_maximum_fusion.11), channel_id=1, source_target_pairs={{0,8},{4,12},{8,0},{12,4},{16,24},{20,28},{24,16},{28,20},{1,9},{5... | collective-permute-start | bytes 1572872 | tf_op jit(solution)/shard_map/ppermute | solution.py:11
  184.2 15.4 %collective-permute-start.31 = (f32[2,128,256]{2,1,0:T(8,128)}, f32[2,128,256]{2,1,0:T(8,128)S(1)}, u32[]{:S(2)}, u32[]{:S(2)}) collective-permute-start(f32[2,128,256]{2,1,0:T(8,128)} %pad_maximum_fusion.12), channel_id=1, source_target_pairs={{0,8},{4,12},{8,0},{12,4},{16,24},{20,28},{24,16},{28,20},{1,9},{5... | collective-permute-start | bytes 786440 | tf_op jit(solution)/shard_map/ppermute | solution.py:11
  195.0 18.5 %collective-permute-start.34 = (f32[2,128,256]{2,1,0:T(8,128)}, f32[2,128,256]{2,1,0:T(8,128)}, u32[]{:S(2)}, u32[]{:S(2)}) collective-permute-start(f32[2,128,256]{2,1,0:T(8,128)} %pad_maximum_fusion.13), channel_id=1, source_target_pairs={{0,16},{4,20},{8,24},{12,28},{16,0},{20,4},{24,8},{28,12},{1,17},{... | collective-permute-start | bytes 786440 | tf_op jit(solution)/shard_map/ppermute | solution.py:11
  200.6 14.6 %collective-permute-start.32 = (f32[1,128,256]{2,1,0:T(8,128)S(1)}, f32[1,128,256]{2,1,0:T(8,128)S(1)}, u32[]{:S(2)}, u32[]{:S(2)}) collective-permute-start(f32[1,128,256]{2,1,0:T(8,128)S(1)} %slice_add_fusion.6), channel_id=1, source_target_pairs={{0,16},{4,20},{8,24},{12,28},{16,0},{20,4},{24,8},{28,12},{1,17},{... | collective-permute-start | bytes 393224 | tf_op jit(solution)/shard_map/ppermute | solution.py:11
  214.5 5.0 %collective-permute-start.35 = (f32[1,128,256]{2,1,0:T(8,128)S(1)}, f32[1,128,256]{2,1,0:T(8,128)S(1)}, u32[]{:S(2)}, u32[]{:S(2)}) collective-permute-start(f32[1,128,256]{2,1,0:T(8,128)S(1)} %slice_add_fusion), channel_id=1, source_target_pairs={{0,4},{4,0},{8,12},{12,8},{16,20},{20,16},{24,28},{28,24},{1,5},{5... | collective-permute-start | bytes 393224 | tf_op jit(solution)/shard_map/ppermute | solution.py:11
  (4 other events, 8.9 us)

commit v2 on v0

v2 whole, which is shorter than its diff:
```python
import functools

import jax
import jax.numpy as jnp
from jax import lax
from jax.experimental import pallas as pl
from jax.experimental.pallas import tpu as pltpu
from jax.sharding import PartitionSpec as P

BLK = 128
LANES = 128
ANY = pl.BlockSpec(memory_space=pl.ANY)
VMEM = pl.BlockSpec(memory_space=pltpu.VMEM)
SMEM = pl.BlockSpec(memory_space=pltpu.SMEM)


def swap(array, axis, mask):
    size = lax.axis_size(axis)
    return lax.ppermute(array, axis, [(i, i ^ mask) for i in range(size)])


def pack_kernel(groups, slots, rows_ref, live_ref, lists_ref, panels_ref, *refs):
    chunks, place_ref, tile_ref = refs[: groups + 1], refs[groups + 1], refs[groups + 2]
    me = lax.axis_index("rows")
    rows_dev = rows_ref.shape[0]
    for place in range(groups):
        place_ref[lax.div(rows_ref[place * BLK], rows_dev) ^ me] = place
    live_blocks = lax.div(live_ref[0], BLK)
    tile_ref[...] = jnp.zeros_like(tile_ref)
    for mask in range(groups):
        start = (mask ^ me) * rows_dev
        for slot in range(slots):
            row = slot * groups + place_ref[mask]
            local = lists_ref[pl.ds(row, 1), :] - start
            tile_ref[pl.ds(2 * slot, 1), pl.ds(0, BLK)] = (local >> 8).astype(jnp.float32)
            tile_ref[pl.ds(2 * slot + 1, 1), pl.ds(0, BLK)] = (local & 255).astype(jnp.float32)
        chunk = chunks[mask]
        tile = tile_ref.shape[0]
        chunk[pl.ds(chunk.shape[0] - tile, tile), :] = tile_ref[...].astype(chunk.dtype)
        for at, count, part, into in pieces_of(mask, groups, slots):
            ref = chunks[mask + part]
            block = at // BLK * groups + place_ref[mask]

            @pl.when(block < live_blocks)
            def _():
                first = pl.multiple_of(block * BLK + at % BLK, 16)
                ref[pl.ds(into, count), :] = panels_ref[pl.ds(first, count), :]

            @pl.when(block >= live_blocks)
            def _():
                ref[pl.ds(into, count), :] = jnp.zeros((count, ref.shape[1]), ref.dtype)


def pieces_of(mask, groups, slots):
    cut = slots * BLK // 2 if mask == groups - 1 else slots * BLK
    step = min(BLK, cut)
    for at in range(0, slots * BLK, step):
        yield at, step, int(at >= cut), at % cut


def list_rows(slots):
    return -(-2 * slots // 16) * 16


def pack(lower_panels, parent_rows, live_counts, groups, slots):
    rows_dev, width = lower_panels.shape
    rows, extra = slots * BLK, list_rows(slots)
    counts = [rows + extra] * (groups - 1) + [rows // 2 + extra, rows // 2]
    return pl.pallas_call(
        functools.partial(pack_kernel, groups, slots),
        out_shape=[jax.ShapeDtypeStruct((n, width), lower_panels.dtype) for n in counts],
        in_specs=[SMEM, SMEM, VMEM, VMEM],
        out_specs=[VMEM] * len(counts),
        scratch_shapes=[
            pltpu.SMEM((groups,), jnp.int32),
            pltpu.VMEM((extra, width), jnp.float32),
        ],
        compiler_params=pltpu.CompilerParams(vmem_limit_bytes=24 * 2**20),
        name="pack",
    )(parent_rows, live_counts, parent_rows.reshape(rows_dev // BLK, BLK), lower_panels)


def pick_kernel(groups, slots, parent_ref, *refs):
    chunks, (out_ref, wide, stage, tiles_ref, lists_ref, rows_ref, sems) = refs[:groups], refs[groups:]
    extra = list_rows(slots)
    reads = []
    for mask, chunk in enumerate(chunks):
        from_ref = chunk.at[pl.ds(chunk.shape[0] - extra, extra), :]
        reads.append(pltpu.make_async_copy(from_ref, tiles_ref.at[mask], sems.at[mask]))
        reads[-1].start()
    for read in reads:
        read.wait()
    rows, columns = parent_ref.shape
    tiles = columns // LANES
    for mask in range(groups):
        for slot in range(slots):
            pair = tiles_ref[mask, :, pl.ds(0, BLK)].astype(jnp.float32)[2 * slot : 2 * slot + 2]
            local = pair[0:1] * 256.0 + pair[1:2]
            lists_ref[pl.ds(mask * slots + slot, 1), :] = local.astype(jnp.int32) * tiles
    move = pltpu.make_async_copy(lists_ref, rows_ref, sems.at[groups])
    move.start()
    step = min(rows, 256)

    @pl.loop(0, rows // step)
    def _(i):
        at = pl.multiple_of(i * step, step)
        for tile in range(tiles):
            wide[pl.ds(at * tiles + tile, step, stride=tiles), :] = parent_ref[
                pl.ds(at, step), pl.ds(tile * LANES, LANES)
            ].astype(jnp.float32)

    move.wait()
    nothing = jnp.zeros((extra, columns), out_ref.dtype)
    count = slots * BLK

    @pl.loop(0, groups)
    def _(mask):
        @pl.loop(0, slots)
        def _(slot):
            base = slot * (BLK * tiles)
            for i in range(BLK):
                row = pl.multiple_of(rows_ref[mask * slots + slot, i], tiles)
                into = pl.multiple_of(base + i * tiles, tiles)
                stage[pl.ds(into, tiles), :] = wide[pl.ds(row, tiles), :]

        def write(into, first, rows):
            for tile in range(tiles):
                out_ref[pl.ds(into, rows), pl.ds(tile * LANES, LANES)] = stage[
                    pl.ds(first * tiles + tile, rows, stride=tiles), :
                ].astype(out_ref.dtype)

        into = pl.multiple_of(mask * (count + extra), 16)

        @pl.when(mask < groups - 1)
        def _():
            write(into, 0, count)
            out_ref[pl.ds(pl.multiple_of(into + count, 16), extra), :] = nothing

        @pl.when(mask == groups - 1)
        def _():
            last, cut = (groups - 1) * (count + extra), count // 2
            write(last, 0, cut)
            out_ref[pl.ds(last + cut, extra), :] = nothing
            write(last + cut + extra, cut, cut)


def pick(parent, chunks, slots):
    groups = len(chunks)
    columns = parent.shape[1]
    tiles = columns // LANES
    extra = list_rows(slots)
    width = chunks[0].shape[1]
    return pl.pallas_call(
        functools.partial(pick_kernel, groups, slots),
        out_shape=jax.ShapeDtypeStruct((groups * (slots * BLK + extra), columns), parent.dtype),
        in_specs=[VMEM] + [ANY] * groups,
        out_specs=VMEM,
        scratch_shapes=[
            pltpu.VMEM((parent.shape[0] * tiles, LANES), jnp.float32),
            pltpu.VMEM((slots * BLK * tiles, LANES), jnp.float32),
            pltpu.VMEM((groups, extra, width), parent.dtype),
            pltpu.VMEM((groups * slots, BLK), jnp.int32),
            pltpu.SMEM((groups * slots, BLK), jnp.int32),
            pltpu.SemaphoreType.DMA((groups + 1,)),
        ],
        compiler_params=pltpu.CompilerParams(vmem_limit_bytes=48 * 2**20),
        name="pick",
    )(parent, *chunks)


def split(value):
    high = value.astype(jnp.bfloat16)
    return high, (value - high.astype(jnp.float32)).astype(jnp.bfloat16)


def dot3(left, right):
    dot = functools.partial(jnp.dot, preferred_element_type=jnp.float32)
    (lh, ll), (rh, rl) = left, right
    return dot(lh, rh) + (dot(lh, rl) + dot(ll, rh))


def solve_kernel(orders, near_ref, far_ref, front_ref, coup_ref, one_ref, two_ref, *refs):
    outs, resid = refs[:4], refs[4]
    me = lax.axis_index("rows")
    share = lax.axis_index("rhs")
    pivot_share = front_ref.shape[0]
    pivots, columns = resid.shape
    panel = pivots // 2
    half_shares = lax.axis_size("rhs") // 2
    width = near_ref.shape[0] // half_shares
    for odd, part_ref in ((0, near_ref), (1, far_ref)):
        for i in range(half_shares):
            at = pl.multiple_of((share ^ (2 * i + odd)) * width, width)
            resid[pl.ds(at, width), :] = -part_ref[pl.ds(i * width, width), :]
    mine = pl.ds(pl.multiple_of(me * pivot_share, pivot_share), pivot_share)
    resid[mine, :] += front_ref[...].astype(jnp.float32)
    two, one, coup = split(two_ref[...]), split(one_ref[...]), split(coup_ref[...])
    middle = columns // 2
    groups = pivots // pivot_share
    for side in range(2):
        cols = pl.ds(side * middle, middle)
        second = dot3(two, split(resid[pl.ds(panel, panel), cols]))
        reduced = resid[pl.ds(0, panel), cols] - dot3(coup, split(second))
        first = dot3(one, split(reduced))
        keep_ref, send_ref = outs[2 * side : 2 * side + 2]
        order = orders[side]
        for block in range(groups):
            source = first if block < groups // 2 else second
            at = (block % (groups // 2)) * pivot_share
            value = source[at : at + pivot_share, :]
            rel = block ^ me
            place = sum(
                ((rel >> bit) & 1) << (len(order) - 1 - i) for i, bit in enumerate(order) if i
            )
            sent = (rel >> order[0]) & 1

            @pl.when(sent == 0)
            def _():
                keep_ref[place] = value

            @pl.when(sent == 1)
            def _():
                send_ref[place] = value


def solve(orders, near, far, front_rhs, coupling, one, two, groups):
    pivot_share, columns = front_rhs.shape
    pivots = groups * pivot_share
    out = jax.ShapeDtypeStruct((groups // 2, pivot_share, columns // 2), jnp.float32)
    return pl.pallas_call(
        functools.partial(solve_kernel, orders),
        out_shape=[out] * 4,
        in_specs=[VMEM] * 6,
        out_specs=[VMEM] * 4,
        scratch_shapes=[pltpu.VMEM((pivots, columns), jnp.float32)],
        compiler_params=pltpu.CompilerParams(vmem_limit_bytes=48 * 2**20),
        name="solve",
    )(near, far, front_rhs, coupling, one, two)


def panel_dot(panel, rows):
    return lax.dot_general(
        panel, rows, (((0,), (0,)), ((), ())), preferred_element_type=jnp.float32
    )


def body(
    lower_panels,
    parent_solution,
    parent_rows,
    live_counts,
    front_rhs,
    coupling,
    inverse_one,
    inverse_two,
):
    groups = lax.axis_size("rows")
    shares = lax.axis_size("rhs")
    rows_dev = parent_rows.shape[0]
    slots = rows_dev // BLK // groups
    chunk_rows = slots * BLK
    bits = list(range(groups.bit_length() - 1))

    chunks = pack(lower_panels, parent_rows, live_counts, groups, slots)
    half = groups // 2
    mask_of = list(range(groups)) + [groups - 1]
    got, nears, fars = {0: chunks[0]}, {}, {}

    def after(value, *events):
        held = [store[key] for store, key in events]
        value, held = lax.optimization_barrier((value, held))
        for (store, key), now in zip(events, held):
            store[key] = now
        return value

    def move(at, *events):
        got[at] = swap(after(chunks[at], *events), "rows", mask_of[at])

    def cross(at, *events):
        own = after(got[at], *events)
        nears[at] = jnp.concatenate(
            [own] + [swap(own, "rhs", other) for other in range(2, shares, 2)], axis=1
        )

    runs = [[0], list(range(1, half)), [half, half + 1]] + [[at] for at in range(half + 2, groups + 1)]
    for at in range(half, groups + 1):
        move(at, *([(got, at - 2)] if at >= half + 2 else []))
    for at in range(1, half):
        move(at, *([(got, at - 9)] if at > 9 else []))
    starts = [0]
    for at in range(groups):
        starts.append(starts[at] + chunks[at].shape[0])
    def cross(own):
        return jnp.concatenate(
            [own] + [swap(own, "rhs", other) for other in range(2, shares, 2)], axis=1
        )
    near_total = far_total = 0.0
    picked = pick(parent_solution, [got[at] for at in range(groups)], slots)
    def add(i):
        rows = [picked[starts[at] : starts[at] + chunks[at].shape[0]] for at in runs[i]]
        rows = jnp.concatenate(rows, axis=0)
        return near_total + panel_dot(nears[i], rows), far_total + panel_dot(fars[i], rows)
    done = 0
    for r, run in enumerate(runs):
        if r == len(runs) - 1:
            while done < len(runs) - 1 - 2:
                near_total, far_total = add(done)
                done += 1
            got[groups], near_total, far_total = lax.optimization_barrier((got[groups], near_total, far_total))
        nears[r] = cross(jnp.concatenate([got[at] for at in run], axis=0))
        fars[r] = swap(nears[r], "rhs", 1)
    while done < len(runs):
        near_total, far_total = add(done)
        done += 1

    orders = (bits, bits[1:] + bits[:1])
    keep_a, send_a, keep_b, send_b = solve(
        orders, near_total, far_total, front_rhs, coupling, inverse_one, inverse_two, groups
    )
    for step in range(len(bits)):
        came_a = swap(send_a, "rows", 1 << orders[0][step])
        came_b = swap(send_b, "rows", 1 << orders[1][step])
        came_a, came_b = lax.optimization_barrier((came_a, came_b))
        middle = keep_a.shape[0] // 2
        send_a, send_b = keep_a[middle:] + came_a[middle:], keep_b[middle:] + came_b[middle:]
        if middle:
            keep_a, keep_b = keep_a[:middle] + came_a[:middle], keep_b[:middle] + came_b[:middle]
    return jnp.concatenate([send_a[0], send_b[0]], axis=1)


def solution(mesh):
    return jax.shard_map(
        body,
        mesh=mesh,
        in_specs=(
            P("rows", "rhs"),
            P("rows", "rhs"),
            P("rows"),
            P("rows"),
            P("rows", "rhs"),
            P(),
            P(),
            P(),
        ),
        out_specs=P("rows", "rhs"),
        check_vma=False,
    )
```

time: 254 us -> 139 us (0.55)
  waiting for transfers between devices: 159 us -> 76.1 us
  starting transfers between devices: 4.82 us -> 32.5 us
  blocking collectives: 25.3 us -> 0 us
  local copies, waits for them, and re-layouts: 28.5 us -> 3.84 us
  Pallas kernels: 0 us -> 16.3 us
  between operations: 14.1 us -> 1.03 us
  matrix products: 16 us -> 8.06 us
  other arithmetic: 5.67 us -> 1.16 us
    all_to_all x1 -> x0, waiting for transfers between devices: 90.9 us -> none  [body(): lax.all_to_all(picked, 'rows', split_axis=0, concat_axis=0, tiled=True)]
    ppermute x0 -> x26, waiting for transfers between devices: none -> 76.1 us  [swap(): return lax.ppermute(array, axis, [(i, i ^ mask) for i in range(size)])]
    reduce_scatter x1 -> x0, waiting for transfers between devices: 67.6 us -> none  [body(): lax.psum_scatter(placed_t - product_t, 'rows', scatter_dimension=0, tiled...]
    ppermute x0 -> x26, starting transfers between devices: none -> 32.5 us  [swap(): return lax.ppermute(array, axis, [(i, i ^ mask) for i in range(size)])]
    all_to_all x2 -> x0, blocking collectives: 25.3 us -> none  [the longest x1 13.7 us: body(): lax.all_to_all(requests, 'rows', split_axis=0, concat_axis=0, tiled=True)]
    gather x2 -> x0, local copies, waits for them, and re-layouts: 25.2 us -> none  [the longest x1 20.2 us: body(): parent_solution[received.reshape(-1)]]
    pallas_call x0 -> x3, Pallas kernels: none -> 16.3 us  [the longest x1 7.53 us: pick(): pl.pallas_call(functools.partial(pick_kernel, groups, slots), out_shape=j...]
    dot_general x4 -> x12, matrix products: 16 us -> 8.06 us  [panel_dot(): lax.dot_general(panel, rows, (((0,), (0,)), ((), ())), preferred_element_...]
  transfers between devices with their start and end apart: 3 -> 26, of which waited for: 2 -> 11; matrix products, arithmetic and copies ran while one was open for 13% -> 6% of each run, Pallas kernels for 0% -> 5%
where the time goes in v2:
time: 139 us
  waiting for transfers between devices  76.1 us (55%)
  starting transfers between devices  32.5 us (23%)
  Pallas kernels  16.3 us (12%)
  matrix products  8.06 us (6%)
  local copies, waits for them, and re-layouts  3.84 us (3%)
    ppermute x26, waiting for transfers between devices, swap(): return lax.ppermute(array, axis, [(i, i ^ mask) for i in range(size)])  76.1 us
    ppermute x26, starting transfers between devices, swap(): return lax.ppermute(array, axis, [(i, i ^ mask) for i in range(size)])  32.5 us
    dot_general x12, matrix products, panel_dot(): lax.dot_general(panel, rows, (((0,), (0,)), ((), ())), preferred_element_...  8.06 us
    pallas_call x1, Pallas kernels, pick(): pl.pallas_call(functools.partial(pick_kernel, groups, slots), out_shape=j...  7.53 us
    pallas_call x1, Pallas kernels, solve(): pl.pallas_call(functools.partial(solve_kernel, orders), out_shape=[out] *...  7.4 us
    unnamed x19, local copies, waits for them, and re-layouts  3.75 us
  transfers between devices with their start and end apart: 26, of which 11 were waited for; matrix products, arithmetic and copies ran while one was open for 6% of the time, Pallas kernels for 5%

profile of v2, /device:TPU:0, one launch (start us, length us, event | category | flops | bytes accessed | tf_op | source)
XLA Modules:
  0.0 139.0 jit_solution(6535660561700769309)
XLA Ops:
  0.7 1.6 %copy-done.1 = bf16[4096,256]{1,0:T(8,128)(2,1)S(1)} copy-done((bf16[4096,256]{1,0:T(8,128)(2,1)S(1)}, bf16[4096,256]{1,0:T(8,128)(2,1)}, u32[]{:S(2)}) %copy-start.1) | copy-done | bytes 2097176
  2.2 0.7 copy-done.4
  3.0 1.4 pack.1
  4.3 4.1 %collective-permute-start = (bf16[528,256]{1,0:T(8,128)(2,1)S(1)}, bf16[528,256]{1,0:T(8,128)(2,1)S(1)}, u32[]{:S(2)}, u32[]{:S(2)}) collective-permute-start(bf16[528,256]{1,0:T(8,128)(2,1)S(1)} %get-tuple-element.35), channel_id=1, source_target_pairs={{0,16},{4,20},{8,24},{12,28},{16,0},{20,4},{24,8},{28,12},{1,17},{... | collective-permute-start | bytes 811016 | tf_op jit(solution)/shard_map/ppermute | solution.py:19
  8.5 1.3 collective-permute-start.7
  9.8 0.2 collective-permute-start.4
  10.0 1.8 %collective-permute-start.5 = (bf16[528,256]{1,0:T(8,128)(2,1)S(1)}, bf16[528,256]{1,0:T(8,128)(2,1)S(1)}, u32[]{:S(2)}, u32[]{:S(2)}) collective-permute-start(bf16[528,256]{1,0:T(8,128)(2,1)S(1)} %get-tuple-element.40), channel_id=1, source_target_pairs={{0,8},{4,12},{8,0},{12,4},{16,24},{20,28},{24,16},{28,20},{1,9},{5... | collective-permute-start | bytes 811016 | tf_op jit(solution)/shard_map/ppermute | solution.py:19
  11.8 1.5 %collective-permute-start.3 = (bf16[528,256]{1,0:T(8,128)(2,1)S(1)}, bf16[528,256]{1,0:T(8,128)(2,1)S(1)}, u32[]{:S(2)}, u32[]{:S(2)}) collective-permute-start(bf16[528,256]{1,0:T(8,128)(2,1)S(1)} %get-tuple-element.38.refs_0_), channel_id=1, source_target_pairs={{0,2},{1,3},{2,0},{3,1},{4,6},{5,7},{6,4},{7,5},{8,10},{9,11},{10,... | collective-permute-start | bytes 811016 | tf_op jit(solution)/shard_map/ppermute | solution.py:19
  13.4 14.0 %collective-permute-done.refs_4_ = bf16[528,256]{1,0:T(8,128)(2,1)S(1)} collective-permute-done((bf16[528,256]{1,0:T(8,128)(2,1)S(1)}, bf16[528,256]{1,0:T(8,128)(2,1)S(1)}, u32[]{:S(2)}, u32[]{:S(2)}) %collective-permute-start) | collective-permute-done | bytes 270368 | tf_op jit(solution)/shard_map/ppermute | solution.py:19
  27.4 0.9 collective-permute-start.6
  28.3 5.2 %collective-permute-done.7.refs_5_ = bf16[528,256]{1,0:T(8,128)(2,1)S(1)} collective-permute-done((bf16[528,256]{1,0:T(8,128)(2,1)S(1)}, bf16[528,256]{1,0:T(8,128)(2,1)S(1)}, u32[]{:S(2)}, u32[]{:S(2)}) %collective-permute-start.7) | collective-permute-done | bytes 270368 | tf_op jit(solution)/shard_map/ppermute | solution.py:19
  33.4 3.4 %collective-permute-start.1 = (bf16[528,256]{1,0:T(8,128)(2,1)S(1)}, bf16[528,256]{1,0:T(8,128)(2,1)S(1)}, u32[]{:S(2)}, u32[]{:S(2)}) collective-permute-start(bf16[528,256]{1,0:T(8,128)(2,1)S(1)} %get-tuple-element.36), channel_id=1, source_target_pairs={{0,24},{4,28},{8,16},{12,20},{16,8},{20,12},{24,0},{28,4},{1,25},{... | collective-permute-start | bytes 811016 | tf_op jit(solution)/shard_map/ppermute | solution.py:19
  36.9 0.4 collective-permute-start.8
  37.3 1.6 %collective-permute-start.10 = (bf16[1056,256]{1,0:T(8,128)(2,1)S(1)}, bf16[1056,256]{1,0:T(8,128)(2,1)S(1)}, u32[]{:S(2)}, u32[]{:S(2)}) collective-permute-start(bf16[1056,256]{1,0:T(8,128)(2,1)S(1)} %constant_dynamic-update-slice_fusion.5), channel_id=1, source_target_pairs={{0,2},{1,3},{2,0},{3,1},{4,6},{5,7},{6,4},{7,5},{8,10},{9,11},{10,... | collective-permute-start | bytes 1622024 | tf_op jit(solution)/shard_map/ppermute | solution.py:19
  38.9 9.0 %collective-permute-done.6.refs_3_ = bf16[528,256]{1,0:T(8,128)(2,1)S(1)} collective-permute-done((bf16[528,256]{1,0:T(8,128)(2,1)S(1)}, bf16[528,256]{1,0:T(8,128)(2,1)S(1)}, u32[]{:S(2)}, u32[]{:S(2)}) %collective-permute-start.6) | collective-permute-done | bytes 270368 | tf_op jit(solution)/shard_map/ppermute | solution.py:19
  47.9 1.6 %collective-permute-start.9 = (bf16[1584,256]{1,0:T(8,128)(2,1)S(1)}, bf16[1584,256]{1,0:T(8,128)(2,1)S(1)}, u32[]{:S(2)}, u32[]{:S(2)}) collective-permute-start(bf16[1584,256]{1,0:T(8,128)(2,1)S(1)} %constant_dynamic-update-slice_fusion.2), channel_id=1, source_target_pairs={{0,2},{1,3},{2,0},{3,1},{4,6},{5,7},{6,4},{7,5},{8,10},{9,11},{10,... | collective-permute-start | bytes 2433032 | tf_op jit(solution)/shard_map/ppermute | solution.py:19
  49.6 0.6 collective-permute-start.15
  50.2 1.6 %collective-permute-start.14 = (bf16[528,256]{1,0:T(8,128)(2,1)S(1)}, bf16[528,256]{1,0:T(8,128)(2,1)S(1)}, u32[]{:S(2)}, u32[]{:S(2)}) collective-permute-start(bf16[528,256]{1,0:T(8,128)(2,1)S(1)} %collective-permute-done.1.refs_6_), channel_id=1, source_target_pairs={{0,2},{1,3},{2,0},{3,1},{4,6},{5,7},{6,4},{7,5},{8,10},{9,11},{10,... | collective-permute-start | bytes 811016 | tf_op jit(solution)/shard_map/ppermute | solution.py:19
  51.8 7.5 %pick.1 = bf16[4224,512]{1,0:T(8,128)(2,1)} custom-call(bf16[4096,512]{1,0:T(8,128)(2,1)S(1)} %copy-done, bf16[528,256]{1,0:T(8,128)(2,1)S(1)} %get-tuple-element.38.refs_0_, bf16[528,256]{1,0:T(8,128)(2,1)S(1)} %collective-permute-done.4.refs_1_, bf16[528,256]{1,0:T(8,128)(2,1)S(1)} %collective-permute-done.5.refs_2_, ...), custom_call_target="tpu_custom_call" | custom-call | tf_op jit(solution)/shard_map/pick/pallas_call | solution.py:153
  59.3 12.6 %collective-permute-done.15 = bf16[272,256]{1,0:T(8,128)(2,1)S(1)} collective-permute-done((bf16[272,256]{1,0:T(8,128)(2,1)S(1)}, bf16[272,256]{1,0:T(8,128)(2,1)S(1)}, u32[]{:S(2)}, u32[]{:S(2)}) %collective-permute-start.15) | collective-permute-done | bytes 139296 | tf_op jit(solution)/shard_map/ppermute | solution.py:19
  71.9 5.1 %collective-permute-start.2 = (bf16[256,256]{1,0:T(8,128)(2,1)S(1)}, bf16[256,256]{1,0:T(8,128)(2,1)S(1)}, u32[]{:S(2)}, u32[]{:S(2)}) collective-permute-start(bf16[256,256]{1,0:T(8,128)(2,1)S(1)} %get-tuple-element.37), channel_id=1, source_target_pairs={{0,28},{4,24},{8,20},{12,16},{16,12},{20,8},{24,4},{28,0},{1,29},{... | collective-permute-start | bytes 393224 | tf_op jit(solution)/shard_map/ppermute | solution.py:19
  77.2 0.6 collective-permute-start.13
  78.0 1.3 copy-done.5
  79.3 0.6 fusion.13
  79.9 0.9 fusion.9
  80.8 0.6 collective-permute-start.17
  81.4 0.5 fusion.17
  81.8 1.1 fusion.2
  83.0 0.6 fusion.5
  83.6 0.9 fusion.7
  84.5 1.2 fusion
  85.6 0.6 fusion.4
  86.2 1.6 %collective-permute-start.16 = (bf16[256,256]{1,0:T(8,128)(2,1)S(1)}, bf16[256,256]{1,0:T(8,128)(2,1)S(1)}, u32[]{:S(2)}, u32[]{:S(2)}) collective-permute-start(bf16[256,256]{1,0:T(8,128)(2,1)S(1)} %collective-permute-done.2), channel_id=1, source_target_pairs={{0,2},{1,3},{2,0},{3,1},{4,6},{5,7},{6,4},{7,5},{8,10},{9,11},{10,... | collective-permute-start | bytes 393224 | tf_op jit(solution)/shard_map/ppermute | solution.py:19
  87.8 0.6 fusion.11
  88.4 3.3 %collective-permute-done.16 = bf16[256,256]{1,0:T(8,128)(2,1)S(1)} collective-permute-done((bf16[256,256]{1,0:T(8,128)(2,1)S(1)}, bf16[256,256]{1,0:T(8,128)(2,1)S(1)}, u32[]{:S(2)}, u32[]{:S(2)}) %collective-permute-start.16) | collective-permute-done | bytes 131104 | tf_op jit(solution)/shard_map/ppermute | solution.py:19
  91.7 0.3 fusion.22
  92.2 0.5 fusion.6.near_ref
  92.7 1.0 collective-permute-done.19
  93.7 0.3 add_add_fusion.far_ref
  94.0 7.4 %solve.1 = (f32[4,128,256]{2,1,0:T(8,128)S(1)}, f32[4,128,256]{2,1,0:T(8,128)S(1)}, f32[4,128,256]{2,1,0:T(8,128)S(1)}, f32[4,128,256]{2,1,0:T(8,128)S(1)}) custom-call(f32[512,512]{1,0:T(8,128)S(1)} %fusion.6.near_ref, f32[512,512]{1,0:T(8,128)S(1)} %add_add_fusion.far_ref, bf16[128,512]{1,0:T(8,128)(2,1)S(1)} %copy-done.3, f32[512,512]{1,0:T(8,128)S(1)} %copy-done.2, ...), custom_call_target="tpu_custom_call" | custom-call | tf_op jit(solution)/shard_map/solve/pallas_call | solution.py:230
  101.6 14.1 %collective-permute-done.20 = f32[4,128,256]{2,1,0:T(8,128)S(1)} collective-permute-done((f32[4,128,256]{2,1,0:T(8,128)S(1)}, f32[4,128,256]{2,1,0:T(8,128)S(1)}, u32[]{:S(2)}, u32[]{:S(2)}) %collective-permute-start.20) | collective-permute-done | bytes 524320 | tf_op jit(solution)/shard_map/ppermute | solution.py:19
  115.9 0.4 collective-permute-start.22
  116.3 3.5 %collective-permute-start.23 = (f32[2,128,256]{2,1,0:T(8,128)S(1)}, f32[2,128,256]{2,1,0:T(8,128)S(1)}, u32[]{:S(2)}, u32[]{:S(2)}) collective-permute-start(f32[2,128,256]{2,1,0:T(8,128)S(1)} %get-tuple-element.62), channel_id=1, source_target_pairs={{0,16},{4,20},{8,24},{12,28},{16,0},{20,4},{24,8},{28,12},{1,17},{... | collective-permute-start | bytes 786440 | tf_op jit(solution)/shard_map/ppermute | solution.py:19
  119.8 9.5 %collective-permute-done.22 = f32[2,128,256]{2,1,0:T(8,128)S(1)} collective-permute-done((f32[2,128,256]{2,1,0:T(8,128)S(1)}, f32[2,128,256]{2,1,0:T(8,128)S(1)}, u32[]{:S(2)}, u32[]{:S(2)}) %collective-permute-start.22) | collective-permute-done | bytes 262176 | tf_op jit(solution)/shard_map/ppermute | solution.py:19
  129.3 1.6 %collective-permute-done.23 = f32[2,128,256]{2,1,0:T(8,128)S(1)} collective-permute-done((f32[2,128,256]{2,1,0:T(8,128)S(1)}, f32[2,128,256]{2,1,0:T(8,128)S(1)}, u32[]{:S(2)}, u32[]{:S(2)}) %collective-permute-start.23) | collective-permute-done | bytes 262176 | tf_op jit(solution)/shard_map/ppermute | solution.py:19
  131.0 1.4 %collective-permute-start.25 = (f32[1,128,256]{2,1,0:T(8,128)S(1)}, f32[1,128,256]{2,1,0:T(8,128)S(1)}, u32[]{:S(2)}, u32[]{:S(2)}) collective-permute-start(f32[1,128,256]{2,1,0:T(8,128)S(1)} %slice_add_fusion.5), channel_id=1, source_target_pairs={{0,4},{4,0},{8,12},{12,8},{16,20},{20,16},{24,28},{28,24},{1,5},{5... | collective-permute-start | bytes 393224 | tf_op jit(solution)/shard_map/ppermute | solution.py:19
  132.4 5.7 %collective-permute-done.24 = f32[1,128,256]{2,1,0:T(8,128)S(1)} collective-permute-done((f32[1,128,256]{2,1,0:T(8,128)S(1)}, f32[1,128,256]{2,1,0:T(8,128)S(1)}, u32[]{:S(2)}, u32[]{:S(2)}) %collective-permute-start.24) | collective-permute-done | bytes 131104 | tf_op jit(solution)/shard_map/ppermute | solution.py:19
  138.3 0.7 pad_maximum_fusion.2
  (52 shorter events, 1.3 us)
Async XLA Ops:
  0.7 1.6 %copy-start.1 = (bf16[4096,256]{1,0:T(8,128)(2,1)S(1)}, bf16[4096,256]{1,0:T(8,128)(2,1)}, u32[]{:S(2)}) copy-start(bf16[4096,256]{1,0:T(8,128)(2,1)} %panels_ref.1) | copy-start | bytes 6291460
  2.2 0.7 copy-start.4
  3.0 48.8 %copy-start = (bf16[4096,512]{1,0:T(8,128)(2,1)S(1)}, bf16[4096,512]{1,0:T(8,128)(2,1)}, u32[]{:S(2)}) copy-start(bf16[4096,512]{1,0:T(8,128)(2,1)} %parent_ref.1) | copy-start | bytes 12582916
  4.3 23.0 %collective-permute-start = (bf16[528,256]{1,0:T(8,128)(2,1)S(1)}, bf16[528,256]{1,0:T(8,128)(2,1)S(1)}, u32[]{:S(2)}, u32[]{:S(2)}) collective-permute-start(bf16[528,256]{1,0:T(8,128)(2,1)S(1)} %get-tuple-element.35), channel_id=1, source_target_pairs={{0,16},{4,20},{8,24},{12,28},{16,0},{20,4},{24,8},{28,12},{1,17},{... | collective-permute-start | bytes 811016 | tf_op jit(solution)/shard_map/ppermute | solution.py:19
  8.5 25.0 %collective-permute-start.7 = (bf16[528,256]{1,0:T(8,128)(2,1)S(1)}, bf16[528,256]{1,0:T(8,128)(2,1)S(1)}, u32[]{:S(2)}, u32[]{:S(2)}) collective-permute-start(bf16[528,256]{1,0:T(8,128)(2,1)S(1)} %get-tuple-element.44), channel_id=1, source_target_pairs={{0,20},{4,16},{8,28},{12,24},{16,4},{20,0},{24,12},{28,8},{1,21},{... | collective-permute-start | bytes 811016 | tf_op jit(solution)/shard_map/ppermute | solution.py:19
  9.8 27.1 %collective-permute-start.4 = (bf16[528,256]{1,0:T(8,128)(2,1)S(1)}, bf16[528,256]{1,0:T(8,128)(2,1)S(1)}, u32[]{:S(2)}, u32[]{:S(2)}) collective-permute-start(bf16[528,256]{1,0:T(8,128)(2,1)S(1)} %get-tuple-element.39), channel_id=1, source_target_pairs={{0,4},{4,0},{8,12},{12,8},{16,20},{20,16},{24,28},{28,24},{1,5},{5... | collective-permute-start | bytes 811016 | tf_op jit(solution)/shard_map/ppermute | solution.py:19
  10.0 27.3 %collective-permute-start.5 = (bf16[528,256]{1,0:T(8,128)(2,1)S(1)}, bf16[528,256]{1,0:T(8,128)(2,1)S(1)}, u32[]{:S(2)}, u32[]{:S(2)}) collective-permute-start(bf16[528,256]{1,0:T(8,128)(2,1)S(1)} %get-tuple-element.40), channel_id=1, source_target_pairs={{0,8},{4,12},{8,0},{12,4},{16,24},{20,28},{24,16},{28,20},{1,9},{5... | collective-permute-start | bytes 811016 | tf_op jit(solution)/shard_map/ppermute | solution.py:19
  11.8 37.6 %collective-permute-start.3 = (bf16[528,256]{1,0:T(8,128)(2,1)S(1)}, bf16[528,256]{1,0:T(8,128)(2,1)S(1)}, u32[]{:S(2)}, u32[]{:S(2)}) collective-permute-start(bf16[528,256]{1,0:T(8,128)(2,1)S(1)} %get-tuple-element.38.refs_0_), channel_id=1, source_target_pairs={{0,2},{1,3},{2,0},{3,1},{4,6},{5,7},{6,4},{7,5},{8,10},{9,11},{10,... | collective-permute-start | bytes 811016 | tf_op jit(solution)/shard_map/ppermute | solution.py:19
  27.4 20.5 %collective-permute-start.6 = (bf16[528,256]{1,0:T(8,128)(2,1)S(1)}, bf16[528,256]{1,0:T(8,128)(2,1)S(1)}, u32[]{:S(2)}, u32[]{:S(2)}) collective-permute-start(bf16[528,256]{1,0:T(8,128)(2,1)S(1)} %get-tuple-element.41), channel_id=1, source_target_pairs={{0,12},{4,8},{8,4},{12,0},{16,28},{20,24},{24,20},{28,16},{1,13},{... | collective-permute-start | bytes 811016 | tf_op jit(solution)/shard_map/ppermute | solution.py:19
  33.4 16.8 %collective-permute-start.1 = (bf16[528,256]{1,0:T(8,128)(2,1)S(1)}, bf16[528,256]{1,0:T(8,128)(2,1)S(1)}, u32[]{:S(2)}, u32[]{:S(2)}) collective-permute-start(bf16[528,256]{1,0:T(8,128)(2,1)S(1)} %get-tuple-element.36), channel_id=1, source_target_pairs={{0,24},{4,28},{8,16},{12,20},{16,8},{20,12},{24,0},{28,4},{1,25},{... | collective-permute-start | bytes 811016 | tf_op jit(solution)/shard_map/ppermute | solution.py:19
  36.9 12.7 %collective-permute-start.8 = (bf16[272,256]{1,0:T(8,128)(2,1)S(1)}, bf16[272,256]{1,0:T(8,128)(2,1)S(1)}, u32[]{:S(2)}, u32[]{:S(2)}) collective-permute-start(bf16[272,256]{1,0:T(8,128)(2,1)S(1)} %get-tuple-element.47), channel_id=1, source_target_pairs={{0,28},{4,24},{8,20},{12,16},{16,12},{20,8},{24,4},{28,0},{1,29},{... | collective-permute-start | bytes 417800 | tf_op jit(solution)/shard_map/ppermute | solution.py:19
  37.3 39.7 %collective-permute-start.10 = (bf16[1056,256]{1,0:T(8,128)(2,1)S(1)}, bf16[1056,256]{1,0:T(8,128)(2,1)S(1)}, u32[]{:S(2)}, u32[]{:S(2)}) collective-permute-start(bf16[1056,256]{1,0:T(8,128)(2,1)S(1)} %constant_dynamic-update-slice_fusion.5), channel_id=1, source_target_pairs={{0,2},{1,3},{2,0},{3,1},{4,6},{5,7},{6,4},{7,5},{8,10},{9,11},{10,... | collective-permute-start | bytes 1622024 | tf_op jit(solution)/shard_map/ppermute | solution.py:19
  47.9 29.8 %collective-permute-start.9 = (bf16[1584,256]{1,0:T(8,128)(2,1)S(1)}, bf16[1584,256]{1,0:T(8,128)(2,1)S(1)}, u32[]{:S(2)}, u32[]{:S(2)}) collective-permute-start(bf16[1584,256]{1,0:T(8,128)(2,1)S(1)} %constant_dynamic-update-slice_fusion.2), channel_id=1, source_target_pairs={{0,2},{1,3},{2,0},{3,1},{4,6},{5,7},{6,4},{7,5},{8,10},{9,11},{10,... | collective-permute-start | bytes 2433032 | tf_op jit(solution)/shard_map/ppermute | solution.py:19
  49.5 36.1 %collective-permute-start.11 = (bf16[528,512]{1,0:T(8,128)(2,1)S(1)}, bf16[528,512]{1,0:T(8,128)(2,1)S(1)}, u32[]{:S(2)}, u32[]{:S(2)}) collective-permute-start(bf16[528,512]{1,0:T(8,128)(2,1)S(1)} %constant_dynamic-update-slice_fusion), channel_id=1, source_target_pairs={{0,1},{1,0},{2,3},{3,2},{4,5},{5,4},{6,7},{7,6},{8,9},{9,8},{10,11... | collective-permute-start | bytes 1622024 | tf_op jit(solution)/shard_map/ppermute | solution.py:19
  49.6 22.3 %collective-permute-start.15 = (bf16[272,256]{1,0:T(8,128)(2,1)S(1)}, bf16[272,256]{1,0:T(8,128)(2,1)S(1)}, u32[]{:S(2)}, u32[]{:S(2)}) collective-permute-start(bf16[272,256]{1,0:T(8,128)(2,1)S(1)} %collective-permute-done.8.refs_7_), channel_id=1, source_target_pairs={{0,2},{1,3},{2,0},{3,1},{4,6},{5,7},{6,4},{7,5},{8,10},{9,11},{10,... | collective-permute-start | bytes 417800 | tf_op jit(solution)/shard_map/ppermute | solution.py:19
  50.2 27.0 %collective-permute-start.14 = (bf16[528,256]{1,0:T(8,128)(2,1)S(1)}, bf16[528,256]{1,0:T(8,128)(2,1)S(1)}, u32[]{:S(2)}, u32[]{:S(2)}) collective-permute-start(bf16[528,256]{1,0:T(8,128)(2,1)S(1)} %collective-permute-done.1.refs_6_), channel_id=1, source_target_pairs={{0,2},{1,3},{2,0},{3,1},{4,6},{5,7},{6,4},{7,5},{8,10},{9,11},{10,... | collective-permute-start | bytes 811016 | tf_op jit(solution)/shard_map/ppermute | solution.py:19
  71.9 14.3 %collective-permute-start.2 = (bf16[256,256]{1,0:T(8,128)(2,1)S(1)}, bf16[256,256]{1,0:T(8,128)(2,1)S(1)}, u32[]{:S(2)}, u32[]{:S(2)}) collective-permute-start(bf16[256,256]{1,0:T(8,128)(2,1)S(1)} %get-tuple-element.37), channel_id=1, source_target_pairs={{0,28},{4,24},{8,20},{12,16},{16,12},{20,8},{24,4},{28,0},{1,29},{... | collective-permute-start | bytes 393224 | tf_op jit(solution)/shard_map/ppermute | solution.py:19
  77.0 3.8 %collective-permute-start.18 = (bf16[272,512]{1,0:T(8,128)(2,1)S(1)}, bf16[272,512]{1,0:T(8,128)(2,1)S(1)}, u32[]{:S(2)}, u32[]{:S(2)}) collective-permute-start(bf16[272,512]{1,0:T(8,128)(2,1)S(1)} %constant_dynamic-update-slice_fusion.9), channel_id=1, source_target_pairs={{0,1},{1,0},{2,3},{3,2},{4,5},{5,4},{6,7},{7,6},{8,9},{9,8},{10,11... | collective-permute-start | bytes 835592 | tf_op jit(solution)/shard_map/ppermute | solution.py:19
  77.1 2.2 %copy-start.5 = (bf16[4224,512]{1,0:T(8,128)(2,1)S(1)}, bf16[4224,512]{1,0:T(8,128)(2,1)}, u32[]{:S(2)}) copy-start(bf16[4224,512]{1,0:T(8,128)(2,1)} %pick.1) | copy-start | bytes 12976132
  77.2 6.4 %collective-permute-start.13 = (bf16[1056,512]{1,0:T(8,128)(2,1)S(1)}, bf16[1056,512]{1,0:T(8,128)(2,1)S(1)}, u32[]{:S(2)}, u32[]{:S(2)}) collective-permute-start(bf16[1056,512]{1,0:T(8,128)(2,1)S(1)} %pad_maximum_fusion.1), channel_id=1, source_target_pairs={{0,1},{1,0},{2,3},{3,2},{4,5},{5,4},{6,7},{7,6},{8,9},{9,8},{10,11... | collective-permute-start | bytes 3244040 | tf_op jit(solution)/shard_map/ppermute | solution.py:19
  77.9 6.5 %collective-permute-start.12 = (bf16[1584,512]{1,0:T(8,128)(2,1)S(1)}, bf16[1584,512]{1,0:T(8,128)(2,1)S(1)}, u32[]{:S(2)}, u32[]{:S(2)}) collective-permute-start(bf16[1584,512]{1,0:T(8,128)(2,1)S(1)} %pad_maximum_fusion), channel_id=1, source_target_pairs={{0,1},{1,0},{2,3},{3,2},{4,5},{5,4},{6,7},{7,6},{8,9},{9,8},{10,11... | collective-permute-start | bytes 4866056 | tf_op jit(solution)/shard_map/ppermute | solution.py:19
  80.8 7.0 %collective-permute-start.17 = (bf16[528,512]{1,0:T(8,128)(2,1)S(1)}, bf16[528,512]{1,0:T(8,128)(2,1)S(1)}, u32[]{:S(2)}, u32[]{:S(2)}) collective-permute-start(bf16[528,512]{1,0:T(8,128)(2,1)S(1)} %constant_dynamic-update-slice_fusion.7), channel_id=1, source_target_pairs={{0,1},{1,0},{2,3},{3,2},{4,5},{5,4},{6,7},{7,6},{8,9},{9,8},{10,11... | collective-permute-start | bytes 1622024 | tf_op jit(solution)/shard_map/ppermute | solution.py:19
  86.2 5.5 %collective-permute-start.16 = (bf16[256,256]{1,0:T(8,128)(2,1)S(1)}, bf16[256,256]{1,0:T(8,128)(2,1)S(1)}, u32[]{:S(2)}, u32[]{:S(2)}) collective-permute-start(bf16[256,256]{1,0:T(8,128)(2,1)S(1)} %collective-permute-done.2), channel_id=1, source_target_pairs={{0,2},{1,3},{2,0},{3,1},{4,6},{5,7},{6,4},{7,5},{8,10},{9,11},{10,... | collective-permute-start | bytes 393224 | tf_op jit(solution)/shard_map/ppermute | solution.py:19
  92.1 1.6 %collective-permute-start.19 = (bf16[256,512]{1,0:T(8,128)(2,1)S(1)}, bf16[256,512]{1,0:T(8,128)(2,1)S(1)}, u32[]{:S(2)}, u32[]{:S(2)}) collective-permute-start(bf16[256,512]{1,0:T(8,128)(2,1)S(1)} %constant_dynamic-update-slice_fusion.11), channel_id=1, source_target_pairs={{0,1},{1,0},{2,3},{3,2},{4,5},{5,4},{6,7},{7,6},{8,9},{9,8},{10,11... | collective-permute-start | bytes 786440 | tf_op jit(solution)/shard_map/ppermute | solution.py:19
  92.7 1.3 copy-start.2
  92.7 1.3 copy-start.3
  101.4 14.3 %collective-permute-start.20 = (f32[4,128,256]{2,1,0:T(8,128)S(1)}, f32[4,128,256]{2,1,0:T(8,128)S(1)}, u32[]{:S(2)}, u32[]{:S(2)}) collective-permute-start(f32[4,128,256]{2,1,0:T(8,128)S(1)} %get-tuple-element.52), channel_id=1, source_target_pairs={{0,4},{4,0},{8,12},{12,8},{16,20},{20,16},{24,28},{28,24},{1,5},{5... | collective-permute-start | bytes 1572872 | tf_op jit(solution)/shard_map/ppermute | solution.py:19
  101.5 14.3 %collective-permute-start.21 = (f32[4,128,256]{2,1,0:T(8,128)S(1)}, f32[4,128,256]{2,1,0:T(8,128)S(1)}, u32[]{:S(2)}, u32[]{:S(2)}) collective-permute-start(f32[4,128,256]{2,1,0:T(8,128)S(1)} %get-tuple-element.53), channel_id=1, source_target_pairs={{0,8},{4,12},{8,0},{12,4},{16,24},{20,28},{24,16},{28,20},{1,9},{5... | collective-permute-start | bytes 1572872 | tf_op jit(solution)/shard_map/ppermute | solution.py:19
  115.9 13.4 %collective-permute-start.22 = (f32[2,128,256]{2,1,0:T(8,128)S(1)}, f32[2,128,256]{2,1,0:T(8,128)S(1)}, u32[]{:S(2)}, u32[]{:S(2)}) collective-permute-start(f32[2,128,256]{2,1,0:T(8,128)S(1)} %get-tuple-element.63), channel_id=1, source_target_pairs={{0,8},{4,12},{8,0},{12,4},{16,24},{20,28},{24,16},{28,20},{1,9},{5... | collective-permute-start | bytes 786440 | tf_op jit(solution)/shard_map/ppermute | solution.py:19
  116.3 14.6 %collective-permute-start.23 = (f32[2,128,256]{2,1,0:T(8,128)S(1)}, f32[2,128,256]{2,1,0:T(8,128)S(1)}, u32[]{:S(2)}, u32[]{:S(2)}) collective-permute-start(f32[2,128,256]{2,1,0:T(8,128)S(1)} %get-tuple-element.62), channel_id=1, source_target_pairs={{0,16},{4,20},{8,24},{12,28},{16,0},{20,4},{24,8},{28,12},{1,17},{... | collective-permute-start | bytes 786440 | tf_op jit(solution)/shard_map/ppermute | solution.py:19
  130.9 7.3 %collective-permute-start.24 = (f32[1,128,256]{2,1,0:T(8,128)S(1)}, f32[1,128,256]{2,1,0:T(8,128)S(1)}, u32[]{:S(2)}, u32[]{:S(2)}) collective-permute-start(f32[1,128,256]{2,1,0:T(8,128)S(1)} %slice_add_fusion.6), channel_id=1, source_target_pairs={{0,16},{4,20},{8,24},{12,28},{16,0},{20,4},{24,8},{28,12},{1,17},{... | collective-permute-start | bytes 393224 | tf_op jit(solution)/shard_map/ppermute | solution.py:19
  131.0 7.2 %collective-permute-start.25 = (f32[1,128,256]{2,1,0:T(8,128)S(1)}, f32[1,128,256]{2,1,0:T(8,128)S(1)}, u32[]{:S(2)}, u32[]{:S(2)}) collective-permute-start(f32[1,128,256]{2,1,0:T(8,128)S(1)} %slice_add_fusion.5), channel_id=1, source_target_pairs={{0,4},{4,0},{8,12},{12,8},{16,20},{20,16},{24,28},{28,24},{1,5},{5... | collective-permute-start | bytes 393224 | tf_op jit(solution)/shard_map/ppermute | solution.py:19

commit v3 on v2

--- a/solution.py
+++ b/solution.py
@@ -9,6 +9,7 @@
 
 BLK = 128
 LANES = 128
+CODE_BITS = 14.96
 ANY = pl.BlockSpec(memory_space=pl.ANY)
 VMEM = pl.BlockSpec(memory_space=pltpu.VMEM)
 SMEM = pl.BlockSpec(memory_space=pltpu.SMEM)
@@ -179,8 +180,48 @@
     return dot(lh, rh) + (dot(lh, rl) + dot(ll, rh))
 
 
-def solve_kernel(orders, near_ref, far_ref, front_ref, coup_ref, one_ref, two_ref, *refs):
-    outs, resid = refs[:4], refs[4]
+def encode(value):
+    value = value * 0.25
+    most = jnp.maximum(jnp.max(jnp.abs(value), axis=0, keepdims=True), 1e-30)
+    exponent = jnp.floor(8.0 * jnp.log2(most)) + 1.0
+    codes = jnp.round(value * jnp.exp2(CODE_BITS - 0.125 * exponent))
+    return codes.astype(jnp.int32).astype(jnp.int16), exponent
+
+
+def decode(codes, exponent):
+    scale = jnp.exp2(0.125 * exponent - CODE_BITS)
+    return codes.astype(jnp.int32).astype(jnp.float32) * scale * 4.0
+
+
+def scale_rows(blocks):
+    return -(-blocks // 16) * 16
+
+
+def write_message(message_ref, scales_ref, blocks):
+    count, rows, _ = blocks.shape
+    scales_ref[...] = jnp.zeros_like(scales_ref)
+    for i in range(count):
+        codes, exponent = encode(blocks[i])
+        message_ref[pl.ds(i * rows, rows), :] = codes
+        scales_ref[pl.ds(i, 1), :] = exponent
+    message_ref[pl.ds(count * rows, scales_ref.shape[0]), :] = (
+        scales_ref[...].astype(jnp.int32).astype(jnp.int16)
+    )
+
+
+def read_message(message_ref, rows, wanted):
+    count = message_ref.shape[0] // rows
+    tail = message_ref[pl.ds(count * rows, message_ref.shape[0] - count * rows), :]
+    exponents = tail.astype(jnp.int32).astype(jnp.float32)
+    return [decode(message_ref[pl.ds(i * rows, rows), :], exponents[i : i + 1]) for i in wanted]
+
+
+def message_shape(blocks, rows, columns):
+    return jax.ShapeDtypeStruct((blocks * rows + scale_rows(blocks), columns), jnp.int16)
+
+
+def solve_kernel(side, order, near_ref, far_ref, front_ref, coup_ref, one_ref, two_ref, *refs):
+    keep_ref, message_ref, resid, send_ref, scales_ref = refs
     me = lax.axis_index("rows")
     share = lax.axis_index("rhs")
     pivot_share = front_ref.shape[0]
@@ -188,54 +229,99 @@
     panel = pivots // 2
     half_shares = lax.axis_size("rhs") // 2
     width = near_ref.shape[0] // half_shares
+    groups = pivots // pivot_share
+    cols = pl.ds(side * columns, columns)
     for odd, part_ref in ((0, near_ref), (1, far_ref)):
         for i in range(half_shares):
             at = pl.multiple_of((share ^ (2 * i + odd)) * width, width)
-            resid[pl.ds(at, width), :] = -part_ref[pl.ds(i * width, width), :]
+            resid[pl.ds(at, width), :] = -part_ref[pl.ds(i * width, width), cols]
     mine = pl.ds(pl.multiple_of(me * pivot_share, pivot_share), pivot_share)
-    resid[mine, :] += front_ref[...].astype(jnp.float32)
-    two, one, coup = split(two_ref[...]), split(one_ref[...]), split(coup_ref[...])
-    middle = columns // 2
-    groups = pivots // pivot_share
-    for side in range(2):
-        cols = pl.ds(side * middle, middle)
-        second = dot3(two, split(resid[pl.ds(panel, panel), cols]))
-        reduced = resid[pl.ds(0, panel), cols] - dot3(coup, split(second))
-        first = dot3(one, split(reduced))
-        keep_ref, send_ref = outs[2 * side : 2 * side + 2]
-        order = orders[side]
-        for block in range(groups):
-            source = first if block < groups // 2 else second
-            at = (block % (groups // 2)) * pivot_share
-            value = source[at : at + pivot_share, :]
-            rel = block ^ me
-            place = sum(
-                ((rel >> bit) & 1) << (len(order) - 1 - i) for i, bit in enumerate(order) if i
-            )
-            sent = (rel >> order[0]) & 1
-
-            @pl.when(sent == 0)
-            def _():
-                keep_ref[place] = value
-
-            @pl.when(sent == 1)
-            def _():
-                send_ref[place] = value
-
-
-def solve(orders, near, far, front_rhs, coupling, one, two, groups):
+    resid[mine, :] += front_ref[:, cols].astype(jnp.float32)
+    second = dot3(split(two_ref[...]), split(resid[pl.ds(panel, panel), :]))
+    reduced = resid[pl.ds(0, panel), :] - dot3(split(coup_ref[...]), split(second))
+    first = dot3(split(one_ref[...]), split(reduced))
+    for block in range(groups):
+        source = first if block < groups // 2 else second
+        at = (block % (groups // 2)) * pivot_share
+        value = source[at : at + pivot_share, :]
+        rel = block ^ me
+        place = sum(
+            ((rel >> bit) & 1) << (len(order) - 1 - i) for i, bit in enumerate(order) if i
+        )
+        sent = (rel >> order[0]) & 1
+
+        @pl.when(sent == 0)
+        def _():
+            keep_ref[place] = value
+
+        @pl.when(sent == 1)
+        def _():
+            send_ref[place] = value
+
+    write_message(message_ref, scales_ref, send_ref)
+
+
+def solve(side, order, near, far, front_rhs, coupling, one, two, groups):
     pivot_share, columns = front_rhs.shape
-    pivots = groups * pivot_share
-    out = jax.ShapeDtypeStruct((groups // 2, pivot_share, columns // 2), jnp.float32)
+    pivots, columns, half = groups * pivot_share, columns // 2, groups // 2
+    blocks = jax.ShapeDtypeStruct((half, pivot_share, columns), jnp.float32)
     return pl.pallas_call(
-        functools.partial(solve_kernel, orders),
-        out_shape=[out] * 4,
+        functools.partial(solve_kernel, side, order),
+        out_shape=[blocks, message_shape(half, pivot_share, columns)],
         in_specs=[VMEM] * 6,
-        out_specs=[VMEM] * 4,
-        scratch_shapes=[pltpu.VMEM((pivots, columns), jnp.float32)],
+        out_specs=[VMEM] * 2,
+        scratch_shapes=[
+            pltpu.VMEM((pivots, columns), jnp.float32),
+            pltpu.VMEM(blocks.shape, jnp.float32),
+            pltpu.VMEM((scale_rows(half), columns), jnp.float32),
+        ],
         compiler_params=pltpu.CompilerParams(vmem_limit_bytes=48 * 2**20),
         name="solve",
     )(near, far, front_rhs, coupling, one, two)
+
+
+def fold_kernel(kept_ref, came_ref, keep_ref, message_ref, send_ref, scales_ref):
+    half, rows, _ = keep_ref.shape
+    for i, value in enumerate(read_message(came_ref, rows, range(half, 2 * half))):
+        send_ref[i] = kept_ref[half + i] + value
+    write_message(message_ref, scales_ref, send_ref)
+    for i, value in enumerate(read_message(came_ref, rows, range(half))):
+        keep_ref[i] = kept_ref[i] + value
+
+
+def fold(kept, came):
+    count, rows, columns = kept.shape
+    half = count // 2
+    blocks = jax.ShapeDtypeStruct((half, rows, columns), jnp.float32)
+    return pl.pallas_call(
+        fold_kernel,
+        out_shape=[blocks, message_shape(half, rows, columns)],
+        in_specs=[VMEM] * 2,
+        out_specs=[VMEM] * 2,
+        scratch_shapes=[
+            pltpu.VMEM(blocks.shape, jnp.float32),
+            pltpu.VMEM((scale_rows(half), columns), jnp.float32),
+        ],
+        compiler_params=pltpu.CompilerParams(vmem_limit_bytes=24 * 2**20),
+        name="fold",
+    )(kept, came)
+
+
+def last_kernel(kept_a, came_a, kept_b, came_b, out_ref):
+    rows, columns = kept_a.shape[1:]
+    for side, (kept, came) in enumerate(((kept_a, came_a), (kept_b, came_b))):
+        out_ref[:, pl.ds(side * columns, columns)] = kept[0] + read_message(came, rows, [0])[0]
+
+
+def last(kept_a, came_a, kept_b, came_b):
+    _, rows, columns = kept_a.shape
+    return pl.pallas_call(
+        last_kernel,
+        out_shape=jax.ShapeDtypeStruct((rows, 2 * columns), jnp.float32),
+        in_specs=[VMEM] * 4,
+        out_specs=VMEM,
+        name="last",
+    )(kept_a, came_a, kept_b, came_b)
 
 
 def panel_dot(panel, rows):
@@ -313,19 +399,26 @@
         near_total, far_total = add(done)
         done += 1
 
-    orders = (bits, bits[1:] + bits[:1])
-    keep_a, send_a, keep_b, send_b = solve(
-        orders, near_total, far_total, front_rhs, coupling, inverse_one, inverse_two, groups
-    )
+    orders = (bits[1:] + bits[:1], bits)
+    kept, sent = [None, None], [None, None]
+    for side in range(2):
+        kept[side], sent[side] = solve(
+            side,
+            orders[side],
+            near_total,
+            far_total,
+            front_rhs,
+            coupling,
+            inverse_one,
+            inverse_two,
+            groups,
+        )
     for step in range(len(bits)):
-        came_a = swap(send_a, "rows", 1 << orders[0][step])
-        came_b = swap(send_b, "rows", 1 << orders[1][step])
-        came_a, came_b = lax.optimization_barrier((came_a, came_b))
-        middle = keep_a.shape[0] // 2
-        send_a, send_b = keep_a[middle:] + came_a[middle:], keep_b[middle:] + came_b[middle:]
-        if middle:
-            keep_a, keep_b = keep_a[:middle] + came_a[:middle], keep_b[:middle] + came_b[:middle]
-    return jnp.concatenate([send_a[0], send_b[0]], axis=1)
+        came = [swap(sent[side], "rows", 1 << orders[side][step]) for side in range(2)]
+        if step < len(bits) - 1:
+            for side in range(2):
+                kept[side], sent[side] = fold(kept[side], came[side])
+    return last(kept[0], came[0], kept[1], came[1])
 
 
 def solution(mesh):

time: 139 us -> 126 us (0.906)
  waiting for transfers between devices: 76.1 us -> 64.6 us
  starting transfers between devices: 32.5 us -> 30 us
  local copies, waits for them, and re-layouts: 3.84 us -> 5.64 us
    ppermute x26, waiting for transfers between devices: 76.1 us -> 64.6 us  [swap(): return lax.ppermute(array, axis, [(i, i ^ mask) for i in range(size)])]
    ppermute x26, starting transfers between devices: 32.5 us -> 30 us  [swap(): return lax.ppermute(array, axis, [(i, i ^ mask) for i in range(size)])]
    unnamed x19 -> x31, local copies, waits for them, and re-layouts: 3.75 us -> 5.55 us
    pallas_call x1 -> x7, Pallas kernels: 7.4 us -> 7.57 us  [the longest x2 5.29 us: solve(): pl.pallas_call(functools.partial(solve_kernel, side, order), out_shape=[b...]
  transfers between devices with their start and end apart: 26 -> 26, of which waited for: 11 -> 12; matrix products, arithmetic and copies ran while one was open for 6% -> 6% of each run, Pallas kernels for 5% -> 8%
where the time goes in v3:
time: 126 us
  waiting for transfers between devices  64.6 us (51%)
  starting transfers between devices  30 us (24%)
  Pallas kernels  16.5 us (13%)
  matrix products  8.08 us (6%)
  local copies, waits for them, and re-layouts  5.64 us (4%)
    ppermute x26, waiting for transfers between devices, swap(): return lax.ppermute(array, axis, [(i, i ^ mask) for i in range(size)])  64.6 us
    ppermute x26, starting transfers between devices, swap(): return lax.ppermute(array, axis, [(i, i ^ mask) for i in range(size)])  30 us
    dot_general x12, matrix products, panel_dot(): lax.dot_general(panel, rows, (((0,), (0,)), ((), ())), preferred_element_...  8.08 us
    pallas_call x1, Pallas kernels, pick(): pl.pallas_call(functools.partial(pick_kernel, groups, slots), out_shape=j...  7.51 us
    unnamed x31, local copies, waits for them, and re-layouts  5.55 us
    pallas_call x2, Pallas kernels, solve(): pl.pallas_call(functools.partial(solve_kernel, side, order), out_shape=[b...  5.29 us
  transfers between devices with their start and end apart: 26, of which 12 were waited for; matrix products, arithmetic and copies ran while one was open for 6% of the time, Pallas kernels for 8%

profile of v3, /device:TPU:0, one launch (start us, length us, event | category | flops | bytes accessed | tf_op | source)
XLA Modules:
  0.0 126.1 jit_solution(17717556156860920810)
XLA Ops:
  0.7 1.6 %copy-done.4 = bf16[4096,256]{1,0:T(8,128)(2,1)S(1)} copy-done((bf16[4096,256]{1,0:T(8,128)(2,1)S(1)}, bf16[4096,256]{1,0:T(8,128)(2,1)}, u32[]{:S(2)}) %copy-start.4) | copy-done | bytes 2097176
  2.2 0.7 copy-done.8
  3.0 1.4 %pack.1 = (bf16[528,256]{1,0:T(8,128)(2,1)S(1)}, bf16[528,256]{1,0:T(8,128)(2,1)S(1)}, bf16[528,256]{1,0:T(8,128)(2,1)S(1)}, bf16[528,256]{1,0:T(8,128)(2,1)S(1)...) custom-call(s32[4096]{0:T(1024)S(1)} %copy-done.8, ...), custom_call_target="tpu_custom_call" | custom-call | tf_op jit(solution)/shard_map/pack/pallas_call | solution.py:70
  4.4 4.0 %collective-permute-start = (bf16[528,256]{1,0:T(8,128)(2,1)S(1)}, bf16[528,256]{1,0:T(8,128)(2,1)S(1)}, u32[]{:S(2)}, u32[]{:S(2)}) collective-permute-start(bf16[528,256]{1,0:T(8,128)(2,1)S(1)} %get-tuple-element.37), channel_id=1, source_target_pairs={{0,16},{4,20},{8,24},{12,28},{16,0},{20,4},{24,8},{28,12},{1,17},{... | collective-permute-start | bytes 811016 | tf_op jit(solution)/shard_map/ppermute | solution.py:20
  8.4 1.3 %collective-permute-start.7 = (bf16[528,256]{1,0:T(8,128)(2,1)S(1)}, bf16[528,256]{1,0:T(8,128)(2,1)S(1)}, u32[]{:S(2)}, u32[]{:S(2)}) collective-permute-start(bf16[528,256]{1,0:T(8,128)(2,1)S(1)} %get-tuple-element.46), channel_id=1, source_target_pairs={{0,20},{4,16},{8,28},{12,24},{16,4},{20,0},{24,12},{28,8},{1,21},{... | collective-permute-start | bytes 811016 | tf_op jit(solution)/shard_map/ppermute | solution.py:20
  10.0 1.9 %collective-permute-start.5 = (bf16[528,256]{1,0:T(8,128)(2,1)S(1)}, bf16[528,256]{1,0:T(8,128)(2,1)S(1)}, u32[]{:S(2)}, u32[]{:S(2)}) collective-permute-start(bf16[528,256]{1,0:T(8,128)(2,1)S(1)} %get-tuple-element.42), channel_id=1, source_target_pairs={{0,8},{4,12},{8,0},{12,4},{16,24},{20,28},{24,16},{28,20},{1,9},{5... | collective-permute-start | bytes 811016 | tf_op jit(solution)/shard_map/ppermute | solution.py:20
  11.8 1.5 %collective-permute-start.3 = (bf16[528,256]{1,0:T(8,128)(2,1)S(1)}, bf16[528,256]{1,0:T(8,128)(2,1)S(1)}, u32[]{:S(2)}, u32[]{:S(2)}) collective-permute-start(bf16[528,256]{1,0:T(8,128)(2,1)S(1)} %get-tuple-element.40.refs_0_), channel_id=1, source_target_pairs={{0,2},{1,3},{2,0},{3,1},{4,6},{5,7},{6,4},{7,5},{8,10},{9,11},{10,... | collective-permute-start | bytes 811016 | tf_op jit(solution)/shard_map/ppermute | solution.py:20
  13.4 13.9 %collective-permute-done.refs_4_ = bf16[528,256]{1,0:T(8,128)(2,1)S(1)} collective-permute-done((bf16[528,256]{1,0:T(8,128)(2,1)S(1)}, bf16[528,256]{1,0:T(8,128)(2,1)S(1)}, u32[]{:S(2)}, u32[]{:S(2)}) %collective-permute-start) | collective-permute-done | bytes 270368 | tf_op jit(solution)/shard_map/ppermute | solution.py:20
  27.3 0.9 collective-permute-start.6
  28.3 5.2 %collective-permute-done.7.refs_5_ = bf16[528,256]{1,0:T(8,128)(2,1)S(1)} collective-permute-done((bf16[528,256]{1,0:T(8,128)(2,1)S(1)}, bf16[528,256]{1,0:T(8,128)(2,1)S(1)}, u32[]{:S(2)}, u32[]{:S(2)}) %collective-permute-start.7) | collective-permute-done | bytes 270368 | tf_op jit(solution)/shard_map/ppermute | solution.py:20
  33.4 3.4 %collective-permute-start.1 = (bf16[528,256]{1,0:T(8,128)(2,1)S(1)}, bf16[528,256]{1,0:T(8,128)(2,1)S(1)}, u32[]{:S(2)}, u32[]{:S(2)}) collective-permute-start(bf16[528,256]{1,0:T(8,128)(2,1)S(1)} %get-tuple-element.38), channel_id=1, source_target_pairs={{0,24},{4,28},{8,16},{12,20},{16,8},{20,12},{24,0},{28,4},{1,25},{... | collective-permute-start | bytes 811016 | tf_op jit(solution)/shard_map/ppermute | solution.py:20
  37.2 1.7 %collective-permute-start.10 = (bf16[1056,256]{1,0:T(8,128)(2,1)S(1)}, bf16[1056,256]{1,0:T(8,128)(2,1)S(1)}, u32[]{:S(2)}, u32[]{:S(2)}) collective-permute-start(bf16[1056,256]{1,0:T(8,128)(2,1)S(1)} %constant_dynamic-update-slice_fusion.5), channel_id=1, source_target_pairs={{0,2},{1,3},{2,0},{3,1},{4,6},{5,7},{6,4},{7,5},{8,10},{9,11},{10,... | collective-permute-start | bytes 1622024 | tf_op jit(solution)/shard_map/ppermute | solution.py:20
  38.9 9.0 %collective-permute-done.6.refs_3_ = bf16[528,256]{1,0:T(8,128)(2,1)S(1)} collective-permute-done((bf16[528,256]{1,0:T(8,128)(2,1)S(1)}, bf16[528,256]{1,0:T(8,128)(2,1)S(1)}, u32[]{:S(2)}, u32[]{:S(2)}) %collective-permute-start.6) | collective-permute-done | bytes 270368 | tf_op jit(solution)/shard_map/ppermute | solution.py:20
  47.9 1.6 %collective-permute-start.9 = (bf16[1584,256]{1,0:T(8,128)(2,1)S(1)}, bf16[1584,256]{1,0:T(8,128)(2,1)S(1)}, u32[]{:S(2)}, u32[]{:S(2)}) collective-permute-start(bf16[1584,256]{1,0:T(8,128)(2,1)S(1)} %constant_dynamic-update-slice_fusion.2), channel_id=1, source_target_pairs={{0,2},{1,3},{2,0},{3,1},{4,6},{5,7},{6,4},{7,5},{8,10},{9,11},{10,... | collective-permute-start | bytes 2433032 | tf_op jit(solution)/shard_map/ppermute | solution.py:20
  49.6 0.6 collective-permute-start.15
  50.2 1.6 %collective-permute-start.14 = (bf16[528,256]{1,0:T(8,128)(2,1)S(1)}, bf16[528,256]{1,0:T(8,128)(2,1)S(1)}, u32[]{:S(2)}, u32[]{:S(2)}) collective-permute-start(bf16[528,256]{1,0:T(8,128)(2,1)S(1)} %collective-permute-done.1.refs_6_), channel_id=1, source_target_pairs={{0,2},{1,3},{2,0},{3,1},{4,6},{5,7},{6,4},{7,5},{8,10},{9,11},{10,... | collective-permute-start | bytes 811016 | tf_op jit(solution)/shard_map/ppermute | solution.py:20
  51.8 7.5 %pick.1 = bf16[4224,512]{1,0:T(8,128)(2,1)} custom-call(bf16[4096,512]{1,0:T(8,128)(2,1)S(1)} %copy-done, bf16[528,256]{1,0:T(8,128)(2,1)S(1)} %get-tuple-element.40.refs_0_, bf16[528,256]{1,0:T(8,128)(2,1)S(1)} %collective-permute-done.4.refs_1_, bf16[528,256]{1,0:T(8,128)(2,1)S(1)} %collective-permute-done.5.refs_2_, ...), custom_call_target="tpu_custom_call" | custom-call | tf_op jit(solution)/shard_map/pick/pallas_call | solution.py:154
  59.3 12.6 %collective-permute-done.15 = bf16[272,256]{1,0:T(8,128)(2,1)S(1)} collective-permute-done((bf16[272,256]{1,0:T(8,128)(2,1)S(1)}, bf16[272,256]{1,0:T(8,128)(2,1)S(1)}, u32[]{:S(2)}, u32[]{:S(2)}) %collective-permute-start.15) | collective-permute-done | bytes 139296 | tf_op jit(solution)/shard_map/ppermute | solution.py:20
  71.9 5.1 %collective-permute-start.2 = (bf16[256,256]{1,0:T(8,128)(2,1)S(1)}, bf16[256,256]{1,0:T(8,128)(2,1)S(1)}, u32[]{:S(2)}, u32[]{:S(2)}) collective-permute-start(bf16[256,256]{1,0:T(8,128)(2,1)S(1)} %get-tuple-element.39), channel_id=1, source_target_pairs={{0,28},{4,24},{8,20},{12,16},{16,12},{20,8},{24,4},{28,0},{1,29},{... | collective-permute-start | bytes 393224 | tf_op jit(solution)/shard_map/ppermute | solution.py:20
  77.3 0.6 collective-permute-start.13
  78.1 1.3 %copy-done.9 = bf16[4224,512]{1,0:T(8,128)(2,1)S(1)} copy-done((bf16[4224,512]{1,0:T(8,128)(2,1)S(1)}, bf16[4224,512]{1,0:T(8,128)(2,1)}, u32[]{:S(2)}) %copy-start.9) | copy-done | bytes 4325400
  79.4 0.6 fusion.13
  80.0 0.9 fusion.9
  80.9 0.6 collective-permute-start.17
  81.4 0.5 fusion.17
  81.9 1.1 fusion.2
  83.0 0.6 fusion.5
  83.7 0.9 fusion.7
  84.5 1.1 fusion
  85.7 0.6 fusion.4
  86.3 1.6 %collective-permute-start.16 = (bf16[256,256]{1,0:T(8,128)(2,1)S(1)}, bf16[256,256]{1,0:T(8,128)(2,1)S(1)}, u32[]{:S(2)}, u32[]{:S(2)}) collective-permute-start(bf16[256,256]{1,0:T(8,128)(2,1)S(1)} %collective-permute-done.2), channel_id=1, source_target_pairs={{0,2},{1,3},{2,0},{3,1},{4,6},{5,7},{6,4},{7,5},{8,10},{9,11},{10,... | collective-permute-start | bytes 393224 | tf_op jit(solution)/shard_map/ppermute | solution.py:20
  87.9 0.6 fusion.11
  88.5 3.3 %collective-permute-done.16 = bf16[256,256]{1,0:T(8,128)(2,1)S(1)} collective-permute-done((bf16[256,256]{1,0:T(8,128)(2,1)S(1)}, bf16[256,256]{1,0:T(8,128)(2,1)S(1)}, u32[]{:S(2)}, u32[]{:S(2)}) %collective-permute-start.16) | collective-permute-done | bytes 131104 | tf_op jit(solution)/shard_map/ppermute | solution.py:20
  92.2 0.5 fusion.6.near_ref
  92.8 0.9 collective-permute-done.19
  94.6 2.6 %solve.2 = (f32[4,128,256]{2,1,0:T(8,128)S(1)}, s16[528,256]{1,0:T(8,128)(2,1)S(1)}) custom-call(f32[512,512]{1,0:T(8,128)S(1)} %fusion.6.near_ref, f32[512,512]{1,0:T(8,128)S(1)} %add_add_fusion.far_ref, bf16[128,512]{1,0:T(8,128)(2,1)S(1)} %copy-done.5, f32[512,512]{1,0:T(8,128)S(1)} %copy-done.1, f32[512,512]{1,0:T(8,128)S(1)} %copy-done.2, ...), custom_call_target="tpu_custom_call" | custom-call | tf_op jit(solution)/shard_map/solve/pallas_call | solution.py:268
  97.4 2.6 %solve.3 = (f32[4,128,256]{2,1,0:T(8,128)S(1)}, s16[528,256]{1,0:T(8,128)(2,1)S(1)}) custom-call(f32[512,512]{1,0:T(8,128)S(1)} %fusion.6.near_ref, f32[512,512]{1,0:T(8,128)S(1)} %add_add_fusion.far_ref, bf16[128,512]{1,0:T(8,128)(2,1)S(1)} %copy-done.5, f32[512,512]{1,0:T(8,128)S(1)} %copy-done.1, f32[512,512]{1,0:T(8,128)S(1)} %copy-done.2, ...), custom_call_target="tpu_custom_call" | custom-call | tf_op jit(solution)/shard_map/solve/pallas_call | solution.py:268
  100.1 6.1 %collective-permute-done.20.came_ref = s16[528,256]{1,0:T(8,128)(2,1)S(1)} collective-permute-done((s16[528,256]{1,0:T(8,128)(2,1)S(1)}, s16[528,256]{1,0:T(8,128)(2,1)S(1)}, u32[]{:S(2)}, u32[]{:S(2)}) %collective-permute-start.20) | collective-permute-done | bytes 270368 | tf_op jit(solution)/shard_map/ppermute | solution.py:20
  106.4 0.8 collective-permute-start.21
  107.2 1.7 %collective-permute-done.23.came_ref = s16[528,256]{1,0:T(8,128)(2,1)S(1)} collective-permute-done((s16[528,256]{1,0:T(8,128)(2,1)S(1)}, s16[528,256]{1,0:T(8,128)(2,1)S(1)}, u32[]{:S(2)}, u32[]{:S(2)}) %collective-permute-start.23) | collective-permute-done | bytes 270368 | tf_op jit(solution)/shard_map/ppermute | solution.py:20
  109.1 1.8 %collective-permute-start.24 = (s16[272,256]{1,0:T(8,128)(2,1)S(1)}, s16[272,256]{1,0:T(8,128)(2,1)S(1)}, u32[]{:S(2)}, u32[]{:S(2)}) collective-permute-start(s16[272,256]{1,0:T(8,128)(2,1)S(1)} %get-tuple-element.62), channel_id=1, source_target_pairs={{0,8},{4,12},{8,0},{12,4},{16,24},{20,28},{24,16},{28,20},{1,9},{5... | collective-permute-start | bytes 417800 | tf_op jit(solution)/shard_map/ppermute | solution.py:20
  110.9 4.7 %collective-permute-done.21.came_ref = s16[272,256]{1,0:T(8,128)(2,1)S(1)} collective-permute-done((s16[272,256]{1,0:T(8,128)(2,1)S(1)}, s16[272,256]{1,0:T(8,128)(2,1)S(1)}, u32[]{:S(2)}, u32[]{:S(2)}) %collective-permute-start.21) | collective-permute-done | bytes 139296 | tf_op jit(solution)/shard_map/ppermute | solution.py:20
  115.8 1.5 %collective-permute-done.24.came_ref = s16[272,256]{1,0:T(8,128)(2,1)S(1)} collective-permute-done((s16[272,256]{1,0:T(8,128)(2,1)S(1)}, s16[272,256]{1,0:T(8,128)(2,1)S(1)}, u32[]{:S(2)}, u32[]{:S(2)}) %collective-permute-start.24) | collective-permute-done | bytes 139296 | tf_op jit(solution)/shard_map/ppermute | solution.py:20
  117.5 0.6 copy-done.7
  118.1 2.0 %collective-permute-done.22.came_a = s16[144,256]{1,0:T(8,128)(2,1)S(1)} collective-permute-done((s16[144,256]{1,0:T(8,128)(2,1)S(1)}, s16[144,256]{1,0:T(8,128)(2,1)S(1)}, u32[]{:S(2)}, u32[]{:S(2)}) %collective-permute-start.22) | collective-permute-done | bytes 73760 | tf_op jit(solution)/shard_map/ppermute | solution.py:20
  120.2 3.5 %collective-permute-done.25.came_b = s16[144,256]{1,0:T(8,128)(2,1)S(1)} collective-permute-done((s16[144,256]{1,0:T(8,128)(2,1)S(1)}, s16[144,256]{1,0:T(8,128)(2,1)S(1)}, u32[]{:S(2)}, u32[]{:S(2)}) %collective-permute-start.25) | collective-permute-done | bytes 73760 | tf_op jit(solution)/shard_map/ppermute | solution.py:20
  123.7 0.6 copy-done.11
  124.3 1.8 %last.1 = f32[128,512]{1,0:T(8,128)} custom-call(f32[1,128,256]{2,1,0:T(8,128)} %copy-done.6, s16[144,256]{1,0:T(8,128)(2,1)} %copy-done.10, f32[1,128,256]{2,1,0:T(8,128)} %copy-done.7, s16[144,256]{1,0:T(8,128)(2,1)} %copy-done.11), custom_call_target="tpu_custom_call" | custom-call | tf_op jit(solution)/shard_map/last/pallas_call | solution.py:318
  (64 shorter events, 3.2 us)
Async XLA Ops:
  0.7 1.6 %copy-start.4 = (bf16[4096,256]{1,0:T(8,128)(2,1)S(1)}, bf16[4096,256]{1,0:T(8,128)(2,1)}, u32[]{:S(2)}) copy-start(bf16[4096,256]{1,0:T(8,128)(2,1)} %panels_ref.1) | copy-start | bytes 6291460
  2.2 0.7 copy-start.8
  3.0 48.8 %copy-start = (bf16[4096,512]{1,0:T(8,128)(2,1)S(1)}, bf16[4096,512]{1,0:T(8,128)(2,1)}, u32[]{:S(2)}) copy-start(bf16[4096,512]{1,0:T(8,128)(2,1)} %parent_ref.1) | copy-start | bytes 12582916
  4.4 22.9 %collective-permute-start = (bf16[528,256]{1,0:T(8,128)(2,1)S(1)}, bf16[528,256]{1,0:T(8,128)(2,1)S(1)}, u32[]{:S(2)}, u32[]{:S(2)}) collective-permute-start(bf16[528,256]{1,0:T(8,128)(2,1)S(1)} %get-tuple-element.37), channel_id=1, source_target_pairs={{0,16},{4,20},{8,24},{12,28},{16,0},{20,4},{24,8},{28,12},{1,17},{... | collective-permute-start | bytes 811016 | tf_op jit(solution)/shard_map/ppermute | solution.py:20
  8.4 25.0 %collective-permute-start.7 = (bf16[528,256]{1,0:T(8,128)(2,1)S(1)}, bf16[528,256]{1,0:T(8,128)(2,1)S(1)}, u32[]{:S(2)}, u32[]{:S(2)}) collective-permute-start(bf16[528,256]{1,0:T(8,128)(2,1)S(1)} %get-tuple-element.46), channel_id=1, source_target_pairs={{0,20},{4,16},{8,28},{12,24},{16,4},{20,0},{24,12},{28,8},{1,21},{... | collective-permute-start | bytes 811016 | tf_op jit(solution)/shard_map/ppermute | solution.py:20
  9.8 27.1 %collective-permute-start.4 = (bf16[528,256]{1,0:T(8,128)(2,1)S(1)}, bf16[528,256]{1,0:T(8,128)(2,1)S(1)}, u32[]{:S(2)}, u32[]{:S(2)}) collective-permute-start(bf16[528,256]{1,0:T(8,128)(2,1)S(1)} %get-tuple-element.41), channel_id=1, source_target_pairs={{0,4},{4,0},{8,12},{12,8},{16,20},{20,16},{24,28},{28,24},{1,5},{5... | collective-permute-start | bytes 811016 | tf_op jit(solution)/shard_map/ppermute | solution.py:20
  10.0 27.3 %collective-permute-start.5 = (bf16[528,256]{1,0:T(8,128)(2,1)S(1)}, bf16[528,256]{1,0:T(8,128)(2,1)S(1)}, u32[]{:S(2)}, u32[]{:S(2)}) collective-permute-start(bf16[528,256]{1,0:T(8,128)(2,1)S(1)} %get-tuple-element.42), channel_id=1, source_target_pairs={{0,8},{4,12},{8,0},{12,4},{16,24},{20,28},{24,16},{28,20},{1,9},{5... | collective-permute-start | bytes 811016 | tf_op jit(solution)/shard_map/ppermute | solution.py:20
  11.8 37.6 %collective-permute-start.3 = (bf16[528,256]{1,0:T(8,128)(2,1)S(1)}, bf16[528,256]{1,0:T(8,128)(2,1)S(1)}, u32[]{:S(2)}, u32[]{:S(2)}) collective-permute-start(bf16[528,256]{1,0:T(8,128)(2,1)S(1)} %get-tuple-element.40.refs_0_), channel_id=1, source_target_pairs={{0,2},{1,3},{2,0},{3,1},{4,6},{5,7},{6,4},{7,5},{8,10},{9,11},{10,... | collective-permute-start | bytes 811016 | tf_op jit(solution)/shard_map/ppermute | solution.py:20
  27.3 20.6 %collective-permute-start.6 = (bf16[528,256]{1,0:T(8,128)(2,1)S(1)}, bf16[528,256]{1,0:T(8,128)(2,1)S(1)}, u32[]{:S(2)}, u32[]{:S(2)}) collective-permute-start(bf16[528,256]{1,0:T(8,128)(2,1)S(1)} %get-tuple-element.43), channel_id=1, source_target_pairs={{0,12},{4,8},{8,4},{12,0},{16,28},{20,24},{24,20},{28,16},{1,13},{... | collective-permute-start | bytes 811016 | tf_op jit(solution)/shard_map/ppermute | solution.py:20
  33.4 16.8 %collective-permute-start.1 = (bf16[528,256]{1,0:T(8,128)(2,1)S(1)}, bf16[528,256]{1,0:T(8,128)(2,1)S(1)}, u32[]{:S(2)}, u32[]{:S(2)}) collective-permute-start(bf16[528,256]{1,0:T(8,128)(2,1)S(1)} %get-tuple-element.38), channel_id=1, source_target_pairs={{0,24},{4,28},{8,16},{12,20},{16,8},{20,12},{24,0},{28,4},{1,25},{... | collective-permute-start | bytes 811016 | tf_op jit(solution)/shard_map/ppermute | solution.py:20
  36.9 12.7 %collective-permute-start.8 = (bf16[272,256]{1,0:T(8,128)(2,1)S(1)}, bf16[272,256]{1,0:T(8,128)(2,1)S(1)}, u32[]{:S(2)}, u32[]{:S(2)}) collective-permute-start(bf16[272,256]{1,0:T(8,128)(2,1)S(1)} %get-tuple-element.49), channel_id=1, source_target_pairs={{0,28},{4,24},{8,20},{12,16},{16,12},{20,8},{24,4},{28,0},{1,29},{... | collective-permute-start | bytes 417800 | tf_op jit(solution)/shard_map/ppermute | solution.py:20
  37.2 39.8 %collective-permute-start.10 = (bf16[1056,256]{1,0:T(8,128)(2,1)S(1)}, bf16[1056,256]{1,0:T(8,128)(2,1)S(1)}, u32[]{:S(2)}, u32[]{:S(2)}) collective-permute-start(bf16[1056,256]{1,0:T(8,128)(2,1)S(1)} %constant_dynamic-update-slice_fusion.5), channel_id=1, source_target_pairs={{0,2},{1,3},{2,0},{3,1},{4,6},{5,7},{6,4},{7,5},{8,10},{9,11},{10,... | collective-permute-start | bytes 1622024 | tf_op jit(solution)/shard_map/ppermute | solution.py:20
  47.9 29.9 %collective-permute-start.9 = (bf16[1584,256]{1,0:T(8,128)(2,1)S(1)}, bf16[1584,256]{1,0:T(8,128)(2,1)S(1)}, u32[]{:S(2)}, u32[]{:S(2)}) collective-permute-start(bf16[1584,256]{1,0:T(8,128)(2,1)S(1)} %constant_dynamic-update-slice_fusion.2), channel_id=1, source_target_pairs={{0,2},{1,3},{2,0},{3,1},{4,6},{5,7},{6,4},{7,5},{8,10},{9,11},{10,... | collective-permute-start | bytes 2433032 | tf_op jit(solution)/shard_map/ppermute | solution.py:20
  49.5 36.2 %collective-permute-start.11 = (bf16[528,512]{1,0:T(8,128)(2,1)S(1)}, bf16[528,512]{1,0:T(8,128)(2,1)S(1)}, u32[]{:S(2)}, u32[]{:S(2)}) collective-permute-start(bf16[528,512]{1,0:T(8,128)(2,1)S(1)} %constant_dynamic-update-slice_fusion), channel_id=1, source_target_pairs={{0,1},{1,0},{2,3},{3,2},{4,5},{5,4},{6,7},{7,6},{8,9},{9,8},{10,11... | collective-permute-start | bytes 1622024 | tf_op jit(solution)/shard_map/ppermute | solution.py:20
  49.6 22.3 %collective-permute-start.15 = (bf16[272,256]{1,0:T(8,128)(2,1)S(1)}, bf16[272,256]{1,0:T(8,128)(2,1)S(1)}, u32[]{:S(2)}, u32[]{:S(2)}) collective-permute-start(bf16[272,256]{1,0:T(8,128)(2,1)S(1)} %collective-permute-done.8.refs_7_), channel_id=1, source_target_pairs={{0,2},{1,3},{2,0},{3,1},{4,6},{5,7},{6,4},{7,5},{8,10},{9,11},{10,... | collective-permute-start | bytes 417800 | tf_op jit(solution)/shard_map/ppermute | solution.py:20
  50.2 27.0 %collective-permute-start.14 = (bf16[528,256]{1,0:T(8,128)(2,1)S(1)}, bf16[528,256]{1,0:T(8,128)(2,1)S(1)}, u32[]{:S(2)}, u32[]{:S(2)}) collective-permute-start(bf16[528,256]{1,0:T(8,128)(2,1)S(1)} %collective-permute-done.1.refs_6_), channel_id=1, source_target_pairs={{0,2},{1,3},{2,0},{3,1},{4,6},{5,7},{6,4},{7,5},{8,10},{9,11},{10,... | collective-permute-start | bytes 811016 | tf_op jit(solution)/shard_map/ppermute | solution.py:20
  71.9 14.4 %collective-permute-start.2 = (bf16[256,256]{1,0:T(8,128)(2,1)S(1)}, bf16[256,256]{1,0:T(8,128)(2,1)S(1)}, u32[]{:S(2)}, u32[]{:S(2)}) collective-permute-start(bf16[256,256]{1,0:T(8,128)(2,1)S(1)} %get-tuple-element.39), channel_id=1, source_target_pairs={{0,28},{4,24},{8,20},{12,16},{16,12},{20,8},{24,4},{28,0},{1,29},{... | collective-permute-start | bytes 393224 | tf_op jit(solution)/shard_map/ppermute | solution.py:20
  77.1 3.8 %collective-permute-start.18 = (bf16[272,512]{1,0:T(8,128)(2,1)S(1)}, bf16[272,512]{1,0:T(8,128)(2,1)S(1)}, u32[]{:S(2)}, u32[]{:S(2)}) collective-permute-start(bf16[272,512]{1,0:T(8,128)(2,1)S(1)} %constant_dynamic-update-slice_fusion.9), channel_id=1, source_target_pairs={{0,1},{1,0},{2,3},{3,2},{4,5},{5,4},{6,7},{7,6},{8,9},{9,8},{10,11... | collective-permute-start | bytes 835592 | tf_op jit(solution)/shard_map/ppermute | solution.py:20
  77.2 2.2 %copy-start.9 = (bf16[4224,512]{1,0:T(8,128)(2,1)S(1)}, bf16[4224,512]{1,0:T(8,128)(2,1)}, u32[]{:S(2)}) copy-start(bf16[4224,512]{1,0:T(8,128)(2,1)} %pick.1) | copy-start | bytes 12976132
  77.3 6.4 %collective-permute-start.13 = (bf16[1056,512]{1,0:T(8,128)(2,1)S(1)}, bf16[1056,512]{1,0:T(8,128)(2,1)S(1)}, u32[]{:S(2)}, u32[]{:S(2)}) collective-permute-start(bf16[1056,512]{1,0:T(8,128)(2,1)S(1)} %pad_maximum_fusion.1), channel_id=1, source_target_pairs={{0,1},{1,0},{2,3},{3,2},{4,5},{5,4},{6,7},{7,6},{8,9},{9,8},{10,11... | collective-permute-start | bytes 3244040 | tf_op jit(solution)/shard_map/ppermute | solution.py:20
  78.0 6.6 %collective-permute-start.12 = (bf16[1584,512]{1,0:T(8,128)(2,1)S(1)}, bf16[1584,512]{1,0:T(8,128)(2,1)S(1)}, u32[]{:S(2)}, u32[]{:S(2)}) collective-permute-start(bf16[1584,512]{1,0:T(8,128)(2,1)S(1)} %pad_maximum_fusion), channel_id=1, source_target_pairs={{0,1},{1,0},{2,3},{3,2},{4,5},{5,4},{6,7},{7,6},{8,9},{9,8},{10,11... | collective-permute-start | bytes 4866056 | tf_op jit(solution)/shard_map/ppermute | solution.py:20
  80.9 7.0 %collective-permute-start.17 = (bf16[528,512]{1,0:T(8,128)(2,1)S(1)}, bf16[528,512]{1,0:T(8,128)(2,1)S(1)}, u32[]{:S(2)}, u32[]{:S(2)}) collective-permute-start(bf16[528,512]{1,0:T(8,128)(2,1)S(1)} %constant_dynamic-update-slice_fusion.7), channel_id=1, source_target_pairs={{0,1},{1,0},{2,3},{3,2},{4,5},{5,4},{6,7},{7,6},{8,9},{9,8},{10,11... | collective-permute-start | bytes 1622024 | tf_op jit(solution)/shard_map/ppermute | solution.py:20
  86.3 5.5 %collective-permute-start.16 = (bf16[256,256]{1,0:T(8,128)(2,1)S(1)}, bf16[256,256]{1,0:T(8,128)(2,1)S(1)}, u32[]{:S(2)}, u32[]{:S(2)}) collective-permute-start(bf16[256,256]{1,0:T(8,128)(2,1)S(1)} %collective-permute-done.2), channel_id=1, source_target_pairs={{0,2},{1,3},{2,0},{3,1},{4,6},{5,7},{6,4},{7,5},{8,10},{9,11},{10,... | collective-permute-start | bytes 393224 | tf_op jit(solution)/shard_map/ppermute | solution.py:20
  92.1 1.6 %collective-permute-start.19 = (bf16[256,512]{1,0:T(8,128)(2,1)S(1)}, bf16[256,512]{1,0:T(8,128)(2,1)S(1)}, u32[]{:S(2)}, u32[]{:S(2)}) collective-permute-start(bf16[256,512]{1,0:T(8,128)(2,1)S(1)} %constant_dynamic-update-slice_fusion.11), channel_id=1, source_target_pairs={{0,1},{1,0},{2,3},{3,2},{4,5},{5,4},{6,7},{7,6},{8,9},{9,8},{10,11... | collective-permute-start | bytes 786440 | tf_op jit(solution)/shard_map/ppermute | solution.py:20
  92.8 1.3 %copy-start.1 = (f32[512,512]{1,0:T(8,128)S(1)}, f32[512,512]{1,0:T(8,128)}, u32[]{:S(2)}) copy-start(f32[512,512]{1,0:T(8,128)} %coup_ref.3) | copy-start | bytes 3145732
  92.8 1.5 %copy-start.2 = (f32[512,512]{1,0:T(8,128)S(1)}, f32[512,512]{1,0:T(8,128)}, u32[]{:S(2)}) copy-start(f32[512,512]{1,0:T(8,128)} %one_ref.3) | copy-start | bytes 3145732
  92.8 1.8 %copy-start.3 = (f32[512,512]{1,0:T(8,128)S(1)}, f32[512,512]{1,0:T(8,128)}, u32[]{:S(2)}) copy-start(f32[512,512]{1,0:T(8,128)} %two_ref.3) | copy-start | bytes 3145732
  92.8 1.8 %copy-start.5 = (bf16[128,512]{1,0:T(8,128)(2,1)S(1)}, bf16[128,512]{1,0:T(8,128)(2,1)}, u32[]{:S(2)}) copy-start(bf16[128,512]{1,0:T(8,128)(2,1)} %front_ref.3) | copy-start | bytes 393220
  97.3 8.9 %collective-permute-start.20 = (s16[528,256]{1,0:T(8,128)(2,1)S(1)}, s16[528,256]{1,0:T(8,128)(2,1)S(1)}, u32[]{:S(2)}, u32[]{:S(2)}) collective-permute-start(s16[528,256]{1,0:T(8,128)(2,1)S(1)} %get-tuple-element.54), channel_id=1, source_target_pairs={{0,8},{4,12},{8,0},{12,4},{16,24},{20,28},{24,16},{28,20},{1,9},{5... | collective-permute-start | bytes 811016 | tf_op jit(solution)/shard_map/ppermute | solution.py:20
  100.0 8.9 %collective-permute-start.23 = (s16[528,256]{1,0:T(8,128)(2,1)S(1)}, s16[528,256]{1,0:T(8,128)(2,1)S(1)}, u32[]{:S(2)}, u32[]{:S(2)}) collective-permute-start(s16[528,256]{1,0:T(8,128)(2,1)S(1)} %get-tuple-element.60), channel_id=1, source_target_pairs={{0,4},{4,0},{8,12},{12,8},{16,20},{20,16},{24,28},{28,24},{1,5},{5... | collective-permute-start | bytes 811016 | tf_op jit(solution)/shard_map/ppermute | solution.py:20
  106.4 9.3 %collective-permute-start.21 = (s16[272,256]{1,0:T(8,128)(2,1)S(1)}, s16[272,256]{1,0:T(8,128)(2,1)S(1)}, u32[]{:S(2)}, u32[]{:S(2)}) collective-permute-start(s16[272,256]{1,0:T(8,128)(2,1)S(1)} %get-tuple-element.56), channel_id=1, source_target_pairs={{0,16},{4,20},{8,24},{12,28},{16,0},{20,4},{24,8},{28,12},{1,17},{... | collective-permute-start | bytes 417800 | tf_op jit(solution)/shard_map/ppermute | solution.py:20
  109.1 8.2 %collective-permute-start.24 = (s16[272,256]{1,0:T(8,128)(2,1)S(1)}, s16[272,256]{1,0:T(8,128)(2,1)S(1)}, u32[]{:S(2)}, u32[]{:S(2)}) collective-permute-start(s16[272,256]{1,0:T(8,128)(2,1)S(1)} %get-tuple-element.62), channel_id=1, source_target_pairs={{0,8},{4,12},{8,0},{12,4},{16,24},{20,28},{24,16},{28,20},{1,9},{5... | collective-permute-start | bytes 417800 | tf_op jit(solution)/shard_map/ppermute | solution.py:20
  115.8 1.7 %copy-start.6 = (f32[1,128,256]{2,1,0:T(8,128)}, f32[1,128,256]{2,1,0:T(8,128)S(1)}, u32[]{:S(2)}) copy-start(f32[1,128,256]{2,1,0:T(8,128)S(1)} %get-tuple-element.57.kept_a) | copy-start | bytes 393220
  115.8 4.4 %collective-permute-start.22 = (s16[144,256]{1,0:T(8,128)(2,1)S(1)}, s16[144,256]{1,0:T(8,128)(2,1)S(1)}, u32[]{:S(2)}, u32[]{:S(2)}) collective-permute-start(s16[144,256]{1,0:T(8,128)(2,1)S(1)} %get-tuple-element.58), channel_id=1, source_target_pairs={{0,4},{4,0},{8,12},{12,8},{16,20},{20,16},{24,28},{28,24},{1,5},{5... | collective-permute-start | bytes 221192 | tf_op jit(solution)/shard_map/ppermute | solution.py:20
  117.5 0.7 copy-start.7
  118.1 5.6 %collective-permute-start.25 = (s16[144,256]{1,0:T(8,128)(2,1)S(1)}, s16[144,256]{1,0:T(8,128)(2,1)S(1)}, u32[]{:S(2)}, u32[]{:S(2)}) collective-permute-start(s16[144,256]{1,0:T(8,128)(2,1)S(1)} %get-tuple-element.64), channel_id=1, source_target_pairs={{0,16},{4,20},{8,24},{12,28},{16,0},{20,4},{24,8},{28,12},{1,17},{... | collective-permute-start | bytes 221192 | tf_op jit(solution)/shard_map/ppermute | solution.py:20
  120.2 3.5 %copy-start.10 = (s16[144,256]{1,0:T(8,128)(2,1)}, s16[144,256]{1,0:T(8,128)(2,1)S(1)}, u32[]{:S(2)}) copy-start(s16[144,256]{1,0:T(8,128)(2,1)S(1)} %collective-permute-done.22.came_a) | copy-start | bytes 221188
  123.7 0.6 copy-start.11

commit v4 on v3

--- a/solution.py
+++ b/solution.py
@@ -10,6 +10,7 @@
 BLK = 128
 LANES = 128
 CODE_BITS = 14.96
+WINDOW = 6
 ANY = pl.BlockSpec(memory_space=pl.ANY)
 VMEM = pl.BlockSpec(memory_space=pltpu.VMEM)
 SMEM = pl.BlockSpec(memory_space=pltpu.SMEM)
@@ -21,7 +22,7 @@
 
 
 def pack_kernel(groups, slots, rows_ref, live_ref, lists_ref, panels_ref, *refs):
-    chunks, place_ref, tile_ref = refs[: groups + 1], refs[groups + 1], refs[groups + 2]
+    chunks, place_ref, tile_ref = refs[:groups], refs[groups], refs[groups + 1]
     me = lax.axis_index("rows")
     rows_dev = rows_ref.shape[0]
     for place in range(groups):
@@ -38,25 +39,17 @@
         chunk = chunks[mask]
         tile = tile_ref.shape[0]
         chunk[pl.ds(chunk.shape[0] - tile, tile), :] = tile_ref[...].astype(chunk.dtype)
-        for at, count, part, into in pieces_of(mask, groups, slots):
-            ref = chunks[mask + part]
-            block = at // BLK * groups + place_ref[mask]
+        for slot in range(slots):
+            block = slot * groups + place_ref[mask]
+            into = (pl.ds(slot * BLK, BLK), slice(None))
 
             @pl.when(block < live_blocks)
             def _():
-                first = pl.multiple_of(block * BLK + at % BLK, 16)
-                ref[pl.ds(into, count), :] = panels_ref[pl.ds(first, count), :]
+                chunk[into] = panels_ref[pl.ds(pl.multiple_of(block * BLK, BLK), BLK), :]
 
             @pl.when(block >= live_blocks)
             def _():
-                ref[pl.ds(into, count), :] = jnp.zeros((count, ref.shape[1]), ref.dtype)
-
-
-def pieces_of(mask, groups, slots):
-    cut = slots * BLK // 2 if mask == groups - 1 else slots * BLK
-    step = min(BLK, cut)
-    for at in range(0, slots * BLK, step):
-        yield at, step, int(at >= cut), at % cut
+                chunk[into] = jnp.zeros((BLK, chunk.shape[1]), chunk.dtype)
 
 
 def list_rows(slots):
@@ -65,13 +58,13 @@
 
 def pack(lower_panels, parent_rows, live_counts, groups, slots):
     rows_dev, width = lower_panels.shape
-    rows, extra = slots * BLK, list_rows(slots)
-    counts = [rows + extra] * (groups - 1) + [rows // 2 + extra, rows // 2]
+    extra = list_rows(slots)
+    chunk = jax.ShapeDtypeStruct((slots * BLK + extra, width), lower_panels.dtype)
     return pl.pallas_call(
         functools.partial(pack_kernel, groups, slots),
-        out_shape=[jax.ShapeDtypeStruct((n, width), lower_panels.dtype) for n in counts],
+        out_shape=[chunk] * groups,
         in_specs=[SMEM, SMEM, VMEM, VMEM],
-        out_specs=[VMEM] * len(counts),
+        out_specs=[VMEM] * groups,
         scratch_shapes=[
             pltpu.SMEM((groups,), jnp.int32),
             pltpu.VMEM((extra, width), jnp.float32),
@@ -124,25 +117,12 @@
                 into = pl.multiple_of(base + i * tiles, tiles)
                 stage[pl.ds(into, tiles), :] = wide[pl.ds(row, tiles), :]
 
-        def write(into, first, rows):
-            for tile in range(tiles):
-                out_ref[pl.ds(into, rows), pl.ds(tile * LANES, LANES)] = stage[
-                    pl.ds(first * tiles + tile, rows, stride=tiles), :
-                ].astype(out_ref.dtype)
-
         into = pl.multiple_of(mask * (count + extra), 16)
-
-        @pl.when(mask < groups - 1)
-        def _():
-            write(into, 0, count)
-            out_ref[pl.ds(pl.multiple_of(into + count, 16), extra), :] = nothing
-
-        @pl.when(mask == groups - 1)
-        def _():
-            last, cut = (groups - 1) * (count + extra), count // 2
-            write(last, 0, cut)
-            out_ref[pl.ds(last + cut, extra), :] = nothing
-            write(last + cut + extra, cut, cut)
+        for tile in range(tiles):
+            out_ref[pl.ds(into, count), pl.ds(tile * LANES, LANES)] = stage[
+                pl.ds(tile, count, stride=tiles), :
+            ].astype(out_ref.dtype)
+        out_ref[pl.ds(pl.multiple_of(into + count, 16), extra), :] = nothing
 
 
 def pick(parent, chunks, slots):
@@ -344,60 +324,66 @@
     shares = lax.axis_size("rhs")
     rows_dev = parent_rows.shape[0]
     slots = rows_dev // BLK // groups
-    chunk_rows = slots * BLK
     bits = list(range(groups.bit_length() - 1))
+    half = groups // 2
+    short, long = list(range(1, half)), list(range(half, groups))
 
     chunks = pack(lower_panels, parent_rows, live_counts, groups, slots)
-    half = groups // 2
-    mask_of = list(range(groups)) + [groups - 1]
-    got, nears, fars = {0: chunks[0]}, {}, {}
-
-    def after(value, *events):
-        held = [store[key] for store, key in events]
-        value, held = lax.optimization_barrier((value, held))
-        for (store, key), now in zip(events, held):
-            store[key] = now
-        return value
-
-    def move(at, *events):
-        got[at] = swap(after(chunks[at], *events), "rows", mask_of[at])
-
-    def cross(at, *events):
-        own = after(got[at], *events)
-        nears[at] = jnp.concatenate(
-            [own] + [swap(own, "rhs", other) for other in range(2, shares, 2)], axis=1
-        )
-
-    runs = [[0], list(range(1, half)), [half, half + 1]] + [[at] for at in range(half + 2, groups + 1)]
-    for at in range(half, groups + 1):
-        move(at, *([(got, at - 2)] if at >= half + 2 else []))
-    for at in range(1, half):
-        move(at, *([(got, at - 9)] if at > 9 else []))
-    starts = [0]
-    for at in range(groups):
-        starts.append(starts[at] + chunks[at].shape[0])
-    def cross(own):
-        return jnp.concatenate(
-            [own] + [swap(own, "rhs", other) for other in range(2, shares, 2)], axis=1
-        )
-    near_total = far_total = 0.0
-    picked = pick(parent_solution, [got[at] for at in range(groups)], slots)
-    def add(i):
-        rows = [picked[starts[at] : starts[at] + chunks[at].shape[0]] for at in runs[i]]
-        rows = jnp.concatenate(rows, axis=0)
-        return near_total + panel_dot(nears[i], rows), far_total + panel_dot(fars[i], rows)
-    done = 0
-    for r, run in enumerate(runs):
-        if r == len(runs) - 1:
-            while done < len(runs) - 1 - 2:
-                near_total, far_total = add(done)
-                done += 1
-            got[groups], near_total, far_total = lax.optimization_barrier((got[groups], near_total, far_total))
-        nears[r] = cross(jnp.concatenate([got[at] for at in run], axis=0))
-        fars[r] = swap(nears[r], "rhs", 1)
-    while done < len(runs):
-        near_total, far_total = add(done)
-        done += 1
+    size = chunks[0].shape[0]
+
+    runs = [[0], short[:-1], [short[-1], long[0]]] + [[mask] for mask in long[1:]]
+    final = len(runs) - 1
+    order = [("move", short[0]), ("move", long[0]), ("cross", 0)]
+    order += [("move", mask) for mask in short[:0:-1]] + [("move", long[2]), ("cross", 1), ("cross", 2)]
+    order += [("move", mask) for mask in long[3:]] + [("move", long[1])]
+    loose = [("cross", run) for run in [final, *range(3, final)]] + [("pair", final)]
+    order += loose
+    store = {("move", 0): chunks[0]}
+    picked, totals = {}, [0.0, 0.0]
+
+    def pair(run):
+        if ("pair", run) not in store:
+            store["pair", run] = swap(store["cross", run], "rhs", 1)
+        return store["pair", run]
+
+    def add(run):
+        for mask in runs[run]:
+            if mask not in picked:
+                masks = list(range(groups - 2)) if mask < groups - 2 else list(range(groups - 2, groups))
+                rows = pick(parent_solution, [store["move", m] for m in masks], slots)
+                for i, m in enumerate(masks):
+                    picked[m] = rows[i * size : (i + 1) * size]
+        rows = jnp.concatenate([picked[mask] for mask in runs[run]], axis=0)
+        for side, panels in enumerate((store["cross", run], pair(run))):
+            totals[side] = totals[side] + panel_dot(panels, rows)
+
+    early = range(final - 1)
+    for at, event in enumerate(order):
+        kind, which = event
+        if event == ("pair", final):
+            for run in early:
+                add(run)
+        if kind == "move":
+            value = chunks[which]
+        elif kind == "cross":
+            value = jnp.concatenate([store["move", mask] for mask in runs[which]], axis=0)
+        else:
+            value = store["cross", which]
+        if at >= WINDOW and event not in loose:
+            ahead = order[at - WINDOW]
+            value, store[ahead] = lax.optimization_barrier((value, store[ahead]))
+        if event == ("pair", final):
+            value, *totals = lax.optimization_barrier((value, *totals))
+        if kind == "move":
+            store[event] = swap(value, "rows", which)
+        elif kind == "cross":
+            others = [swap(value, "rhs", other) for other in range(2, shares, 2)]
+            store[event] = jnp.concatenate([value] + others, axis=1)
+        else:
+            store[event] = swap(value, "rhs", 1)
+    for run in range(len(early), len(runs)):
+        add(run)
+    near_total, far_total = totals
 
     orders = (bits[1:] + bits[:1], bits)
     kept, sent = [None, None], [None, None]

time: 126 us -> 113 us (0.90)
  waiting for transfers between devices: 64.6 us -> 44.8 us
  starting transfers between devices: 30 us -> 33.1 us
  local copies, waits for them, and re-layouts: 5.64 us -> 7.69 us
    ppermute x26 -> x25, waiting for transfers between devices: 64.6 us -> 44.8 us  [swap(): return lax.ppermute(array, axis, [(i, i ^ mask) for i in range(size)])]
    ppermute x26 -> x25, starting transfers between devices: 30 us -> 33.1 us  [swap(): return lax.ppermute(array, axis, [(i, i ^ mask) for i in range(size)])]
    unnamed x31 -> x35, local copies, waits for them, and re-layouts: 5.55 us -> 7.57 us
    pallas_call x1 -> x2, Pallas kernels: 7.51 us -> 8.59 us  [pick(): pl.pallas_call(functools.partial(pick_kernel, groups, slots), out_shape=j...]
  transfers between devices with their start and end apart: 26 -> 25, of which waited for: 12 -> 13; matrix products, arithmetic and copies ran while one was open for 6% -> 8% of each run, Pallas kernels for 8% -> 10%
where the time goes in v4:
time: 113 us
  waiting for transfers between devices  44.8 us (40%)
  starting transfers between devices  33.1 us (29%)
  Pallas kernels  17.5 us (15%)
  matrix products  8.28 us (7%)
  local copies, waits for them, and re-layouts  7.69 us (7%)
    ppermute x25, waiting for transfers between devices, swap(): return lax.ppermute(array, axis, [(i, i ^ mask) for i in range(size)])  44.8 us
    ppermute x25, starting transfers between devices, swap(): return lax.ppermute(array, axis, [(i, i ^ mask) for i in range(size)])  33.1 us
    pallas_call x2, Pallas kernels, pick(): pl.pallas_call(functools.partial(pick_kernel, groups, slots), out_shape=j...  8.59 us
    dot_general x12, matrix products, panel_dot(): lax.dot_general(panel, rows, (((0,), (0,)), ((), ())), preferred_element_...  8.28 us
    unnamed x35, local copies, waits for them, and re-layouts  7.57 us
    pallas_call x2, Pallas kernels, solve(): pl.pallas_call(functools.partial(solve_kernel, side, order), out_shape=[b...  5.29 us
  transfers between devices with their start and end apart: 25, of which 13 were waited for; matrix products, arithmetic and copies ran while one was open for 8% of the time, Pallas kernels for 10%

profile of v4, /device:TPU:0, one launch (start us, length us, event | category | flops | bytes accessed | tf_op | source)
XLA Modules:
  0.0 112.9 jit_solution(10038514702283443170)
XLA Ops:
  0.7 1.6 %copy-done.4 = bf16[4096,256]{1,0:T(8,128)(2,1)S(1)} copy-done((bf16[4096,256]{1,0:T(8,128)(2,1)S(1)}, bf16[4096,256]{1,0:T(8,128)(2,1)}, u32[]{:S(2)}) %copy-start.4) | copy-done | bytes 2097176
  2.2 0.7 copy-done.8
  3.0 1.3 %pack.1 = (bf16[528,256]{1,0:T(8,128)(2,1)S(1)}, bf16[528,256]{1,0:T(8,128)(2,1)S(1)}, bf16[528,256]{1,0:T(8,128)(2,1)S(1)}, bf16[528,256]{1,0:T(8,128)(2,1)S(1)...) custom-call(s32[4096]{0:T(1024)S(1)} %copy-done.8, ...), custom_call_target="tpu_custom_call" | custom-call | tf_op jit(solution)/shard_map/pack/pallas_call | solution.py:63
  4.3 3.0 %collective-permute-start = (bf16[528,256]{1,0:T(8,128)(2,1)S(1)}, bf16[528,256]{1,0:T(8,128)(2,1)S(1)}, u32[]{:S(2)}, u32[]{:S(2)}) collective-permute-start(bf16[528,256]{1,0:T(8,128)(2,1)S(1)} %get-tuple-element.37.refs_0_), channel_id=1, source_target_pairs={{0,2},{1,3},{2,0},{3,1},{4,6},{5,7},{6,4},{7,5},{8,10},{9,11},{10,... | collective-permute-start | bytes 811016 | tf_op jit(solution)/shard_map/ppermute | solution.py:21
  7.3 2.6 %collective-permute-start.6 = (bf16[528,256]{1,0:T(8,128)(2,1)S(1)}, bf16[528,256]{1,0:T(8,128)(2,1)S(1)}, u32[]{:S(2)}, u32[]{:S(2)}) collective-permute-start(bf16[528,256]{1,0:T(8,128)(2,1)S(1)} %get-tuple-element.46), channel_id=1, source_target_pairs={{0,16},{4,20},{8,24},{12,28},{16,0},{20,4},{24,8},{28,12},{1,17},{... | collective-permute-start | bytes 811016 | tf_op jit(solution)/shard_map/ppermute | solution.py:21
  9.9 2.5 %collective-permute-start.5 = (bf16[528,256]{1,0:T(8,128)(2,1)S(1)}, bf16[528,256]{1,0:T(8,128)(2,1)S(1)}, u32[]{:S(2)}, u32[]{:S(2)}) collective-permute-start(bf16[528,256]{1,0:T(8,128)(2,1)S(1)} %get-tuple-element.44), channel_id=1, source_target_pairs={{0,12},{4,8},{8,4},{12,0},{16,28},{20,24},{24,20},{28,16},{1,13},{... | collective-permute-start | bytes 811016 | tf_op jit(solution)/shard_map/ppermute | solution.py:21
  13.8 3.9 %collective-permute-start.15 = (bf16[528,256]{1,0:T(8,128)(2,1)S(1)}, bf16[528,256]{1,0:T(8,128)(2,1)S(1)}, u32[]{:S(2)}, u32[]{:S(2)}) collective-permute-start(bf16[528,256]{1,0:T(8,128)(2,1)S(1)} %get-tuple-element.52), channel_id=1, source_target_pairs={{0,24},{4,28},{8,16},{12,20},{16,8},{20,12},{24,0},{28,4},{1,25},{... | collective-permute-start | bytes 811016 | tf_op jit(solution)/shard_map/ppermute | solution.py:21
  17.7 5.5 %collective-permute-done.6.refs_4_ = bf16[528,256]{1,0:T(8,128)(2,1)S(1)} collective-permute-done((bf16[528,256]{1,0:T(8,128)(2,1)S(1)}, bf16[528,256]{1,0:T(8,128)(2,1)S(1)}, u32[]{:S(2)}, u32[]{:S(2)}) %collective-permute-start.6) | collective-permute-done | bytes 270368 | tf_op jit(solution)/shard_map/ppermute | solution.py:21
  23.2 3.3 %collective-permute-start.1 = (bf16[528,256]{1,0:T(8,128)(2,1)S(1)}, bf16[528,256]{1,0:T(8,128)(2,1)S(1)}, u32[]{:S(2)}, u32[]{:S(2)}) collective-permute-start(bf16[528,256]{1,0:T(8,128)(2,1)S(1)} %get-tuple-element.38), channel_id=1, source_target_pairs={{0,28},{4,24},{8,20},{12,16},{16,12},{20,8},{24,4},{28,0},{1,29},{... | collective-permute-start | bytes 811016 | tf_op jit(solution)/shard_map/ppermute | solution.py:21
  26.6 0.6 collective-permute-start.9
  27.2 3.2 %collective-permute-done.4.refs_2_ = bf16[528,256]{1,0:T(8,128)(2,1)S(1)} collective-permute-done((bf16[528,256]{1,0:T(8,128)(2,1)S(1)}, bf16[528,256]{1,0:T(8,128)(2,1)S(1)}, u32[]{:S(2)}, u32[]{:S(2)}) %collective-permute-start.4) | collective-permute-done | bytes 270368 | tf_op jit(solution)/shard_map/ppermute | solution.py:21
  30.5 1.4 %collective-permute-start.7 = (bf16[528,256]{1,0:T(8,128)(2,1)S(1)}, bf16[528,256]{1,0:T(8,128)(2,1)S(1)}, u32[]{:S(2)}, u32[]{:S(2)}) collective-permute-start(bf16[528,256]{1,0:T(8,128)(2,1)S(1)} %get-tuple-element.48), channel_id=1, source_target_pairs={{0,20},{4,16},{8,28},{12,24},{16,4},{20,0},{24,12},{28,8},{1,21},{... | collective-permute-start | bytes 811016 | tf_op jit(solution)/shard_map/ppermute | solution.py:21
  31.9 0.9 constant_dynamic-update-slice_fusion.3
  33.3 2.9 %collective-permute-done.15.refs_0_ = bf16[528,256]{1,0:T(8,128)(2,1)S(1)} collective-permute-done((bf16[528,256]{1,0:T(8,128)(2,1)S(1)}, bf16[528,256]{1,0:T(8,128)(2,1)S(1)}, u32[]{:S(2)}, u32[]{:S(2)}) %collective-permute-start.15) | collective-permute-done | bytes 270368 | tf_op jit(solution)/shard_map/ppermute | solution.py:21
  36.8 0.7 constant_dynamic-update-slice_fusion.9
  37.5 5.5 %collective-permute-done.1.refs_1_ = bf16[528,256]{1,0:T(8,128)(2,1)S(1)} collective-permute-done((bf16[528,256]{1,0:T(8,128)(2,1)S(1)}, bf16[528,256]{1,0:T(8,128)(2,1)S(1)}, u32[]{:S(2)}, u32[]{:S(2)}) %collective-permute-start.1) | collective-permute-done | bytes 270368 | tf_op jit(solution)/shard_map/ppermute | solution.py:21
  43.0 2.1 %pick.3 = bf16[1056,512]{1,0:T(8,128)(2,1)S(1)} custom-call(bf16[4096,512]{1,0:T(8,128)(2,1)S(1)} %copy-done, bf16[528,256]{1,0:T(8,128)(2,1)S(1)} %collective-permute-done.15.refs_0_, bf16[528,256]{1,0:T(8,128)(2,1)S(1)} %collective-permute-done.1.refs_1_), custom_call_target="tpu_custom_call" | custom-call | tf_op jit(solution)/shard_map/pick/pallas_call | solution.py:134
  45.1 12.6 %collective-permute-done.7.refs_5_ = bf16[528,256]{1,0:T(8,128)(2,1)S(1)} collective-permute-done((bf16[528,256]{1,0:T(8,128)(2,1)S(1)}, bf16[528,256]{1,0:T(8,128)(2,1)S(1)}, u32[]{:S(2)}, u32[]{:S(2)}) %collective-permute-start.7) | collective-permute-done | bytes 270368 | tf_op jit(solution)/shard_map/ppermute | solution.py:21
  58.3 6.5 %pick.2 = bf16[3168,512]{1,0:T(8,128)(2,1)S(1)} custom-call(bf16[4096,512]{1,0:T(8,128)(2,1)} %parent_ref.3, bf16[528,256]{1,0:T(8,128)(2,1)S(1)} %get-tuple-element.37.refs_0_, bf16[528,256]{1,0:T(8,128)(2,1)S(1)} %collective-permute-done.3.refs_1_, bf16[528,256]{1,0:T(8,128)(2,1)S(1)} %collective-permute-done.4.refs_2_, ...), custom_call_target="tpu_custom_call" | custom-call | tf_op jit(solution)/shard_map/pick/pallas_call | solution.py:134
  64.8 1.6 %collective-permute-start.10 = (bf16[528,256]{1,0:T(8,128)(2,1)S(1)}, bf16[528,256]{1,0:T(8,128)(2,1)S(1)}, u32[]{:S(2)}, u32[]{:S(2)}) collective-permute-start(bf16[528,256]{1,0:T(8,128)(2,1)S(1)} %collective-permute-done.7.refs_5_), channel_id=1, source_target_pairs={{0,2},{1,3},{2,0},{3,1},{4,6},{5,7},{6,4},{7,5},{8,10},{9,11},{10,... | collective-permute-start | bytes 811016 | tf_op jit(solution)/shard_map/ppermute | solution.py:21
  66.4 0.6 fusion.19
  67.4 0.9 fusion.5
  68.9 0.9 fusion.9
  69.7 2.2 %collective-permute-done.10 = bf16[528,256]{1,0:T(8,128)(2,1)S(1)} collective-permute-done((bf16[528,256]{1,0:T(8,128)(2,1)S(1)}, bf16[528,256]{1,0:T(8,128)(2,1)S(1)}, u32[]{:S(2)}, u32[]{:S(2)}) %collective-permute-start.10) | collective-permute-done | bytes 270368 | tf_op jit(solution)/shard_map/ppermute | solution.py:21
  72.1 0.6 fusion.2
  73.3 0.6 convolution_add_fusion.1
  74.0 0.6 fusion.21
  74.6 0.9 fusion.3
  75.5 0.9 fusion.7
  76.3 0.6 fusion.1
  77.2 0.6 fusion.17
  77.8 0.6 add_add_fusion.1.near_ref
  79.0 0.6 fusion.11
  80.0 0.8 copy-done.1
  81.5 2.6 %solve.2 = (f32[4,128,256]{2,1,0:T(8,128)S(1)}, s16[528,256]{1,0:T(8,128)(2,1)S(1)}) custom-call(f32[512,512]{1,0:T(8,128)S(1)} %add_add_fusion.1.near_ref, f32[512,512]{1,0:T(8,128)S(1)} %add_add_fusion.far_ref, bf16[128,512]{1,0:T(8,128)(2,1)S(1)} %copy-done.5, f32[512,512]{1,0:T(8,128)S(1)} %copy-done.1, f32[512,512]{1,0:T(8,128)S(1)} %copy-done.2, ...), custom_call_target="tpu_custom_call" | custom-call | tf_op jit(solution)/shard_map/solve/pallas_call | solution.py:248
  84.1 0.8 collective-permute-start.19
  84.9 2.6 %solve.3 = (f32[4,128,256]{2,1,0:T(8,128)S(1)}, s16[528,256]{1,0:T(8,128)(2,1)S(1)}) custom-call(f32[512,512]{1,0:T(8,128)S(1)} %add_add_fusion.1.near_ref, f32[512,512]{1,0:T(8,128)S(1)} %add_add_fusion.far_ref, bf16[128,512]{1,0:T(8,128)(2,1)S(1)} %copy-done.5, f32[512,512]{1,0:T(8,128)S(1)} %copy-done.1, f32[512,512]{1,0:T(8,128)S(1)} %copy-done.2, ...), custom_call_target="tpu_custom_call" | custom-call | tf_op jit(solution)/shard_map/solve/pallas_call | solution.py:248
  87.6 1.6 %collective-permute-start.22 = (s16[528,256]{1,0:T(8,128)(2,1)S(1)}, s16[528,256]{1,0:T(8,128)(2,1)S(1)}, u32[]{:S(2)}, u32[]{:S(2)}) collective-permute-start(s16[528,256]{1,0:T(8,128)(2,1)S(1)} %get-tuple-element.62), channel_id=1, source_target_pairs={{0,4},{4,0},{8,12},{12,8},{16,20},{20,16},{24,28},{28,24},{1,5},{5... | collective-permute-start | bytes 811016 | tf_op jit(solution)/shard_map/ppermute | solution.py:21
  89.2 3.6 %collective-permute-done.19.came_ref = s16[528,256]{1,0:T(8,128)(2,1)S(1)} collective-permute-done((s16[528,256]{1,0:T(8,128)(2,1)S(1)}, s16[528,256]{1,0:T(8,128)(2,1)S(1)}, u32[]{:S(2)}, u32[]{:S(2)}) %collective-permute-start.19) | collective-permute-done | bytes 270368 | tf_op jit(solution)/shard_map/ppermute | solution.py:21
  92.9 3.4 %collective-permute-start.20 = (s16[272,256]{1,0:T(8,128)(2,1)S(1)}, s16[272,256]{1,0:T(8,128)(2,1)S(1)}, u32[]{:S(2)}, u32[]{:S(2)}) collective-permute-start(s16[272,256]{1,0:T(8,128)(2,1)S(1)} %get-tuple-element.58), channel_id=1, source_target_pairs={{0,16},{4,20},{8,24},{12,28},{16,0},{20,4},{24,8},{28,12},{1,17},{... | collective-permute-start | bytes 417800 | tf_op jit(solution)/shard_map/ppermute | solution.py:21
  96.5 1.8 %collective-permute-start.23 = (s16[272,256]{1,0:T(8,128)(2,1)S(1)}, s16[272,256]{1,0:T(8,128)(2,1)S(1)}, u32[]{:S(2)}, u32[]{:S(2)}) collective-permute-start(s16[272,256]{1,0:T(8,128)(2,1)S(1)} %get-tuple-element.64), channel_id=1, source_target_pairs={{0,8},{4,12},{8,0},{12,4},{16,24},{20,28},{24,16},{28,20},{1,9},{5... | collective-permute-start | bytes 417800 | tf_op jit(solution)/shard_map/ppermute | solution.py:21
  98.3 4.6 %collective-permute-done.20.came_ref = s16[272,256]{1,0:T(8,128)(2,1)S(1)} collective-permute-done((s16[272,256]{1,0:T(8,128)(2,1)S(1)}, s16[272,256]{1,0:T(8,128)(2,1)S(1)}, u32[]{:S(2)}, u32[]{:S(2)}) %collective-permute-start.20) | collective-permute-done | bytes 139296 | tf_op jit(solution)/shard_map/ppermute | solution.py:21
  103.8 0.6 copy-done.7
  104.4 2.5 %collective-permute-start.24 = (s16[144,256]{1,0:T(8,128)(2,1)S(1)}, s16[144,256]{1,0:T(8,128)(2,1)S(1)}, u32[]{:S(2)}, u32[]{:S(2)}) collective-permute-start(s16[144,256]{1,0:T(8,128)(2,1)S(1)} %get-tuple-element.66), channel_id=1, source_target_pairs={{0,16},{4,20},{8,24},{12,28},{16,0},{20,4},{24,8},{28,12},{1,17},{... | collective-permute-start | bytes 221192 | tf_op jit(solution)/shard_map/ppermute | solution.py:21
  106.9 0.6 collective-permute-done.21.came_a
  107.5 3.0 %collective-permute-done.24.came_b = s16[144,256]{1,0:T(8,128)(2,1)S(1)} collective-permute-done((s16[144,256]{1,0:T(8,128)(2,1)S(1)}, s16[144,256]{1,0:T(8,128)(2,1)S(1)}, u32[]{:S(2)}, u32[]{:S(2)}) %collective-permute-start.24) | collective-permute-done | bytes 73760 | tf_op jit(solution)/shard_map/ppermute | solution.py:21
  110.4 0.6 copy-done.14
  111.1 1.8 %last.1 = f32[128,512]{1,0:T(8,128)} custom-call(f32[1,128,256]{2,1,0:T(8,128)} %copy-done.6, s16[144,256]{1,0:T(8,128)(2,1)} %copy-done.13, f32[1,128,256]{2,1,0:T(8,128)} %copy-done.7, s16[144,256]{1,0:T(8,128)(2,1)} %copy-done.14), custom_call_target="tpu_custom_call" | custom-call | tf_op jit(solution)/shard_map/last/pallas_call | solution.py:298
  (68 shorter events, 7.8 us)
Async XLA Ops:
  0.7 1.6 %copy-start.4 = (bf16[4096,256]{1,0:T(8,128)(2,1)S(1)}, bf16[4096,256]{1,0:T(8,128)(2,1)}, u32[]{:S(2)}) copy-start(bf16[4096,256]{1,0:T(8,128)(2,1)} %panels_ref.1) | copy-start | bytes 6291460
  2.2 0.7 copy-start.8
  4.3 9.5 %collective-permute-start = (bf16[528,256]{1,0:T(8,128)(2,1)S(1)}, bf16[528,256]{1,0:T(8,128)(2,1)S(1)}, u32[]{:S(2)}, u32[]{:S(2)}) collective-permute-start(bf16[528,256]{1,0:T(8,128)(2,1)S(1)} %get-tuple-element.37.refs_0_), channel_id=1, source_target_pairs={{0,2},{1,3},{2,0},{3,1},{4,6},{5,7},{6,4},{7,5},{8,10},{9,11},{10,... | collective-permute-start | bytes 811016 | tf_op jit(solution)/shard_map/ppermute | solution.py:21
  7.3 15.9 %collective-permute-start.6 = (bf16[528,256]{1,0:T(8,128)(2,1)S(1)}, bf16[528,256]{1,0:T(8,128)(2,1)S(1)}, u32[]{:S(2)}, u32[]{:S(2)}) collective-permute-start(bf16[528,256]{1,0:T(8,128)(2,1)S(1)} %get-tuple-element.46), channel_id=1, source_target_pairs={{0,16},{4,20},{8,24},{12,28},{16,0},{20,4},{24,8},{28,12},{1,17},{... | collective-permute-start | bytes 811016 | tf_op jit(solution)/shard_map/ppermute | solution.py:21
  9.9 16.6 %collective-permute-start.5 = (bf16[528,256]{1,0:T(8,128)(2,1)S(1)}, bf16[528,256]{1,0:T(8,128)(2,1)S(1)}, u32[]{:S(2)}, u32[]{:S(2)}) collective-permute-start(bf16[528,256]{1,0:T(8,128)(2,1)S(1)} %get-tuple-element.44), channel_id=1, source_target_pairs={{0,12},{4,8},{8,4},{12,0},{16,28},{20,24},{24,20},{28,16},{1,13},{... | collective-permute-start | bytes 811016 | tf_op jit(solution)/shard_map/ppermute | solution.py:21
  12.4 18.0 %collective-permute-start.4 = (bf16[528,256]{1,0:T(8,128)(2,1)S(1)}, bf16[528,256]{1,0:T(8,128)(2,1)S(1)}, u32[]{:S(2)}, u32[]{:S(2)}) collective-permute-start(bf16[528,256]{1,0:T(8,128)(2,1)S(1)} %get-tuple-element.41), channel_id=1, source_target_pairs={{0,8},{4,12},{8,0},{12,4},{16,24},{20,28},{24,16},{28,20},{1,9},{5... | collective-permute-start | bytes 811016 | tf_op jit(solution)/shard_map/ppermute | solution.py:21
  12.9 17.6 %collective-permute-start.3 = (bf16[528,256]{1,0:T(8,128)(2,1)S(1)}, bf16[528,256]{1,0:T(8,128)(2,1)S(1)}, u32[]{:S(2)}, u32[]{:S(2)}) collective-permute-start(bf16[528,256]{1,0:T(8,128)(2,1)S(1)} %get-tuple-element.40), channel_id=1, source_target_pairs={{0,4},{4,0},{8,12},{12,8},{16,20},{20,16},{24,28},{28,24},{1,5},{5... | collective-permute-start | bytes 811016 | tf_op jit(solution)/shard_map/ppermute | solution.py:21
  13.8 22.4 %collective-permute-start.15 = (bf16[528,256]{1,0:T(8,128)(2,1)S(1)}, bf16[528,256]{1,0:T(8,128)(2,1)S(1)}, u32[]{:S(2)}, u32[]{:S(2)}) collective-permute-start(bf16[528,256]{1,0:T(8,128)(2,1)S(1)} %get-tuple-element.52), channel_id=1, source_target_pairs={{0,24},{4,28},{8,16},{12,20},{16,8},{20,12},{24,0},{28,4},{1,25},{... | collective-permute-start | bytes 811016 | tf_op jit(solution)/shard_map/ppermute | solution.py:21
  23.2 19.8 %collective-permute-start.1 = (bf16[528,256]{1,0:T(8,128)(2,1)S(1)}, bf16[528,256]{1,0:T(8,128)(2,1)S(1)}, u32[]{:S(2)}, u32[]{:S(2)}) collective-permute-start(bf16[528,256]{1,0:T(8,128)(2,1)S(1)} %get-tuple-element.38), channel_id=1, source_target_pairs={{0,28},{4,24},{8,20},{12,16},{16,12},{20,8},{24,4},{28,0},{1,29},{... | collective-permute-start | bytes 811016 | tf_op jit(solution)/shard_map/ppermute | solution.py:21
  26.6 40.6 %collective-permute-start.9 = (bf16[1056,256]{1,0:T(8,128)(2,1)S(1)}, bf16[1056,256]{1,0:T(8,128)(2,1)S(1)}, u32[]{:S(2)}, u32[]{:S(2)}) collective-permute-start(bf16[1056,256]{1,0:T(8,128)(2,1)S(1)} %pad_maximum_fusion.2), channel_id=1, source_target_pairs={{0,2},{1,3},{2,0},{3,1},{4,6},{5,7},{6,4},{7,5},{8,10},{9,11},{10,... | collective-permute-start | bytes 1622024 | tf_op jit(solution)/shard_map/ppermute | solution.py:21
  27.2 15.8 %copy-start = (bf16[4096,512]{1,0:T(8,128)(2,1)S(1)}, bf16[4096,512]{1,0:T(8,128)(2,1)}, u32[]{:S(2)}) copy-start(bf16[4096,512]{1,0:T(8,128)(2,1)} %parent_ref.3) | copy-start | bytes 12582916
  30.5 27.2 %collective-permute-start.7 = (bf16[528,256]{1,0:T(8,128)(2,1)S(1)}, bf16[528,256]{1,0:T(8,128)(2,1)S(1)}, u32[]{:S(2)}, u32[]{:S(2)}) collective-permute-start(bf16[528,256]{1,0:T(8,128)(2,1)S(1)} %get-tuple-element.48), channel_id=1, source_target_pairs={{0,20},{4,16},{8,28},{12,24},{16,4},{20,0},{24,12},{28,8},{1,21},{... | collective-permute-start | bytes 811016 | tf_op jit(solution)/shard_map/ppermute | solution.py:21
  32.8 35.4 %collective-permute-start.8 = (bf16[1056,256]{1,0:T(8,128)(2,1)S(1)}, bf16[1056,256]{1,0:T(8,128)(2,1)S(1)}, u32[]{:S(2)}, u32[]{:S(2)}) collective-permute-start(bf16[1056,256]{1,0:T(8,128)(2,1)S(1)} %pad_maximum_fusion.1), channel_id=1, source_target_pairs={{0,2},{1,3},{2,0},{3,1},{4,6},{5,7},{6,4},{7,5},{8,10},{9,11},{10,... | collective-permute-start | bytes 1622024 | tf_op jit(solution)/shard_map/ppermute | solution.py:21
  36.2 28.6 %collective-permute-start.16 = (bf16[528,256]{1,0:T(8,128)(2,1)S(1)}, bf16[528,256]{1,0:T(8,128)(2,1)S(1)}, u32[]{:S(2)}, u32[]{:S(2)}) collective-permute-start(bf16[528,256]{1,0:T(8,128)(2,1)S(1)} %collective-permute-done.15.refs_0_), channel_id=1, source_target_pairs={{0,2},{1,3},{2,0},{3,1},{4,6},{5,7},{6,4},{7,5},{8,10},{9,11},{10,... | collective-permute-start | bytes 811016 | tf_op jit(solution)/shard_map/ppermute | solution.py:21
  43.0 33.4 %collective-permute-start.11 = (bf16[528,512]{1,0:T(8,128)(2,1)S(1)}, bf16[528,512]{1,0:T(8,128)(2,1)S(1)}, u32[]{:S(2)}, u32[]{:S(2)}) collective-permute-start(bf16[528,512]{1,0:T(8,128)(2,1)S(1)} %pad_maximum_fusion), channel_id=1, source_target_pairs={{0,1},{1,0},{2,3},{3,2},{4,5},{5,4},{6,7},{7,6},{8,9},{9,8},{10,11... | collective-permute-start | bytes 1622024 | tf_op jit(solution)/shard_map/ppermute | solution.py:21
  45.1 21.3 %copy-start.10 = (bf16[528,512]{1,0:T(8,128)(2,1)S(1)}, bf16[528,512]{1,0:T(8,128)(2,1)}, u32[]{:S(2)}) copy-start(bf16[528,512]{1,0:T(8,128)(2,1)} %constant_dynamic-update-slice_fusion.9) | copy-start | bytes 1622020
  57.8 14.9 %collective-permute-start.2 = (bf16[528,256]{1,0:T(8,128)(2,1)S(1)}, bf16[528,256]{1,0:T(8,128)(2,1)S(1)}, u32[]{:S(2)}, u32[]{:S(2)}) collective-permute-start(bf16[528,256]{1,0:T(8,128)(2,1)S(1)} %collective-permute-done.1.refs_1_), channel_id=1, source_target_pairs={{0,2},{1,3},{2,0},{3,1},{4,6},{5,7},{6,4},{7,5},{8,10},{9,11},{10,... | collective-permute-start | bytes 811016 | tf_op jit(solution)/shard_map/ppermute | solution.py:21
  64.8 7.1 %collective-permute-start.10 = (bf16[528,256]{1,0:T(8,128)(2,1)S(1)}, bf16[528,256]{1,0:T(8,128)(2,1)S(1)}, u32[]{:S(2)}, u32[]{:S(2)}) collective-permute-start(bf16[528,256]{1,0:T(8,128)(2,1)S(1)} %collective-permute-done.7.refs_5_), channel_id=1, source_target_pairs={{0,2},{1,3},{2,0},{3,1},{4,6},{5,7},{6,4},{7,5},{8,10},{9,11},{10,... | collective-permute-start | bytes 811016 | tf_op jit(solution)/shard_map/ppermute | solution.py:21
  66.4 0.8 copy-start.11
  67.3 1.2 %copy-start.9 = (bf16[1056,512]{1,0:T(8,128)(2,1)S(1)}, bf16[1056,512]{1,0:T(8,128)(2,1)}, u32[]{:S(2)}) copy-start(bf16[1056,512]{1,0:T(8,128)(2,1)} %constant_dynamic-update-slice_fusion.3) | copy-start | bytes 3244036
  67.3 7.3 %collective-permute-start.13 = (bf16[1056,512]{1,0:T(8,128)(2,1)S(1)}, bf16[1056,512]{1,0:T(8,128)(2,1)S(1)}, u32[]{:S(2)}, u32[]{:S(2)}) collective-permute-start(bf16[1056,512]{1,0:T(8,128)(2,1)S(1)} %constant_dynamic-update-slice_fusion.4), channel_id=1, source_target_pairs={{0,1},{1,0},{2,3},{3,2},{4,5},{5,4},{6,7},{7,6},{8,9},{9,8},{10,11... | collective-permute-start | bytes 3244040 | tf_op jit(solution)/shard_map/ppermute | solution.py:21
  68.6 6.9 %collective-permute-start.12 = (bf16[1056,512]{1,0:T(8,128)(2,1)S(1)}, bf16[1056,512]{1,0:T(8,128)(2,1)S(1)}, u32[]{:S(2)}, u32[]{:S(2)}) collective-permute-start(bf16[1056,512]{1,0:T(8,128)(2,1)S(1)} %constant_dynamic-update-slice_fusion.2), channel_id=1, source_target_pairs={{0,1},{1,0},{2,3},{3,2},{4,5},{5,4},{6,7},{7,6},{8,9},{9,8},{10,11... | collective-permute-start | bytes 3244040 | tf_op jit(solution)/shard_map/ppermute | solution.py:21
  72.0 1.0 copy-start.12
  72.0 2.0 %collective-permute-start.14 = (bf16[528,512]{1,0:T(8,128)(2,1)S(1)}, bf16[528,512]{1,0:T(8,128)(2,1)S(1)}, u32[]{:S(2)}, u32[]{:S(2)}) collective-permute-start(bf16[528,512]{1,0:T(8,128)(2,1)S(1)} %constant_dynamic-update-slice_fusion.6), channel_id=1, source_target_pairs={{0,1},{1,0},{2,3},{3,2},{4,5},{5,4},{6,7},{7,6},{8,9},{9,8},{10,11... | collective-permute-start | bytes 1622024 | tf_op jit(solution)/shard_map/ppermute | solution.py:21
  73.0 4.2 %collective-permute-start.17 = (bf16[528,512]{1,0:T(8,128)(2,1)S(1)}, bf16[528,512]{1,0:T(8,128)(2,1)S(1)}, u32[]{:S(2)}, u32[]{:S(2)}) collective-permute-start(bf16[528,512]{1,0:T(8,128)(2,1)S(1)} %copy-done.12), channel_id=1, source_target_pairs={{0,1},{1,0},{2,3},{3,2},{4,5},{5,4},{6,7},{7,6},{8,9},{9,8},{10,11... | collective-permute-start | bytes 1622024 | tf_op jit(solution)/shard_map/ppermute | solution.py:21
  77.0 2.0 %collective-permute-start.18 = (bf16[528,512]{1,0:T(8,128)(2,1)S(1)}, bf16[528,512]{1,0:T(8,128)(2,1)S(1)}, u32[]{:S(2)}, u32[]{:S(2)}) collective-permute-start(bf16[528,512]{1,0:T(8,128)(2,1)S(1)} %constant_dynamic-update-slice_fusion), channel_id=1, source_target_pairs={{0,1},{1,0},{2,3},{3,2},{4,5},{5,4},{6,7},{7,6},{8,9},{9,8},{10,11... | collective-permute-start | bytes 1622024 | tf_op jit(solution)/shard_map/ppermute | solution.py:21
  79.6 1.2 %copy-start.1 = (f32[512,512]{1,0:T(8,128)S(1)}, f32[512,512]{1,0:T(8,128)}, u32[]{:S(2)}) copy-start(f32[512,512]{1,0:T(8,128)} %coup_ref.3) | copy-start | bytes 3145732
  79.6 1.5 %copy-start.2 = (f32[512,512]{1,0:T(8,128)S(1)}, f32[512,512]{1,0:T(8,128)}, u32[]{:S(2)}) copy-start(f32[512,512]{1,0:T(8,128)} %one_ref.3) | copy-start | bytes 3145732
  79.6 1.8 %copy-start.3 = (f32[512,512]{1,0:T(8,128)S(1)}, f32[512,512]{1,0:T(8,128)}, u32[]{:S(2)}) copy-start(f32[512,512]{1,0:T(8,128)} %two_ref.3) | copy-start | bytes 3145732
  79.6 1.8 %copy-start.5 = (bf16[128,512]{1,0:T(8,128)(2,1)S(1)}, bf16[128,512]{1,0:T(8,128)(2,1)}, u32[]{:S(2)}) copy-start(bf16[128,512]{1,0:T(8,128)(2,1)} %front_ref.3) | copy-start | bytes 393220
  84.1 8.6 %collective-permute-start.19 = (s16[528,256]{1,0:T(8,128)(2,1)S(1)}, s16[528,256]{1,0:T(8,128)(2,1)S(1)}, u32[]{:S(2)}, u32[]{:S(2)}) collective-permute-start(s16[528,256]{1,0:T(8,128)(2,1)S(1)} %get-tuple-element.56), channel_id=1, source_target_pairs={{0,8},{4,12},{8,0},{12,4},{16,24},{20,28},{24,16},{28,20},{1,9},{5... | collective-permute-start | bytes 811016 | tf_op jit(solution)/shard_map/ppermute | solution.py:21
  87.6 8.8 %collective-permute-start.22 = (s16[528,256]{1,0:T(8,128)(2,1)S(1)}, s16[528,256]{1,0:T(8,128)(2,1)S(1)}, u32[]{:S(2)}, u32[]{:S(2)}) collective-permute-start(s16[528,256]{1,0:T(8,128)(2,1)S(1)} %get-tuple-element.62), channel_id=1, source_target_pairs={{0,4},{4,0},{8,12},{12,8},{16,20},{20,16},{24,28},{28,24},{1,5},{5... | collective-permute-start | bytes 811016 | tf_op jit(solution)/shard_map/ppermute | solution.py:21
  92.9 10.0 %collective-permute-start.20 = (s16[272,256]{1,0:T(8,128)(2,1)S(1)}, s16[272,256]{1,0:T(8,128)(2,1)S(1)}, u32[]{:S(2)}, u32[]{:S(2)}) collective-permute-start(s16[272,256]{1,0:T(8,128)(2,1)S(1)} %get-tuple-element.58), channel_id=1, source_target_pairs={{0,16},{4,20},{8,24},{12,28},{16,0},{20,4},{24,8},{28,12},{1,17},{... | collective-permute-start | bytes 417800 | tf_op jit(solution)/shard_map/ppermute | solution.py:21
  96.5 7.1 %collective-permute-start.23 = (s16[272,256]{1,0:T(8,128)(2,1)S(1)}, s16[272,256]{1,0:T(8,128)(2,1)S(1)}, u32[]{:S(2)}, u32[]{:S(2)}) collective-permute-start(s16[272,256]{1,0:T(8,128)(2,1)S(1)} %get-tuple-element.64), channel_id=1, source_target_pairs={{0,8},{4,12},{8,0},{12,4},{16,24},{20,28},{24,16},{28,20},{1,9},{5... | collective-permute-start | bytes 417800 | tf_op jit(solution)/shard_map/ppermute | solution.py:21
  103.0 0.7 copy-start.6
  103.0 4.4 %collective-permute-start.21 = (s16[144,256]{1,0:T(8,128)(2,1)S(1)}, s16[144,256]{1,0:T(8,128)(2,1)S(1)}, u32[]{:S(2)}, u32[]{:S(2)}) collective-permute-start(s16[144,256]{1,0:T(8,128)(2,1)S(1)} %get-tuple-element.60), channel_id=1, source_target_pairs={{0,4},{4,0},{8,12},{12,8},{16,20},{20,16},{24,28},{28,24},{1,5},{5... | collective-permute-start | bytes 221192 | tf_op jit(solution)/shard_map/ppermute | solution.py:21
  103.7 0.7 copy-start.7
  104.4 6.0 %collective-permute-start.24 = (s16[144,256]{1,0:T(8,128)(2,1)S(1)}, s16[144,256]{1,0:T(8,128)(2,1)S(1)}, u32[]{:S(2)}, u32[]{:S(2)}) collective-permute-start(s16[144,256]{1,0:T(8,128)(2,1)S(1)} %get-tuple-element.66), channel_id=1, source_target_pairs={{0,16},{4,20},{8,24},{12,28},{16,0},{20,4},{24,8},{28,12},{1,17},{... | collective-permute-start | bytes 221192 | tf_op jit(solution)/shard_map/ppermute | solution.py:21
  107.5 3.0 %copy-start.13 = (s16[144,256]{1,0:T(8,128)(2,1)}, s16[144,256]{1,0:T(8,128)(2,1)S(1)}, u32[]{:S(2)}) copy-start(s16[144,256]{1,0:T(8,128)(2,1)S(1)} %collective-permute-done.21.came_a) | copy-start | bytes 221188
  110.4 0.6 copy-start.14

commit v5 on v4

--- a/solution.py
+++ b/solution.py
@@ -160,6 +160,13 @@
     return dot(lh, rh) + (dot(lh, rl) + dot(ll, rh))
 
 
+def triangle_dot(matrix, rows):
+    half = matrix[0].shape[0] // 2
+    upper = dot3([part[:half] for part in matrix], rows)
+    lower = dot3([part[half:, half:] for part in matrix], [part[half:] for part in rows])
+    return jnp.concatenate([upper, lower], axis=0)
+
+
 def encode(value):
     value = value * 0.25
     most = jnp.maximum(jnp.max(jnp.abs(value), axis=0, keepdims=True), 1e-30)
@@ -217,9 +224,9 @@
             resid[pl.ds(at, width), :] = -part_ref[pl.ds(i * width, width), cols]
     mine = pl.ds(pl.multiple_of(me * pivot_share, pivot_share), pivot_share)
     resid[mine, :] += front_ref[:, cols].astype(jnp.float32)
-    second = dot3(split(two_ref[...]), split(resid[pl.ds(panel, panel), :]))
+    second = triangle_dot(split(two_ref[...]), split(resid[pl.ds(panel, panel), :]))
     reduced = resid[pl.ds(0, panel), :] - dot3(split(coup_ref[...]), split(second))
-    first = dot3(split(one_ref[...]), split(reduced))
+    first = triangle_dot(split(one_ref[...]), split(reduced))
     for block in range(groups):
         source = first if block < groups // 2 else second
         at = (block % (groups // 2)) * pivot_share

time: 113 us -> 113 us (level)
  transfers between devices with their start and end apart: 25 -> 25, of which waited for: 13 -> 12; matrix products, arithmetic and copies ran while one was open for 8% -> 9% of each run, Pallas kernels for 10% -> 10%
where the time goes in v5:
time: 113 us
  waiting for transfers between devices  45.3 us (40%)
  starting transfers between devices  32.5 us (29%)
  Pallas kernels  17.2 us (15%)
  matrix products  8.27 us (7%)
  local copies, waits for them, and re-layouts  7.7 us (7%)
    ppermute x25, waiting for transfers between devices, swap(): return lax.ppermute(array, axis, [(i, i ^ mask) for i in range(size)])  45.3 us
    ppermute x25, starting transfers between devices, swap(): return lax.ppermute(array, axis, [(i, i ^ mask) for i in range(size)])  32.5 us
    pallas_call x2, Pallas kernels, pick(): pl.pallas_call(functools.partial(pick_kernel, groups, slots), out_shape=j...  8.59 us
    dot_general x12, matrix products, panel_dot(): lax.dot_general(panel, rows, (((0,), (0,)), ((), ())), preferred_element_...  8.27 us
    unnamed x35, local copies, waits for them, and re-layouts  7.57 us
    pallas_call x2, Pallas kernels, solve(): pl.pallas_call(functools.partial(solve_kernel, side, order), out_shape=[b...  4.97 us
  transfers between devices with their start and end apart: 25, of which 12 were waited for; matrix products, arithmetic and copies ran while one was open for 9% of the time, Pallas kernels for 10%

profile of v5, /device:TPU:0, one launch (start us, length us, event | category | flops | bytes accessed | tf_op | source)
XLA Modules:
  0.0 112.5 jit_solution(17476566790135843128)
XLA Ops:
  0.7 1.6 %copy-done.4 = bf16[4096,256]{1,0:T(8,128)(2,1)S(1)} copy-done((bf16[4096,256]{1,0:T(8,128)(2,1)S(1)}, bf16[4096,256]{1,0:T(8,128)(2,1)}, u32[]{:S(2)}) %copy-start.4) | copy-done | bytes 2097176
  2.2 0.7 copy-done.8
  3.0 1.4 %pack.1 = (bf16[528,256]{1,0:T(8,128)(2,1)S(1)}, bf16[528,256]{1,0:T(8,128)(2,1)S(1)}, bf16[528,256]{1,0:T(8,128)(2,1)S(1)}, bf16[528,256]{1,0:T(8,128)(2,1)S(1)...) custom-call(s32[4096]{0:T(1024)S(1)} %copy-done.8, ...), custom_call_target="tpu_custom_call" | custom-call | tf_op jit(solution)/shard_map/pack/pallas_call | solution.py:63
  4.4 3.0 %collective-permute-start = (bf16[528,256]{1,0:T(8,128)(2,1)S(1)}, bf16[528,256]{1,0:T(8,128)(2,1)S(1)}, u32[]{:S(2)}, u32[]{:S(2)}) collective-permute-start(bf16[528,256]{1,0:T(8,128)(2,1)S(1)} %get-tuple-element.37.refs_0_), channel_id=1, source_target_pairs={{0,2},{1,3},{2,0},{3,1},{4,6},{5,7},{6,4},{7,5},{8,10},{9,11},{10,... | collective-permute-start | bytes 811016 | tf_op jit(solution)/shard_map/ppermute | solution.py:21
  7.4 2.5 %collective-permute-start.6 = (bf16[528,256]{1,0:T(8,128)(2,1)S(1)}, bf16[528,256]{1,0:T(8,128)(2,1)S(1)}, u32[]{:S(2)}, u32[]{:S(2)}) collective-permute-start(bf16[528,256]{1,0:T(8,128)(2,1)S(1)} %get-tuple-element.46), channel_id=1, source_target_pairs={{0,16},{4,20},{8,24},{12,28},{16,0},{20,4},{24,8},{28,12},{1,17},{... | collective-permute-start | bytes 811016 | tf_op jit(solution)/shard_map/ppermute | solution.py:21
  9.9 2.5 %collective-permute-start.5 = (bf16[528,256]{1,0:T(8,128)(2,1)S(1)}, bf16[528,256]{1,0:T(8,128)(2,1)S(1)}, u32[]{:S(2)}, u32[]{:S(2)}) collective-permute-start(bf16[528,256]{1,0:T(8,128)(2,1)S(1)} %get-tuple-element.44), channel_id=1, source_target_pairs={{0,12},{4,8},{8,4},{12,0},{16,28},{20,24},{24,20},{28,16},{1,13},{... | collective-permute-start | bytes 811016 | tf_op jit(solution)/shard_map/ppermute | solution.py:21
  13.8 3.8 %collective-permute-start.15 = (bf16[528,256]{1,0:T(8,128)(2,1)S(1)}, bf16[528,256]{1,0:T(8,128)(2,1)S(1)}, u32[]{:S(2)}, u32[]{:S(2)}) collective-permute-start(bf16[528,256]{1,0:T(8,128)(2,1)S(1)} %get-tuple-element.52), channel_id=1, source_target_pairs={{0,24},{4,28},{8,16},{12,20},{16,8},{20,12},{24,0},{28,4},{1,25},{... | collective-permute-start | bytes 811016 | tf_op jit(solution)/shard_map/ppermute | solution.py:21
  17.7 5.5 %collective-permute-done.6.refs_4_ = bf16[528,256]{1,0:T(8,128)(2,1)S(1)} collective-permute-done((bf16[528,256]{1,0:T(8,128)(2,1)S(1)}, bf16[528,256]{1,0:T(8,128)(2,1)S(1)}, u32[]{:S(2)}, u32[]{:S(2)}) %collective-permute-start.6) | collective-permute-done | bytes 270368 | tf_op jit(solution)/shard_map/ppermute | solution.py:21
  23.2 3.4 %collective-permute-start.1 = (bf16[528,256]{1,0:T(8,128)(2,1)S(1)}, bf16[528,256]{1,0:T(8,128)(2,1)S(1)}, u32[]{:S(2)}, u32[]{:S(2)}) collective-permute-start(bf16[528,256]{1,0:T(8,128)(2,1)S(1)} %get-tuple-element.38), channel_id=1, source_target_pairs={{0,28},{4,24},{8,20},{12,16},{16,12},{20,8},{24,4},{28,0},{1,29},{... | collective-permute-start | bytes 811016 | tf_op jit(solution)/shard_map/ppermute | solution.py:21
  26.6 0.6 collective-permute-start.9
  27.3 12.2 %collective-permute-done.4.refs_2_ = bf16[528,256]{1,0:T(8,128)(2,1)S(1)} collective-permute-done((bf16[528,256]{1,0:T(8,128)(2,1)S(1)}, bf16[528,256]{1,0:T(8,128)(2,1)S(1)}, u32[]{:S(2)}, u32[]{:S(2)}) %collective-permute-start.4) | collective-permute-done | bytes 270368 | tf_op jit(solution)/shard_map/ppermute | solution.py:21
  39.6 0.9 constant_dynamic-update-slice_fusion.3
  40.7 1.7 %collective-permute-start.16 = (bf16[528,256]{1,0:T(8,128)(2,1)S(1)}, bf16[528,256]{1,0:T(8,128)(2,1)S(1)}, u32[]{:S(2)}, u32[]{:S(2)}) collective-permute-start(bf16[528,256]{1,0:T(8,128)(2,1)S(1)} %collective-permute-done.15.refs_0_), channel_id=1, source_target_pairs={{0,2},{1,3},{2,0},{3,1},{4,6},{5,7},{6,4},{7,5},{8,10},{9,11},{10,... | collective-permute-start | bytes 811016 | tf_op jit(solution)/shard_map/ppermute | solution.py:21
  42.5 0.7 constant_dynamic-update-slice_fusion.9
  43.3 2.1 %pick.3 = bf16[1056,512]{1,0:T(8,128)(2,1)S(1)} custom-call(bf16[4096,512]{1,0:T(8,128)(2,1)S(1)} %copy-done, bf16[528,256]{1,0:T(8,128)(2,1)S(1)} %collective-permute-done.15.refs_0_, bf16[528,256]{1,0:T(8,128)(2,1)S(1)} %collective-permute-done.1.refs_1_), custom_call_target="tpu_custom_call" | custom-call | tf_op jit(solution)/shard_map/pick/pallas_call | solution.py:134
  45.4 12.3 %collective-permute-done.7.refs_5_ = bf16[528,256]{1,0:T(8,128)(2,1)S(1)} collective-permute-done((bf16[528,256]{1,0:T(8,128)(2,1)S(1)}, bf16[528,256]{1,0:T(8,128)(2,1)S(1)}, u32[]{:S(2)}, u32[]{:S(2)}) %collective-permute-start.7) | collective-permute-done | bytes 270368 | tf_op jit(solution)/shard_map/ppermute | solution.py:21
  57.7 0.5 collective-permute-start.2
  58.3 6.5 %pick.2 = bf16[3168,512]{1,0:T(8,128)(2,1)S(1)} custom-call(bf16[4096,512]{1,0:T(8,128)(2,1)} %parent_ref.3, bf16[528,256]{1,0:T(8,128)(2,1)S(1)} %get-tuple-element.37.refs_0_, bf16[528,256]{1,0:T(8,128)(2,1)S(1)} %collective-permute-done.3.refs_1_, bf16[528,256]{1,0:T(8,128)(2,1)S(1)} %collective-permute-done.4.refs_2_, ...), custom_call_target="tpu_custom_call" | custom-call | tf_op jit(solution)/shard_map/pick/pallas_call | solution.py:134
  64.8 1.6 %collective-permute-start.10 = (bf16[528,256]{1,0:T(8,128)(2,1)S(1)}, bf16[528,256]{1,0:T(8,128)(2,1)S(1)}, u32[]{:S(2)}, u32[]{:S(2)}) collective-permute-start(bf16[528,256]{1,0:T(8,128)(2,1)S(1)} %collective-permute-done.7.refs_5_), channel_id=1, source_target_pairs={{0,2},{1,3},{2,0},{3,1},{4,6},{5,7},{6,4},{7,5},{8,10},{9,11},{10,... | collective-permute-start | bytes 811016 | tf_op jit(solution)/shard_map/ppermute | solution.py:21
  66.4 0.6 fusion.19
  67.3 0.9 fusion.5
  68.8 0.9 fusion.9
  69.7 2.2 %collective-permute-done.10 = bf16[528,256]{1,0:T(8,128)(2,1)S(1)} collective-permute-done((bf16[528,256]{1,0:T(8,128)(2,1)S(1)}, bf16[528,256]{1,0:T(8,128)(2,1)S(1)}, u32[]{:S(2)}, u32[]{:S(2)}) %collective-permute-start.10) | collective-permute-done | bytes 270368 | tf_op jit(solution)/shard_map/ppermute | solution.py:21
  72.0 0.6 fusion.2
  73.2 0.6 convolution_add_fusion.1
  73.9 0.6 fusion.21
  74.6 0.9 fusion.3
  75.4 0.9 fusion.7
  76.3 0.6 fusion.1
  77.2 0.6 fusion.17
  77.8 0.6 add_add_fusion.1.near_ref
  78.4 0.5 collective-permute-done.18
  79.0 0.6 fusion.11
  80.0 0.8 copy-done.1
  81.4 2.5 %solve.2 = (f32[4,128,256]{2,1,0:T(8,128)S(1)}, s16[528,256]{1,0:T(8,128)(2,1)S(1)}) custom-call(f32[512,512]{1,0:T(8,128)S(1)} %add_add_fusion.1.near_ref, f32[512,512]{1,0:T(8,128)S(1)} %add_add_fusion.far_ref, bf16[128,512]{1,0:T(8,128)(2,1)S(1)} %copy-done.5, f32[512,512]{1,0:T(8,128)S(1)} %copy-done.1, f32[512,512]{1,0:T(8,128)S(1)} %copy-done.2, ...), custom_call_target="tpu_custom_call" | custom-call | tf_op jit(solution)/shard_map/solve/pallas_call | solution.py:255
  83.9 0.8 collective-permute-start.19
  84.8 2.5 %solve.3 = (f32[4,128,256]{2,1,0:T(8,128)S(1)}, s16[528,256]{1,0:T(8,128)(2,1)S(1)}) custom-call(f32[512,512]{1,0:T(8,128)S(1)} %add_add_fusion.1.near_ref, f32[512,512]{1,0:T(8,128)S(1)} %add_add_fusion.far_ref, bf16[128,512]{1,0:T(8,128)(2,1)S(1)} %copy-done.5, f32[512,512]{1,0:T(8,128)S(1)} %copy-done.1, f32[512,512]{1,0:T(8,128)S(1)} %copy-done.2, ...), custom_call_target="tpu_custom_call" | custom-call | tf_op jit(solution)/shard_map/solve/pallas_call | solution.py:255
  87.2 1.7 %collective-permute-start.22 = (s16[528,256]{1,0:T(8,128)(2,1)S(1)}, s16[528,256]{1,0:T(8,128)(2,1)S(1)}, u32[]{:S(2)}, u32[]{:S(2)}) collective-permute-start(s16[528,256]{1,0:T(8,128)(2,1)S(1)} %get-tuple-element.62), channel_id=1, source_target_pairs={{0,4},{4,0},{8,12},{12,8},{16,20},{20,16},{24,28},{28,24},{1,5},{5... | collective-permute-start | bytes 811016 | tf_op jit(solution)/shard_map/ppermute | solution.py:21
  88.9 3.7 %collective-permute-done.19.came_ref = s16[528,256]{1,0:T(8,128)(2,1)S(1)} collective-permute-done((s16[528,256]{1,0:T(8,128)(2,1)S(1)}, s16[528,256]{1,0:T(8,128)(2,1)S(1)}, u32[]{:S(2)}, u32[]{:S(2)}) %collective-permute-start.19) | collective-permute-done | bytes 270368 | tf_op jit(solution)/shard_map/ppermute | solution.py:21
  92.7 3.5 %collective-permute-start.20 = (s16[272,256]{1,0:T(8,128)(2,1)S(1)}, s16[272,256]{1,0:T(8,128)(2,1)S(1)}, u32[]{:S(2)}, u32[]{:S(2)}) collective-permute-start(s16[272,256]{1,0:T(8,128)(2,1)S(1)} %get-tuple-element.58), channel_id=1, source_target_pairs={{0,16},{4,20},{8,24},{12,28},{16,0},{20,4},{24,8},{28,12},{1,17},{... | collective-permute-start | bytes 417800 | tf_op jit(solution)/shard_map/ppermute | solution.py:21
  96.4 1.8 %collective-permute-start.23 = (s16[272,256]{1,0:T(8,128)(2,1)S(1)}, s16[272,256]{1,0:T(8,128)(2,1)S(1)}, u32[]{:S(2)}, u32[]{:S(2)}) collective-permute-start(s16[272,256]{1,0:T(8,128)(2,1)S(1)} %get-tuple-element.64), channel_id=1, source_target_pairs={{0,8},{4,12},{8,0},{12,4},{16,24},{20,28},{24,16},{28,20},{1,9},{5... | collective-permute-start | bytes 417800 | tf_op jit(solution)/shard_map/ppermute | solution.py:21
  98.2 4.6 %collective-permute-done.20.came_ref = s16[272,256]{1,0:T(8,128)(2,1)S(1)} collective-permute-done((s16[272,256]{1,0:T(8,128)(2,1)S(1)}, s16[272,256]{1,0:T(8,128)(2,1)S(1)}, u32[]{:S(2)}, u32[]{:S(2)}) %collective-permute-start.20) | collective-permute-done | bytes 139296 | tf_op jit(solution)/shard_map/ppermute | solution.py:21
  103.6 0.6 copy-done.7
  104.3 2.3 %collective-permute-start.24 = (s16[144,256]{1,0:T(8,128)(2,1)S(1)}, s16[144,256]{1,0:T(8,128)(2,1)S(1)}, u32[]{:S(2)}, u32[]{:S(2)}) collective-permute-start(s16[144,256]{1,0:T(8,128)(2,1)S(1)} %get-tuple-element.66), channel_id=1, source_target_pairs={{0,16},{4,20},{8,24},{12,28},{16,0},{20,4},{24,8},{28,12},{1,17},{... | collective-permute-start | bytes 221192 | tf_op jit(solution)/shard_map/ppermute | solution.py:21
  106.6 0.8 collective-permute-done.21.came_a
  107.3 2.7 %collective-permute-done.24.came_b = s16[144,256]{1,0:T(8,128)(2,1)S(1)} collective-permute-done((s16[144,256]{1,0:T(8,128)(2,1)S(1)}, s16[144,256]{1,0:T(8,128)(2,1)S(1)}, u32[]{:S(2)}, u32[]{:S(2)}) %collective-permute-start.24) | collective-permute-done | bytes 73760 | tf_op jit(solution)/shard_map/ppermute | solution.py:21
  110.1 0.6 copy-done.14
  110.7 1.8 %last.1 = f32[128,512]{1,0:T(8,128)} custom-call(f32[1,128,256]{2,1,0:T(8,128)} %copy-done.6, s16[144,256]{1,0:T(8,128)(2,1)} %copy-done.13, f32[1,128,256]{2,1,0:T(8,128)} %copy-done.7, s16[144,256]{1,0:T(8,128)(2,1)} %copy-done.14), custom_call_target="tpu_custom_call" | custom-call | tf_op jit(solution)/shard_map/last/pallas_call | solution.py:305
  (68 shorter events, 6.1 us)
Async XLA Ops:
  0.7 1.6 %copy-start.4 = (bf16[4096,256]{1,0:T(8,128)(2,1)S(1)}, bf16[4096,256]{1,0:T(8,128)(2,1)}, u32[]{:S(2)}) copy-start(bf16[4096,256]{1,0:T(8,128)(2,1)} %panels_ref.1) | copy-start | bytes 6291460
  2.2 0.7 copy-start.8
  4.4 9.5 %collective-permute-start = (bf16[528,256]{1,0:T(8,128)(2,1)S(1)}, bf16[528,256]{1,0:T(8,128)(2,1)S(1)}, u32[]{:S(2)}, u32[]{:S(2)}) collective-permute-start(bf16[528,256]{1,0:T(8,128)(2,1)S(1)} %get-tuple-element.37.refs_0_), channel_id=1, source_target_pairs={{0,2},{1,3},{2,0},{3,1},{4,6},{5,7},{6,4},{7,5},{8,10},{9,11},{10,... | collective-permute-start | bytes 811016 | tf_op jit(solution)/shard_map/ppermute | solution.py:21
  7.4 15.8 %collective-permute-start.6 = (bf16[528,256]{1,0:T(8,128)(2,1)S(1)}, bf16[528,256]{1,0:T(8,128)(2,1)S(1)}, u32[]{:S(2)}, u32[]{:S(2)}) collective-permute-start(bf16[528,256]{1,0:T(8,128)(2,1)S(1)} %get-tuple-element.46), channel_id=1, source_target_pairs={{0,16},{4,20},{8,24},{12,28},{16,0},{20,4},{24,8},{28,12},{1,17},{... | collective-permute-start | bytes 811016 | tf_op jit(solution)/shard_map/ppermute | solution.py:21
  9.9 16.7 %collective-permute-start.5 = (bf16[528,256]{1,0:T(8,128)(2,1)S(1)}, bf16[528,256]{1,0:T(8,128)(2,1)S(1)}, u32[]{:S(2)}, u32[]{:S(2)}) collective-permute-start(bf16[528,256]{1,0:T(8,128)(2,1)S(1)} %get-tuple-element.44), channel_id=1, source_target_pairs={{0,12},{4,8},{8,4},{12,0},{16,28},{20,24},{24,20},{28,16},{1,13},{... | collective-permute-start | bytes 811016 | tf_op jit(solution)/shard_map/ppermute | solution.py:21
  12.4 27.0 %collective-permute-start.4 = (bf16[528,256]{1,0:T(8,128)(2,1)S(1)}, bf16[528,256]{1,0:T(8,128)(2,1)S(1)}, u32[]{:S(2)}, u32[]{:S(2)}) collective-permute-start(bf16[528,256]{1,0:T(8,128)(2,1)S(1)} %get-tuple-element.41), channel_id=1, source_target_pairs={{0,8},{4,12},{8,0},{12,4},{16,24},{20,28},{24,16},{28,20},{1,9},{5... | collective-permute-start | bytes 811016 | tf_op jit(solution)/shard_map/ppermute | solution.py:21
  12.9 26.5 %collective-permute-start.3 = (bf16[528,256]{1,0:T(8,128)(2,1)S(1)}, bf16[528,256]{1,0:T(8,128)(2,1)S(1)}, u32[]{:S(2)}, u32[]{:S(2)}) collective-permute-start(bf16[528,256]{1,0:T(8,128)(2,1)S(1)} %get-tuple-element.40), channel_id=1, source_target_pairs={{0,4},{4,0},{8,12},{12,8},{16,20},{20,16},{24,28},{28,24},{1,5},{5... | collective-permute-start | bytes 811016 | tf_op jit(solution)/shard_map/ppermute | solution.py:21
  13.8 26.9 %collective-permute-start.15 = (bf16[528,256]{1,0:T(8,128)(2,1)S(1)}, bf16[528,256]{1,0:T(8,128)(2,1)S(1)}, u32[]{:S(2)}, u32[]{:S(2)}) collective-permute-start(bf16[528,256]{1,0:T(8,128)(2,1)S(1)} %get-tuple-element.52), channel_id=1, source_target_pairs={{0,24},{4,28},{8,16},{12,20},{16,8},{20,12},{24,0},{28,4},{1,25},{... | collective-permute-start | bytes 811016 | tf_op jit(solution)/shard_map/ppermute | solution.py:21
  23.2 20.1 %collective-permute-start.1 = (bf16[528,256]{1,0:T(8,128)(2,1)S(1)}, bf16[528,256]{1,0:T(8,128)(2,1)S(1)}, u32[]{:S(2)}, u32[]{:S(2)}) collective-permute-start(bf16[528,256]{1,0:T(8,128)(2,1)S(1)} %get-tuple-element.38), channel_id=1, source_target_pairs={{0,28},{4,24},{8,20},{12,16},{16,12},{20,8},{24,4},{28,0},{1,29},{... | collective-permute-start | bytes 811016 | tf_op jit(solution)/shard_map/ppermute | solution.py:21
  26.6 40.6 %collective-permute-start.9 = (bf16[1056,256]{1,0:T(8,128)(2,1)S(1)}, bf16[1056,256]{1,0:T(8,128)(2,1)S(1)}, u32[]{:S(2)}, u32[]{:S(2)}) collective-permute-start(bf16[1056,256]{1,0:T(8,128)(2,1)S(1)} %pad_maximum_fusion.2), channel_id=1, source_target_pairs={{0,2},{1,3},{2,0},{3,1},{4,6},{5,7},{6,4},{7,5},{8,10},{9,11},{10,... | collective-permute-start | bytes 1622024 | tf_op jit(solution)/shard_map/ppermute | solution.py:21
  27.2 16.0 %copy-start = (bf16[4096,512]{1,0:T(8,128)(2,1)S(1)}, bf16[4096,512]{1,0:T(8,128)(2,1)}, u32[]{:S(2)}) copy-start(bf16[4096,512]{1,0:T(8,128)(2,1)} %parent_ref.3) | copy-start | bytes 12582916
  39.5 18.2 %collective-permute-start.7 = (bf16[528,256]{1,0:T(8,128)(2,1)S(1)}, bf16[528,256]{1,0:T(8,128)(2,1)S(1)}, u32[]{:S(2)}, u32[]{:S(2)}) collective-permute-start(bf16[528,256]{1,0:T(8,128)(2,1)S(1)} %get-tuple-element.48), channel_id=1, source_target_pairs={{0,20},{4,16},{8,28},{12,24},{16,4},{20,0},{24,12},{28,8},{1,21},{... | collective-permute-start | bytes 811016 | tf_op jit(solution)/shard_map/ppermute | solution.py:21
  40.4 27.7 %collective-permute-start.8 = (bf16[1056,256]{1,0:T(8,128)(2,1)S(1)}, bf16[1056,256]{1,0:T(8,128)(2,1)S(1)}, u32[]{:S(2)}, u32[]{:S(2)}) collective-permute-start(bf16[1056,256]{1,0:T(8,128)(2,1)S(1)} %pad_maximum_fusion.1), channel_id=1, source_target_pairs={{0,2},{1,3},{2,0},{3,1},{4,6},{5,7},{6,4},{7,5},{8,10},{9,11},{10,... | collective-permute-start | bytes 1622024 | tf_op jit(solution)/shard_map/ppermute | solution.py:21
  40.7 24.0 %collective-permute-start.16 = (bf16[528,256]{1,0:T(8,128)(2,1)S(1)}, bf16[528,256]{1,0:T(8,128)(2,1)S(1)}, u32[]{:S(2)}, u32[]{:S(2)}) collective-permute-start(bf16[528,256]{1,0:T(8,128)(2,1)S(1)} %collective-permute-done.15.refs_0_), channel_id=1, source_target_pairs={{0,2},{1,3},{2,0},{3,1},{4,6},{5,7},{6,4},{7,5},{8,10},{9,11},{10,... | collective-permute-start | bytes 811016 | tf_op jit(solution)/shard_map/ppermute | solution.py:21
  43.2 33.1 %collective-permute-start.11 = (bf16[528,512]{1,0:T(8,128)(2,1)S(1)}, bf16[528,512]{1,0:T(8,128)(2,1)S(1)}, u32[]{:S(2)}, u32[]{:S(2)}) collective-permute-start(bf16[528,512]{1,0:T(8,128)(2,1)S(1)} %pad_maximum_fusion), channel_id=1, source_target_pairs={{0,1},{1,0},{2,3},{3,2},{4,5},{5,4},{6,7},{7,6},{8,9},{9,8},{10,11... | collective-permute-start | bytes 1622024 | tf_op jit(solution)/shard_map/ppermute | solution.py:21
  45.4 21.0 %copy-start.10 = (bf16[528,512]{1,0:T(8,128)(2,1)S(1)}, bf16[528,512]{1,0:T(8,128)(2,1)}, u32[]{:S(2)}) copy-start(bf16[528,512]{1,0:T(8,128)(2,1)} %constant_dynamic-update-slice_fusion.9) | copy-start | bytes 1622020
  57.7 14.9 %collective-permute-start.2 = (bf16[528,256]{1,0:T(8,128)(2,1)S(1)}, bf16[528,256]{1,0:T(8,128)(2,1)S(1)}, u32[]{:S(2)}, u32[]{:S(2)}) collective-permute-start(bf16[528,256]{1,0:T(8,128)(2,1)S(1)} %collective-permute-done.1.refs_1_), channel_id=1, source_target_pairs={{0,2},{1,3},{2,0},{3,1},{4,6},{5,7},{6,4},{7,5},{8,10},{9,11},{10,... | collective-permute-start | bytes 811016 | tf_op jit(solution)/shard_map/ppermute | solution.py:21
  64.8 7.1 %collective-permute-start.10 = (bf16[528,256]{1,0:T(8,128)(2,1)S(1)}, bf16[528,256]{1,0:T(8,128)(2,1)S(1)}, u32[]{:S(2)}, u32[]{:S(2)}) collective-permute-start(bf16[528,256]{1,0:T(8,128)(2,1)S(1)} %collective-permute-done.7.refs_5_), channel_id=1, source_target_pairs={{0,2},{1,3},{2,0},{3,1},{4,6},{5,7},{6,4},{7,5},{8,10},{9,11},{10,... | collective-permute-start | bytes 811016 | tf_op jit(solution)/shard_map/ppermute | solution.py:21
  66.4 0.8 copy-start.11
  67.2 1.2 %copy-start.9 = (bf16[1056,512]{1,0:T(8,128)(2,1)S(1)}, bf16[1056,512]{1,0:T(8,128)(2,1)}, u32[]{:S(2)}) copy-start(bf16[1056,512]{1,0:T(8,128)(2,1)} %constant_dynamic-update-slice_fusion.3) | copy-start | bytes 3244036
  67.2 7.3 %collective-permute-start.13 = (bf16[1056,512]{1,0:T(8,128)(2,1)S(1)}, bf16[1056,512]{1,0:T(8,128)(2,1)S(1)}, u32[]{:S(2)}, u32[]{:S(2)}) collective-permute-start(bf16[1056,512]{1,0:T(8,128)(2,1)S(1)} %constant_dynamic-update-slice_fusion.4), channel_id=1, source_target_pairs={{0,1},{1,0},{2,3},{3,2},{4,5},{5,4},{6,7},{7,6},{8,9},{9,8},{10,11... | collective-permute-start | bytes 3244040 | tf_op jit(solution)/shard_map/ppermute | solution.py:21
  68.5 6.9 %collective-permute-start.12 = (bf16[1056,512]{1,0:T(8,128)(2,1)S(1)}, bf16[1056,512]{1,0:T(8,128)(2,1)S(1)}, u32[]{:S(2)}, u32[]{:S(2)}) collective-permute-start(bf16[1056,512]{1,0:T(8,128)(2,1)S(1)} %constant_dynamic-update-slice_fusion.2), channel_id=1, source_target_pairs={{0,1},{1,0},{2,3},{3,2},{4,5},{5,4},{6,7},{7,6},{8,9},{9,8},{10,11... | collective-permute-start | bytes 3244040 | tf_op jit(solution)/shard_map/ppermute | solution.py:21
  71.9 1.0 copy-start.12
  71.9 2.0 %collective-permute-start.14 = (bf16[528,512]{1,0:T(8,128)(2,1)S(1)}, bf16[528,512]{1,0:T(8,128)(2,1)S(1)}, u32[]{:S(2)}, u32[]{:S(2)}) collective-permute-start(bf16[528,512]{1,0:T(8,128)(2,1)S(1)} %constant_dynamic-update-slice_fusion.6), channel_id=1, source_target_pairs={{0,1},{1,0},{2,3},{3,2},{4,5},{5,4},{6,7},{7,6},{8,9},{9,8},{10,11... | collective-permute-start | bytes 1622024 | tf_op jit(solution)/shard_map/ppermute | solution.py:21
  73.0 4.2 %collective-permute-start.17 = (bf16[528,512]{1,0:T(8,128)(2,1)S(1)}, bf16[528,512]{1,0:T(8,128)(2,1)S(1)}, u32[]{:S(2)}, u32[]{:S(2)}) collective-permute-start(bf16[528,512]{1,0:T(8,128)(2,1)S(1)} %copy-done.12), channel_id=1, source_target_pairs={{0,1},{1,0},{2,3},{3,2},{4,5},{5,4},{6,7},{7,6},{8,9},{9,8},{10,11... | collective-permute-start | bytes 1622024 | tf_op jit(solution)/shard_map/ppermute | solution.py:21
  77.0 2.0 %collective-permute-start.18 = (bf16[528,512]{1,0:T(8,128)(2,1)S(1)}, bf16[528,512]{1,0:T(8,128)(2,1)S(1)}, u32[]{:S(2)}, u32[]{:S(2)}) collective-permute-start(bf16[528,512]{1,0:T(8,128)(2,1)S(1)} %constant_dynamic-update-slice_fusion), channel_id=1, source_target_pairs={{0,1},{1,0},{2,3},{3,2},{4,5},{5,4},{6,7},{7,6},{8,9},{9,8},{10,11... | collective-permute-start | bytes 1622024 | tf_op jit(solution)/shard_map/ppermute | solution.py:21
  79.5 1.2 %copy-start.1 = (f32[512,512]{1,0:T(8,128)S(1)}, f32[512,512]{1,0:T(8,128)}, u32[]{:S(2)}) copy-start(f32[512,512]{1,0:T(8,128)} %coup_ref.3) | copy-start | bytes 3145732
  79.6 1.5 %copy-start.2 = (f32[512,512]{1,0:T(8,128)S(1)}, f32[512,512]{1,0:T(8,128)}, u32[]{:S(2)}) copy-start(f32[512,512]{1,0:T(8,128)} %one_ref.3) | copy-start | bytes 3145732
  79.6 1.8 %copy-start.3 = (f32[512,512]{1,0:T(8,128)S(1)}, f32[512,512]{1,0:T(8,128)}, u32[]{:S(2)}) copy-start(f32[512,512]{1,0:T(8,128)} %two_ref.3) | copy-start | bytes 3145732
  79.6 1.8 %copy-start.5 = (bf16[128,512]{1,0:T(8,128)(2,1)S(1)}, bf16[128,512]{1,0:T(8,128)(2,1)}, u32[]{:S(2)}) copy-start(bf16[128,512]{1,0:T(8,128)(2,1)} %front_ref.3) | copy-start | bytes 393220
  83.9 8.7 %collective-permute-start.19 = (s16[528,256]{1,0:T(8,128)(2,1)S(1)}, s16[528,256]{1,0:T(8,128)(2,1)S(1)}, u32[]{:S(2)}, u32[]{:S(2)}) collective-permute-start(s16[528,256]{1,0:T(8,128)(2,1)S(1)} %get-tuple-element.56), channel_id=1, source_target_pairs={{0,8},{4,12},{8,0},{12,4},{16,24},{20,28},{24,16},{28,20},{1,9},{5... | collective-permute-start | bytes 811016 | tf_op jit(solution)/shard_map/ppermute | solution.py:21
  87.2 9.0 %collective-permute-start.22 = (s16[528,256]{1,0:T(8,128)(2,1)S(1)}, s16[528,256]{1,0:T(8,128)(2,1)S(1)}, u32[]{:S(2)}, u32[]{:S(2)}) collective-permute-start(s16[528,256]{1,0:T(8,128)(2,1)S(1)} %get-tuple-element.62), channel_id=1, source_target_pairs={{0,4},{4,0},{8,12},{12,8},{16,20},{20,16},{24,28},{28,24},{1,5},{5... | collective-permute-start | bytes 811016 | tf_op jit(solution)/shard_map/ppermute | solution.py:21
  92.7 10.1 %collective-permute-start.20 = (s16[272,256]{1,0:T(8,128)(2,1)S(1)}, s16[272,256]{1,0:T(8,128)(2,1)S(1)}, u32[]{:S(2)}, u32[]{:S(2)}) collective-permute-start(s16[272,256]{1,0:T(8,128)(2,1)S(1)} %get-tuple-element.58), channel_id=1, source_target_pairs={{0,16},{4,20},{8,24},{12,28},{16,0},{20,4},{24,8},{28,12},{1,17},{... | collective-permute-start | bytes 417800 | tf_op jit(solution)/shard_map/ppermute | solution.py:21
  96.4 7.1 %collective-permute-start.23 = (s16[272,256]{1,0:T(8,128)(2,1)S(1)}, s16[272,256]{1,0:T(8,128)(2,1)S(1)}, u32[]{:S(2)}, u32[]{:S(2)}) collective-permute-start(s16[272,256]{1,0:T(8,128)(2,1)S(1)} %get-tuple-element.64), channel_id=1, source_target_pairs={{0,8},{4,12},{8,0},{12,4},{16,24},{20,28},{24,16},{28,20},{1,9},{5... | collective-permute-start | bytes 417800 | tf_op jit(solution)/shard_map/ppermute | solution.py:21
  102.9 0.7 copy-start.6
  102.9 4.4 %collective-permute-start.21 = (s16[144,256]{1,0:T(8,128)(2,1)S(1)}, s16[144,256]{1,0:T(8,128)(2,1)S(1)}, u32[]{:S(2)}, u32[]{:S(2)}) collective-permute-start(s16[144,256]{1,0:T(8,128)(2,1)S(1)} %get-tuple-element.60), channel_id=1, source_target_pairs={{0,4},{4,0},{8,12},{12,8},{16,20},{20,16},{24,28},{28,24},{1,5},{5... | collective-permute-start | bytes 221192 | tf_op jit(solution)/shard_map/ppermute | solution.py:21
  103.6 0.7 copy-start.7
  104.3 5.8 %collective-permute-start.24 = (s16[144,256]{1,0:T(8,128)(2,1)S(1)}, s16[144,256]{1,0:T(8,128)(2,1)S(1)}, u32[]{:S(2)}, u32[]{:S(2)}) collective-permute-start(s16[144,256]{1,0:T(8,128)(2,1)S(1)} %get-tuple-element.66), channel_id=1, source_target_pairs={{0,16},{4,20},{8,24},{12,28},{16,0},{20,4},{24,8},{28,12},{1,17},{... | collective-permute-start | bytes 221192 | tf_op jit(solution)/shard_map/ppermute | solution.py:21
  107.3 2.7 %copy-start.13 = (s16[144,256]{1,0:T(8,128)(2,1)}, s16[144,256]{1,0:T(8,128)(2,1)S(1)}, u32[]{:S(2)}) copy-start(s16[144,256]{1,0:T(8,128)(2,1)S(1)} %collective-permute-done.21.came_a) | copy-start | bytes 221188
  110.1 0.6 copy-start.14
